TPU v7x, 32 devices: a whole 2x2x4 slice. The times are simulated.
32 devices in a mesh: row: 16 (over z, y, x), head: 2 (over core).
Axes of the slice: x: 2, y: 2, z: 4, core: 2. Of those that a mesh axis runs over, the one named last changes fastest.
Arguments:
- memory: float32 [16384, 172], P('row'), may hold values from -4 to 4
- sources: int32 [16, 1024], P('row'), may hold values from 0 to 1023, each once within a row
- dest_ids: int32 [16384], P('row'), may hold values from 0 to 16383
- neighbours: int32 [16384, 10], P('row'), may hold values from 0 to 16383
- delta_t: float32 [16384], P('row'), may hold values from 0.25 to 4
- nbr_delta: float32 [16384, 10], P('row'), may hold values from 0.25 to 4
- edge_feat: bfloat16 [16384, 172], P('row'), may hold values from -6 to 6
- window_count: int32 [16], P('row'), may hold values from 1 to 1024, as said below
- message_weight: float32 [688, 516], P(None, 'head'), may hold values from -0.21875 to 0.21875
- message_weight_moment: float32 [688, 516], P(None, 'head'), may hold values from -0.0009765625 to 0.0009765625
- message_weight_square: float32 [688, 516], P(None, 'head'), may hold values from 6.1035155e-10 to 6.1035155e-09
- state_weight: float32 [172, 516], P(None, 'head'), may hold values from -0.4375 to 0.4375
- state_weight_moment: float32 [172, 516], P(None, 'head'), may hold values from -0.0009765625 to 0.0009765625
- state_weight_square: float32 [172, 516], P(None, 'head'), may hold values from 6.1035155e-10 to 6.1035155e-09
- gate_bias: float32 [2, 516], P(None, 'head'), may hold values from -1.75 to 1.75
- gate_bias_moment: float32 [2, 516], P(None, 'head'), may hold values from -0.0009765625 to 0.0009765625
- gate_bias_square: float32 [2, 516], P(None, 'head'), may hold values from 6.1035155e-10 to 6.1035155e-09
- time_param: float32 [2, 172], replicated, may hold values from 0.1 to 3
- time_param_moment: float32 [2, 172], replicated, may hold values from -0.0009765625 to 0.0009765625
- time_param_square: float32 [2, 172], replicated, may hold values from 6.1035155e-10 to 6.1035155e-09
- attend_weight: float32 [3, 344, 172], P(None, None, 'head'), may hold values from -0.625 to 0.625
- attend_weight_moment: float32 [3, 344, 172], P(None, None, 'head'), may hold values from -0.0009765625 to 0.0009765625
- attend_weight_square: float32 [3, 344, 172], P(None, None, 'head'), may hold values from 6.1035155e-10 to 6.1035155e-09
- dense_first: float32 [2, 172, 172], P(None, 'head'), may hold values from -0.3125 to 0.3125
- dense_first_moment: float32 [2, 172, 172], P(None, 'head'), may hold values from -0.0009765625 to 0.0009765625
- dense_first_square: float32 [2, 172, 172], P(None, 'head'), may hold values from 6.1035155e-10 to 6.1035155e-09
- dense_second: float32 [172, 172], P(None, 'head'), may hold values from -0.4375 to 0.4375
- dense_second_moment: float32 [172, 172], P(None, 'head'), may hold values from -0.0009765625 to 0.0009765625
- dense_second_square: float32 [172, 172], P(None, 'head'), may hold values from 6.1035155e-10 to 6.1035155e-09
- target_weight: float32 [172, 172], replicated, may hold values from -0.4375 to 0.4375
- target_weight_moment: float32 [172, 172], replicated, may hold values from -0.0009765625 to 0.0009765625
- target_weight_square: float32 [172, 172], replicated, may hold values from 6.1035155e-10 to 6.1035155e-09
Outputs:
- new_memory: float32 [16384, 172], P('row', 'head')
- loss_sum: float32 [], replicated
- live_rows: float32 [], replicated
- message_weight_new: float32 [688, 516], P(None, 'head')
- message_weight_moment_new: float32 [688, 516], P(None, 'head')
- message_weight_square_new: float32 [688, 516], P(None, 'head')
- state_weight_new: float32 [172, 516], P(None, 'head')
- state_weight_moment_new: float32 [172, 516], P(None, 'head')
- state_weight_square_new: float32 [172, 516], P(None, 'head')
- gate_bias_new: float32 [2, 516], P(None, 'head')
- gate_bias_moment_new: float32 [2, 516], P(None, 'head')
- gate_bias_square_new: float32 [2, 516], P(None, 'head')
- time_param_new: float32 [2, 172], replicated
- time_param_moment_new: float32 [2, 172], replicated
- time_param_square_new: float32 [2, 172], replicated
- attend_weight_new: float32 [3, 344, 172], P(None, None, 'head')
- attend_weight_moment_new: float32 [3, 344, 172], P(None, None, 'head')
- attend_weight_square_new: float32 [3, 344, 172], P(None, None, 'head')
- dense_first_new: float32 [2, 172, 172], P(None, 'head')
- dense_first_moment_new: float32 [2, 172, 172], P(None, 'head')
- dense_first_square_new: float32 [2, 172, 172], P(None, 'head')
- dense_second_new: float32 [172, 172], P(None, 'head')
- dense_second_moment_new: float32 [172, 172], P(None, 'head')
- dense_second_square_new: float32 [172, 172], P(None, 'head')
- target_weight_new: float32 [172, 172], replicated
- target_weight_moment_new: float32 [172, 172], replicated
- target_weight_square_new: float32 [172, 172], replicated
Inputs may be any that keep to these rules, and one draw needn't show every extreme that they name: Each row of sources holds every number of 0 to 1023 once. The events of row block b that count are its first window_count[b]; the last block's are all of them.
All inputs are finite; a program needn't handle non-finite values.
Results may differ from a plain program's by a relative error of at most 0.0022.
The roundings to bfloat16 on the way count: a program that leaves them out, or rounds other values in their place, can miss the bound.
Values may be sent and summed in bfloat16 or wider, within the bound.
No kernel may reach another device: no remote copies, remote signals or barrier semaphores. Data moves between devices by JAX's collectives and lax.ppermute only.
A program may use at most 256 MiB of HBM per device.

v0:
```python
import functools
import math

import jax
import jax.numpy as jnp
from jax import lax
from jax.experimental import pallas as pl
from jax.experimental.pallas import tpu as pltpu
from jax.sharding import PartitionSpec as P

STEP = 10
LOGIT_SCALE = 0.25
BETA_ONE = 0.9
BETA_TWO = 0.999
RATE = 0.05
EPSILON = 1e-08
BF = jnp.bfloat16
F32 = jnp.float32
PLANE = 4
PAD = 88
LO_BASE = 256
VMEM_LIMIT = 58 * 2**20
VMEM_WHOLE = 62 * 2**20
TABLE_ROWS_MAX = 16384


def nn(a, b):
    return jnp.dot(a, b, preferred_element_type=F32)


def nt(a, b):
    return lax.dot_general(a, b, (((1,), (1,)), ((), ())), preferred_element_type=F32)


def tn(a, b):
    return lax.dot_general(a, b, (((0,), (0,)), ((), ())), preferred_element_type=F32)


def split3(x):
    first = x.astype(BF)
    rest = x - first.astype(F32)
    second = rest.astype(BF)
    third = (rest - second.astype(F32)).astype(BF)
    return first, second, third


def sin_cos(x):
    turns = jnp.floor(x * (1.0 / math.pi) + 0.5)
    r = ((x - turns * 3.140625) - turns * 0.0009679794311523438) + turns * 3.2584135922775204e-07
    sign = 1.0 - 2.0 * (turns - 2.0 * jnp.floor(turns * 0.5))
    r2 = r * r
    s = SIN[4]
    for k in (3, 2, 1, 0):
        s = s * r2 + SIN[k]
    c = COS[5]
    for k in (4, 3, 2, 1, 0):
        c = c * r2 + COS[k]
    return sign * (r * s), sign * c


SIN = (
    0.9999999956301436,
    -0.16666657831257647,
    0.008333047252581481,
    -0.00019808792312667284,
    2.6045791061554316e-06,
)
COS = (
    0.9999999997746029,
    -0.49999999344091517,
    0.0416666357232742,
    -0.0013888354556677485,
    2.4759808628775167e-05,
    -2.604520000579671e-07,
)


def vmem_call(kernel, out_shape, in_spaces, scratch=(), limit=VMEM_LIMIT, flops=0, nbytes=0):
    spaces = {"s": pltpu.SMEM, "v": pltpu.VMEM, "a": pl.ANY}
    return pl.pallas_call(
        kernel,
        out_shape=out_shape,
        in_specs=[pl.BlockSpec(memory_space=spaces[s]) for s in in_spaces],
        out_specs=jax.tree.map(lambda _: pl.BlockSpec(memory_space=pltpu.VMEM), out_shape),
        scratch_shapes=list(scratch),
        compiler_params=pltpu.CompilerParams(vmem_limit_bytes=limit),
        cost_estimate=pl.CostEstimate(flops=flops, bytes_accessed=nbytes, transcendentals=0),
    )


def shape(*dims, dtype=F32):
    return jax.ShapeDtypeStruct(dims, dtype)


def codes_kernel(mem, src, delta, ndelta, tcol, srct, code_d, sin_d, code_n, sin_n):
    model_width, rows = mem.shape
    events = src.shape[1]
    nbrs = ndelta.shape[0]
    pick = (lax.broadcasted_iota(jnp.int32, (rows, events), 0) == src[...]).astype(BF)
    parts = split3(mem[...])
    srct[...] = nn(parts[0], pick) + nn(parts[1], pick) + nn(parts[2], pick)
    freq, phase = tcol[:, 0:1], tcol[:, 1:2]
    sin_v, cos_v = sin_cos(delta[...] * freq + phase)
    code_d[...] = cos_v.astype(BF)
    sin_d[...] = sin_v

    def body(j, carry):
        cols = pl.ds(pl.multiple_of(j * events, events), events)
        s, c = sin_cos(ndelta[pl.ds(j, 1), :] * freq + phase)
        code_n[:, cols] = c.astype(BF)
        sin_n[:, cols] = s
        return carry

    lax.fori_loop(0, nbrs, body, 0)


def weights_kernel(
    meta, mw, mw_o, sw, sw_o, aw, aw_o, df, df_o, ds, ds_o, tw,
    o_m, o_s, o_q, o_kvm, o_kvc, o_kvct, o_f, o_ft, o_d, o_dt, o_tt,
):
    head = meta[1]
    width = tw.shape[0]
    units = width // 2

    def put(h, mw, sw, aw, df, ds):
        o_m[h] = mw[...].astype(BF)
        o_s[h] = sw[...].T.astype(BF)
        o_q[h] = aw[0].astype(BF)
        zero = jnp.zeros((PAD - units, 2 * width), F32)
        pair = jnp.concatenate([aw[1], zero, aw[2], zero], 0)
        wide = jnp.concatenate(
            [pair[:, :width], jnp.zeros((2 * PAD, 256 - width), F32)], 1
        )
        rows = pl.ds(pl.multiple_of(h * 2 * PAD, 2 * PAD), 2 * PAD)
        o_kvm[rows] = wide.astype(BF)
        code = pair[:, width:]
        o_kvc[rows] = code.astype(BF)
        o_kvct[h] = code.T.astype(BF)
        for i in range(2):
            o_f[i, h] = df[i].astype(BF)
            o_ft[i, h] = df[i].T.astype(BF)
        o_d[h] = ds[...].astype(BF)
        o_dt[h] = ds[...].T.astype(BF)

    put(head, mw, sw, aw, df, ds)
    put(1 - head, mw_o, sw_o, aw_o, df_o, ds_o)
    o_tt[...] = tw[...].T.astype(BF)


def chunk_rows(mem_a, mem_b, c, planes, meta, events):
    lo = lax.rem(c, PLANE)
    rest = lax.div(c, PLANE)
    hi = lax.rem(rest, planes)
    half = lax.div(rest, planes)
    first = mem_a[half, lo, hi]
    second = mem_b[half, hi, lo]
    row = meta[0] ^ (hi * PLANE + lo)
    base = row * (2 * events) + (meta[1] ^ half) * events
    return jnp.concatenate([first, second], 0), base, half


def step_kernel(
    planes, use_table,
    meta, idx, mem_a, mem_b, srct, code_d, sin_d, code_n, sin_n, edge, delta, ndelta, tcol, bias,
    w_m, w_s, w_q, w_kvm, w_kvc, w_kvct, w_f, w_ft, w_d, w_dt, w_tt, gathered_in, wcount,
    o_fresh, o_pack,
    near, msg, qin, emb, keyt, count, stat, scores, probs, fresh_s, att_s, gates, acc_m, tgrad,
):
    width, events = srct.shape
    units = width // 2
    nbrs = ndelta.shape[0]
    chunks = 2 * planes * PLANE
    lookups = (nbrs + 1) * events
    scale = 1.0 / math.sqrt(units)
    row_pos, head = meta[0], meta[1]
    hi_rows = count.shape[0]

    count[...] = jnp.zeros_like(count)
    stat[...] = jnp.zeros_like(stat)
    target_t = w_tt[...]

    def per_chunk(c, table):
        x, base, half = chunk_rows(mem_a, mem_b, c, planes, meta, events)
        wide = x.astype(F32)
        if use_table:
            keyt[c] = nn(target_t, x[:width]).astype(BF)
        id_hi = wide[width : width + 1].astype(jnp.int32)
        id_lo = wide[width + 1 : width + 2].astype(jnp.int32)
        hot_hi = (lax.broadcasted_iota(jnp.int32, (hi_rows, events), 0) == id_hi).astype(BF)
        hot_lo = (lax.broadcasted_iota(jnp.int32, (LO_BASE, events), 0) == id_lo).astype(BF)
        count[...] += nt(hot_hi, hot_lo)
        here = (wide[width + 2 : width + 3] * LO_BASE + wide[width + 3 : width + 4])[:, :128]
        stat[0:1, :] += jnp.where(half == 0, here, 0.0)
        if table is not None:
            turned = wide.T
            table[pl.ds(pl.multiple_of(2 * base, 2), events, stride=2), :] = turned[:, :128]
            table[pl.ds(2 * base + 1, events, stride=2), :] = jnp.concatenate(
                [turned[:, 128:], jnp.zeros((events, 256 - wide.shape[0]), F32)], 1
            )

    def gather_rows(table, gathered):
        lax.fori_loop(0, chunks, lambda c, s: (per_chunk(c, table), s)[1], 0)
        unroll = 32

        def body(i, carry):
            for u in range(unroll):
                k = i * unroll + u
                gathered[pl.ds(pl.multiple_of(2 * k, 2), 2), :] = table[
                    pl.ds(pl.multiple_of(idx[k], 2), 2), :
                ]
            return carry

        lax.fori_loop(0, lookups // unroll, body, 0)
        for j in range(nbrs + 1):
            low = gathered[pl.ds(2 * j * events, events, stride=2), :]
            high = gathered[pl.ds(2 * j * events + 1, events, stride=2), :]
            near[pl.ds(j * events, events), :] = jnp.concatenate([low, high], 1).astype(BF)

    if use_table:
        pl.run_scoped(
            gather_rows,
            pltpu.VMEM((2 * chunks * events, 128), F32),
            pltpu.VMEM((2 * lookups, 128), F32),
        )
    else:
        lax.fori_loop(0, chunks, lambda c, s: (per_chunk(c, None), s)[1], 0)
        near = gathered_in
    count[...] = jnp.where(count[...] > 0.5, jnp.log(jnp.maximum(count[...], 1.0)), -1e30)
    live_rows = stat[0:1, 0:1]

    def rest(kvt, pair):
        dest = near[pl.ds(nbrs * events, events), :]
        dest_t = dest.astype(F32).T[:width]
        msg[0:width] = srct[...]
        msg[width : 2 * width] = dest_t
        msg[2 * width : 3 * width] = code_d[...].astype(F32)
        msg[3 * width : 4 * width] = edge[...].astype(F32)
        message = msg[...].astype(BF)
        src_low = srct[...].astype(BF)
        dest_key = nn(target_t, dest_t.astype(BF)).astype(BF)

        def gate_values(h):
            gate_in = nn(w_m[h], message) + bias[h, :, 0:1]
            gate_state = nn(w_s[h], src_low) + bias[h, :, 1:2]
            reset = jax.nn.sigmoid(gate_in[:units] + gate_state[:units])
            update = jax.nn.sigmoid(
                gate_in[units : 2 * units] + gate_state[units : 2 * units]
            )
            state_c = gate_state[2 * units :]
            candidate = jnp.tanh(gate_in[2 * units :] + reset * state_c)
            return reset, update, candidate, state_c

        for h in range(2):
            reset, update, candidate, state_c = gate_values(h)
            for k, v in enumerate((reset, update, candidate, state_c)):
                gates[h, k] = v
            fresh = (1.0 - update) * candidate + update * srct[h * units : (h + 1) * units]
            o_fresh[h] = fresh
            qin[h * units : (h + 1) * units] = fresh
        _, zero_cos = sin_cos(tcol[...])
        zero_sin, _ = sin_cos(tcol[...])
        qin[width : 2 * width] = jnp.broadcast_to(zero_cos[:, 1:2], (width, events))
        query_in = qin[...].astype(BF)
        fresh_low = query_in[:width]

        def project(j, carry):
            cols = pl.ds(pl.multiple_of(j * events, events), events)
            kvt[:, cols] = nt(w_kvm[...], near[cols, :]) + nn(w_kvc[...], code_n[:, cols])
            return carry

        lax.fori_loop(0, nbrs, project, 0)
        attended_low = []
        for h in range(2):
            key_at, value_at = h * 2 * PAD, h * 2 * PAD + PAD
            queries = nn(w_q[h], query_in)
            fresh_s[h, :units] = queries
            for j in range(nbrs):
                cols = pl.ds(j * events, events)
                scores[j : j + 1] = (
                    jnp.sum(queries * kvt[key_at : key_at + units, cols], 0, keepdims=True) * scale
                )
            score = scores[0:nbrs]
            grown = jnp.exp(score - jnp.max(score, 0, keepdims=True))
            prob = grown / jnp.sum(grown, 0, keepdims=True)
            probs[h, 0:nbrs] = prob
            total = jnp.zeros((units, events), F32)
            for j in range(nbrs):
                cols = pl.ds(j * events, events)
                total = total + prob[j : j + 1] * kvt[value_at : value_at + units, cols]
            att_s[h, :units] = total
            attended_low.append(total.astype(BF))
        fresh_lows = [qin[h * units : (h + 1) * units].astype(BF) for h in range(2)]
        hidden = (nn(w_ft[0, 0], attended_low[0]) + nn(w_ft[0, 1], attended_low[1])) + (
            nn(w_ft[1, 0], fresh_lows[0]) + nn(w_ft[1, 1], fresh_lows[1])
        )
        sigmoid_h = jax.nn.sigmoid(hidden)
        mixed_low = (hidden * sigmoid_h).astype(BF)
        emb_halves = [nn(w_dt[h], mixed_low) for h in range(2)]
        emb[0:units] = emb_halves[0]
        emb[units:width] = emb_halves[1]
        emb_low = emb[...].astype(BF)
        emb_rows = (LOGIT_SCALE * emb_low.astype(F32)).T.astype(BF)
        own_logit = LOGIT_SCALE * jnp.sum(
            emb_low.astype(F32) * dest_key.astype(F32), 0, keepdims=True
        )

        group = 4 if use_table else 2

        def soft_section(logits, acc, top, total):
            top[...] = jnp.full_like(top, -1e30)
            total[...] = jnp.zeros_like(total)
            acc[...] = jnp.zeros_like(acc)

            def body(g, carry):
                parts = []
                for s in range(group):
                    c = g * group + s
                    x, base, _ = chunk_rows(mem_a, mem_b, c, planes, meta, events)
                    parts.append(x)
                    at = lax.div(base, LO_BASE)
                    shift = jnp.concatenate(
                        [count[pl.ds(at + k, 1), :] for k in range(events // LO_BASE)], 1
                    )
                    keys = keyt[c] if use_table else nn(target_t, x[:width]).astype(BF)
                    logits[:, s * events : (s + 1) * events] = nn(emb_rows, keys) + shift
                old = top[:, 0:1]
                new = jnp.maximum(old, jnp.max(logits[...], 1, keepdims=True))
                grown = jnp.exp(logits[...] - new)
                fade = jnp.exp(old - new)
                total[...] = total[...] * fade + jnp.sum(grown, 1, keepdims=True)
                top[...] = jnp.broadcast_to(new, top.shape)
                low = grown.astype(BF)
                more = nt(low[:, 0:events], parts[0])
                for s in range(1, group):
                    more = more + nt(low[:, s * events : (s + 1) * events], parts[s])
                acc[...] = acc[...] * fade + more
                return carry

            lax.fori_loop(0, chunks // group, body, 0)
            acc_m[...] = (acc[...] / total[:, 0:1]).T
            stat[8:16, :] = jnp.zeros((8, 128), F32)
            probs[2] = jnp.broadcast_to(top[:, 0:1] + jnp.log(total[:, 0:1]), (events, 128)).T[:16]

        pl.run_scoped(
            soft_section,
            pltpu.VMEM((events, group * events), F32),
            pltpu.VMEM((events, mem_a.shape[3] + mem_b.shape[3]), F32),
            pltpu.VMEM((events, 128), F32),
            pltpu.VMEM((events, 128), F32),
        )
        log_total = probs[2, 0:1]
        position = lax.broadcasted_iota(jnp.int32, (1, events), 1) + head * events
        live = (position < wcount[0]).astype(F32)
        loss = jnp.sum((log_total - own_logit) * live, 1, keepdims=True)
        weight = live / live_rows
        own_prob = jnp.exp(own_logit - log_total)
        own_grad = ((own_prob - 1.0) * weight).astype(BF).astype(F32) - own_prob * weight
        mean_mem = acc_m[:width]
        spread = weight * mean_mem + own_grad * dest_t
        parts = split3(spread)
        target_grad = LOGIT_SCALE * (nt(parts[0], emb_low) + nt(parts[1], emb_low) + nt(parts[2], emb_low))
        parts = split3(mean_mem)
        mean_key = nn(target_t, parts[0]) + nn(target_t, parts[1]) + nn(target_t, parts[2])
        emb_grad = LOGIT_SCALE * (weight * mean_key + own_grad * dest_key.astype(F32))

        o_pack[...] = jnp.zeros_like(o_pack)
        row_qk, row_vf, row_sd, row_t, row_b = pack_rows(units)

        def slot(h):
            return h ^ head

        emb_grad_low = [emb_grad[h * units : (h + 1) * units].astype(BF) for h in range(2)]
        mixed_grad = nn(w_d[0], emb_grad_low[0]) + nn(w_d[1], emb_grad_low[1])
        hidden_grad = (mixed_grad * sigmoid_h * (1.0 + hidden * (1.0 - sigmoid_h))).astype(BF)
        for h in range(2):
            second = nt(mixed_low, emb_grad_low[h])
            place = slot(h)
            o_pack[place, row_sd : row_sd + units, 3 * units : 4 * units] = second[:units]
            o_pack[place, row_sd : row_sd + units, 7 * units : 8 * units] = second[units:]
            for i, v in enumerate((attended_low[h], fresh_lows[h])):
                o_pack[place, row_vf : row_vf + units, (2 + i) * width : (3 + i) * width] = nt(
                    v, hidden_grad
                )
            quarter = units // 2
            for k in range(2):
                o_pack[place, row_t : row_t + quarter, k * width : (k + 1) * width] = target_grad[
                    h * units + k * quarter : h * units + (k + 1) * quarter
                ]

        tgrad[...] = jnp.zeros_like(tgrad)
        query_lows = []
        prob_terms = []
        att_grads = []
        for h in range(2):
            value_at = h * 2 * PAD + PAD
            att_grad = nn(w_f[0, h], hidden_grad)
            prob = probs[h, 0:nbrs]
            for j in range(nbrs):
                cols = pl.ds(j * events, events)
                scores[j : j + 1] = jnp.sum(
                    att_grad * kvt[value_at : value_at + units, cols], 0, keepdims=True
                )
            prob_grad = scores[0:nbrs]
            prob_terms.append(prob * (prob_grad - jnp.sum(prob * prob_grad, 0, keepdims=True)))
            att_grads.append(att_grad)
            total = jnp.zeros((units, events), F32)
            key_at = h * 2 * PAD
            for j in range(nbrs):
                cols = pl.ds(j * events, events)
                total = total + prob_terms[h][j : j + 1] * kvt[key_at : key_at + units, cols]
            query_lows.append((total * scale).astype(BF))
        fill = jnp.zeros((PAD - units, events), F32)
        for j in range(nbrs):
            cols = pl.ds(j * events, events)
            pieces = []
            for h in range(2):
                pieces += [
                    (prob_terms[h][j : j + 1] * scale) * fresh_s[h, :units], fill,
                    probs[h, j : j + 1] * att_grads[h], fill,
                ]
            pair_j = jnp.concatenate(pieces, 0).astype(BF)
            pair[:, cols] = pair_j
            code_grad = nn(w_kvct[0], pair_j[: 2 * PAD]) + nn(w_kvct[1], pair_j[2 * PAD :])
            slope = sin_n[:, cols] * code_grad
            tgrad[1, :width] -= slope
            tgrad[0, :width] -= slope * ndelta[j : j + 1]
        near_grad = nn(pair[...], near[pl.ds(0, nbrs * events), :])
        code_wgrad = nt(pair[...], code_n[...])
        for h in range(2):
            place = slot(h)
            base = h * 2 * PAD
            query_grad = nt(query_lows[h], query_in)
            o_pack[place, row_qk : row_qk + units, 0 : 2 * width] = query_grad
            for k, (row, lane) in enumerate(((row_qk, 2 * width), (row_vf, 0))):
                at = base + k * PAD
                o_pack[place, row : row + units, lane : lane + width] = near_grad[
                    at : at + units, :width
                ]
                o_pack[place, row : row + units, lane + width : lane + 2 * width] = code_wgrad[
                    at : at + units
                ]
        query_in_grad = tn(w_q[0], query_lows[0]) + tn(w_q[1], query_lows[1])
        zero_term = zero_sin[:, 1:2] * query_in_grad[width:]
        tgrad[1, :width] -= zero_term

        code_dt_grad = jnp.zeros((width, events), F32)
        ones = jnp.ones((8, events), BF)
        for h in range(2):
            place = slot(h)
            reset, update, candidate, state_c = (gates[h, k] for k in range(4))
            fresh_grad = nn(w_f[1, h], hidden_grad) + query_in_grad[h * units : (h + 1) * units]
            own_state = srct[h * units : (h + 1) * units]
            candidate_pre = fresh_grad * (1.0 - update) * (1.0 - candidate * candidate)
            update_pre = fresh_grad * (own_state - candidate) * update * (1.0 - update)
            reset_pre = candidate_pre * state_c * reset * (1.0 - reset)
            in_grad = jnp.concatenate([reset_pre, update_pre, candidate_pre], 0).astype(BF)
            state_grad = jnp.concatenate([reset_pre, update_pre, candidate_pre * reset], 0).astype(BF)
            o_pack[place, 0 : 3 * units, :] = nt(in_grad, message)
            state_w = nt(src_low, state_grad)
            o_pack[place, row_sd : row_sd + units, 0 : 3 * units] = state_w[:units]
            o_pack[place, row_sd : row_sd + units, 4 * units : 7 * units] = state_w[units:]
            o_pack[place, row_b : row_b + 1, 0 : 3 * units] = nt(ones, in_grad)[0:1]
            o_pack[place, row_b + 1 : row_b + 2, 0 : 3 * units] = nt(ones, state_grad)[0:1]
            code_dt_grad = code_dt_grad + tn(w_m[h][:, 2 * width : 3 * width], in_grad)
        slope = sin_d[...] * code_dt_grad
        tgrad[1, :width] -= slope
        tgrad[0, :width] -= slope * delta[...]
        ones_f = jnp.ones((8, events), F32)
        for i in range(2):
            line = lax.dot_general(
                ones_f, tgrad[i, :width], (((1,), (1,)), ((), ())),
                precision=lax.Precision.HIGHEST, preferred_element_type=F32,
            )[0:1]
            for place in range(2):
                o_pack[place, row_b + 2 + i : row_b + 3 + i, 0:width] = line
        for place in range(2):
            o_pack[place, row_b + 4 : row_b + 5, 0:128] = jnp.broadcast_to(loss, (1, 128))
            o_pack[place, row_b + 5 : row_b + 6, 0:128] = stat[0:1, :]

    pl.run_scoped(
        rest,
        pltpu.VMEM((4 * PAD, nbrs * events), F32),
        pltpu.VMEM((4 * PAD, nbrs * events), BF),
    )


def pack_rows(units):
    step = -(-units // 8) * 8
    first = -(-3 * units // 8) * 8
    return first, first + step, first + 2 * step, first + 3 * step, first + 3 * step + -(-units // 16) * 8


def pack_height(units):
    return -(-(pack_rows(units)[-1] + 8) // 64) * 64


def memory_kernel(mem, fresh, src, wcount, out):
    units, rows = mem.shape
    pick = (lax.broadcasted_iota(jnp.int32, (rows, rows), 1) == src[...]).astype(BF)
    parts = split3(fresh[...])
    moved = nn(parts[0], pick) + nn(parts[1], pick) + nn(parts[2], pick)
    alive = (lax.broadcasted_iota(jnp.int32, (16, rows), 1) < wcount[0]).astype(BF)
    hit = nn(alive, pick)[0:1] > 0.5
    out[...] = jnp.where(hit, moved, mem[...])


def adam_step(master, moment, square, gradient):
    moment_new = BETA_ONE * moment + (1.0 - BETA_ONE) * gradient
    square_new = BETA_TWO * square + (1.0 - BETA_TWO) * gradient * gradient
    master_new = master - RATE * (moment_new / (1.0 - BETA_ONE**STEP)) / (
        jnp.sqrt(square_new / (1.0 - BETA_TWO**STEP)) + EPSILON
    )
    return (master_new, moment_new, square_new)


def flips(count, step):
    return [(i, i ^ step) for i in range(count)]


def per_device(
    n_row,
    memory, sources, dest_ids, neighbours, delta_t, nbr_delta, edge_feat, window_count,
    message_weight, message_weight_moment, message_weight_square,
    state_weight, state_weight_moment, state_weight_square,
    gate_bias, gate_bias_moment, gate_bias_square,
    time_param, time_param_moment, time_param_square,
    attend_weight, attend_weight_moment, attend_weight_square,
    dense_first, dense_first_moment, dense_first_square,
    dense_second, dense_second_moment, dense_second_square,
    target_weight, target_weight_moment, target_weight_square,
):
    rows, width = memory.shape
    units = width // 2
    events = rows // 2
    nbrs = neighbours.shape[1]
    planes = n_row // PLANE
    total_rows = n_row * rows
    head = lax.axis_index("head")
    row = lax.axis_index("row")
    meta = jnp.stack([row, head]).astype(jnp.int32)

    def own(x, axis):
        return lax.dynamic_slice_in_dim(x, head * events, events, axis)

    def swap(x):
        return lax.ppermute(x, "head", [(0, 1), (1, 0)])

    def hop(x, step):
        return lax.ppermute(x, "row", flips(n_row, step))

    mem_t = memory.T
    own_ids = own(dest_ids, 0)
    lines = jnp.stack(
        [
            own_ids // LO_BASE,
            own_ids % LO_BASE,
            jnp.broadcast_to(window_count[0] // LO_BASE, (events,)),
            jnp.broadcast_to(window_count[0] % LO_BASE, (events,)),
        ]
    )
    block = jnp.concatenate([own(mem_t, 1).astype(BF), lines.astype(BF)], 0)
    cut = 112
    part_a, part_b = block[:cut][None], block[cut:][None]
    line_a = jnp.concatenate([part_a] + [hop(part_a, d * PLANE) for d in range(1, planes)], 0)
    plane_b = jnp.concatenate([part_b] + [hop(part_b, d) for d in range(1, PLANE)], 0)
    all_a = jnp.stack([line_a] + [hop(line_a, d) for d in range(1, PLANE)])
    all_b = jnp.stack([plane_b] + [hop(plane_b, d * PLANE) for d in range(1, planes)])
    mem_a = jnp.stack([all_a, swap(all_a)])
    mem_b = jnp.stack([all_b, swap(all_b)])

    src = own(sources, 1)
    delta = own(delta_t[None], 1)
    ndelta = own(nbr_delta.T, 1)
    tcol = time_param.T
    code_shapes = (
        shape(width, events), shape(width, events, dtype=BF), shape(width, events),
        shape(width, nbrs * events, dtype=BF), shape(width, nbrs * events),
    )
    srct, code_d, sin_d, code_n, sin_n = vmem_call(codes_kernel, code_shapes, "vvvvv")(
        mem_t, src, delta, ndelta, tcol
    )
    mw, aw = message_weight.T, attend_weight.transpose(0, 2, 1)
    weights = (mw, state_weight, aw, dense_first, dense_second)
    pairs = []
    for w in weights:
        pairs += [w, swap(w)]
    gb = gate_bias.T
    gb_o = swap(gb)
    bias = jnp.where(head == 0, jnp.stack([gb, gb_o]), jnp.stack([gb_o, gb]))
    bf = functools.partial(shape, dtype=BF)
    w_shapes = (
        bf(2, 3 * units, 4 * width), bf(2, 3 * units, width), bf(2, units, 2 * width),
        bf(4 * PAD, 256), bf(4 * PAD, width), bf(2, width, 2 * PAD),
        bf(2, 2, units, width), bf(2, 2, width, units), bf(2, width, units), bf(2, units, width),
        bf(width, width),
    )
    prepared = vmem_call(weights_kernel, w_shapes, "s" + "v" * 11)(meta, *pairs, target_weight)

    index = jnp.concatenate([own(neighbours.T, 1).reshape(-1), own_ids])
    use_table = total_rows <= TABLE_ROWS_MAX
    lookups = (nbrs + 1) * events
    if use_table:
        gathered = jnp.zeros((16, 128), BF)
    else:
        order = jnp.arange(n_row, dtype=jnp.int32) ^ row
        full_a = mem_a.transpose(0, 2, 1, 4, 3).reshape(2, n_row, events, cut)
        full_b = mem_b.transpose(0, 1, 2, 4, 3).reshape(2, n_row, events, block.shape[0] - cut)
        full = jnp.concatenate([full_a, full_b], 3)
        at = index // rows
        half = (index % rows) // events
        gathered = full[half ^ head, at ^ row, index % events]
        gathered = jnp.pad(gathered, ((0, 0), (0, 256 - block.shape[0])))
        del order
    height = pack_height(units)
    hi_rows = total_rows // LO_BASE
    scratch = [
        pltpu.VMEM((lookups if use_table else 16, 256), BF),
        pltpu.VMEM((4 * width, events), F32),
        pltpu.VMEM((2 * width, events), F32),
        pltpu.VMEM((width, events), F32),
        pltpu.VMEM((2 * n_row if use_table else 1, width, events), BF),
        pltpu.VMEM((hi_rows, LO_BASE), F32),
        pltpu.VMEM((16, 128), F32),
        pltpu.VMEM((16, events), F32),
        pltpu.VMEM((3, 16, events), F32),
        pltpu.VMEM((2, PAD, events), F32),
        pltpu.VMEM((2, PAD, events), F32),
        pltpu.VMEM((2, 4, units, events), F32),
        pltpu.VMEM((block.shape[0], events), F32),
        pltpu.VMEM((2, PAD * 2, events), F32),
    ]
    fresh, pack = vmem_call(
        functools.partial(step_kernel, planes, use_table),
        (shape(2, units, events), shape(2, height, 4 * width)),
        "ss" + "v" * 24 + "s",
        scratch,
        VMEM_LIMIT if use_table else VMEM_WHOLE,
    )(
        meta, 2 * index, mem_a, mem_b, srct, code_d, sin_d, code_n, sin_n, own(edge_feat.T, 1),
        delta, ndelta, tcol, bias, *prepared, gathered, window_count,
    )

    fresh_own = lax.dynamic_index_in_dim(fresh, head, 0, False)
    fresh_sent = swap(lax.dynamic_index_in_dim(fresh, 1 - head, 0, False))
    both = jnp.where(
        head == 0,
        jnp.concatenate([fresh_own, fresh_sent], 1),
        jnp.concatenate([fresh_sent, fresh_own], 1),
    )
    base_cols = lax.dynamic_slice_in_dim(mem_t, head * units, units, 0)
    new_memory = vmem_call(memory_kernel, shape(units, rows), "vvvs")(
        base_cols, both, sources.reshape(rows, 1), window_count
    ).T

    buf = pack[0] + swap(pack[1])
    cut_steps = []
    step = 1
    while step < PLANE:
        bit = (row // step) % 2
        half = buf.shape[0] // 2
        keep = lax.dynamic_slice_in_dim(buf, bit * half, half, 0)
        send = lax.dynamic_slice_in_dim(buf, (1 - bit) * half, half, 0)
        buf = keep + hop(send, step)
        cut_steps.append((step, bit))
        step *= 2
    while step < n_row:
        buf = buf + hop(buf, step)
        step *= 2
    for step, bit in reversed(cut_steps):
        got = hop(buf, step)
        buf = jnp.where(bit == 0, jnp.concatenate([buf, got], 0), jnp.concatenate([got, buf], 0))

    row_qk, row_vf, row_sd, row_t, row_b = pack_rows(units)
    quarter = units // 2
    shared = buf[row_t : row_b + 8]
    shared_o = swap(shared)
    first = jnp.where(head == 0, shared, shared_o)
    second = jnp.where(head == 0, shared_o, shared)
    target_sum = jnp.concatenate(
        [p[:quarter, k * width : (k + 1) * width] for p in (first, second) for k in range(2)], 0
    )
    small = first[row_b - row_t :]
    time_sum = small[2:4, :width]
    loss_sum = small[4, 0]
    live_rows = small[5, 0] * (1.0 / (2 * n_row))
    bias_sum = buf[row_b : row_b + 2, : 3 * units]
    message_sum = buf[: 3 * units]
    query_sum = buf[row_qk : row_qk + units, : 2 * width]
    key_sum = buf[row_qk : row_qk + units, 2 * width :]
    value_sum = buf[row_vf : row_vf + units, : 2 * width]
    attend_sum = jnp.stack([query_sum, key_sum, value_sum])
    first_sum = jnp.stack(
        [buf[row_vf : row_vf + units, k * width : (k + 1) * width] for k in (2, 3)]
    )
    state_sum = jnp.concatenate(
        [buf[row_sd : row_sd + units, k : k + 3 * units] for k in (0, 4 * units)], 0
    )
    second_sum = jnp.concatenate(
        [buf[row_sd : row_sd + units, k : k + units] for k in (3 * units, 7 * units)], 0
    )

    def turned(x):
        return x.transpose(0, 2, 1)

    message_out = adam_step(mw, message_weight_moment.T, message_weight_square.T, message_sum)
    message_out = tuple(x.T for x in message_out)
    state_out = adam_step(state_weight, state_weight_moment, state_weight_square, state_sum)
    bias_out = adam_step(gate_bias, gate_bias_moment, gate_bias_square, bias_sum)
    time_out = adam_step(time_param, time_param_moment, time_param_square, time_sum)
    attend_out = adam_step(aw, turned(attend_weight_moment), turned(attend_weight_square), attend_sum)
    attend_out = tuple(turned(x) for x in attend_out)
    first_out = adam_step(dense_first, dense_first_moment, dense_first_square, first_sum)
    second_out = adam_step(dense_second, dense_second_moment, dense_second_square, second_sum)
    target_out = adam_step(target_weight, target_weight_moment, target_weight_square, target_sum)
    return (
        new_memory, loss_sum, live_rows,
        *message_out, *state_out, *bias_out, *time_out, *attend_out, *first_out, *second_out, *target_out,
    )


def solution(mesh):
    cols = P(None, "head")
    third = P(None, None, "head")
    middle = P(None, "head", None)
    by_row = P("row", None)
    in_specs = (
        (by_row, by_row, P("row"), by_row, P("row"), by_row, by_row, P("row"))
        + (cols,) * 9 + (P(),) * 3 + (third,) * 3 + (middle,) * 3 + (cols,) * 3 + (P(),) * 3
    )
    out_specs = (
        (P("row", "head"), P(), P())
        + (cols,) * 9 + (P(),) * 3 + (third,) * 3 + (middle,) * 3 + (cols,) * 3 + (P(),) * 3
    )
    return jax.shard_map(
        functools.partial(per_device, mesh.shape["row"]),
        mesh=mesh, in_specs=in_specs, out_specs=out_specs, check_vma=False,
    )
```

profile of v0, /device:TPU:0, one launch (start us, length us, event | category | flops | bytes accessed | tf_op | source)
XLA Modules:
  0.0 297.9 jit_solution(4102933634744778977)
XLA Ops:
  0.7 1.1 fusion.6
  1.8 3.1 %collective-permute-start = (bf16[1,112,512]{2,1,0:T(8,128)(2,1)S(1)}, bf16[1,112,512]{2,1,0:T(8,128)(2,1)S(1)}, u32[]{:S(2)}, u32[]{:S(2)}) collective-permute-start(bf16[1,112,512]{2,1,0:T(8,128)(2,1)S(1)} %slice_bitcast_fusion.4), channel_id=1, source_target_pairs={{0,8},{2,10},{4,12},{6,14},{8,0},{10,2},{12,4},{14,6},{16,24},{18,... | collective-permute-start | bytes 344072 | tf_op jit(solution)/shard_map/ppermute | solution.py:549
  4.9 2.6 collective-permute-start.1
  8.0 8.5 %collective-permute-done.1 = bf16[1,112,512]{2,1,0:T(8,128)(2,1)S(1)} collective-permute-done((bf16[1,112,512]{2,1,0:T(8,128)(2,1)S(1)}, bf16[1,112,512]{2,1,0:T(8,128)(2,1)S(1)}, u32[]{:S(2)}, u32[]{:S(2)}) %collective-permute-start.1) | collective-permute-done | bytes 114720 | tf_op jit(solution)/shard_map/ppermute | solution.py:549
  16.6 1.6 collective-permute-start.3
  18.2 1.5 collective-permute-start.4
  21.2 9.0 %collective-permute-done.3 = bf16[4,112,512]{2,1,0:T(8,128)(2,1)S(1)} collective-permute-done((bf16[4,112,512]{2,1,0:T(8,128)(2,1)S(1)}, bf16[4,112,512]{2,1,0:T(8,128)(2,1)S(1)}, u32[]{:S(2)}, u32[]{:S(2)}) %collective-permute-start.3) | collective-permute-done | bytes 458784 | tf_op jit(solution)/shard_map/ppermute | solution.py:549
  30.2 7.6 %collective-permute-done.4 = bf16[4,112,512]{2,1,0:T(8,128)(2,1)S(1)} collective-permute-done((bf16[4,112,512]{2,1,0:T(8,128)(2,1)S(1)}, bf16[4,112,512]{2,1,0:T(8,128)(2,1)S(1)}, u32[]{:S(2)}, u32[]{:S(2)}) %collective-permute-start.4) | collective-permute-done | bytes 458784 | tf_op jit(solution)/shard_map/ppermute | solution.py:549
  37.8 0.8 copy-done.11
  38.7 2.7 fusion.20
  41.5 1.2 collective-permute-start.7
  42.6 1.0 collective-permute-start.8
  43.6 1.4 collective-permute-start.9
  45.0 1.0 collective-permute-done.7
  46.0 0.9 collective-permute-done.8
  46.9 1.9 collective-permute-done.9
  48.8 2.8 collective-permute-start.10
  51.6 1.1 collective-permute-start.11
  52.7 1.4 collective-permute-start.12
  54.1 7.0 %collective-permute-done.10 = bf16[4,64,512]{2,1,0:T(8,128)(2,1)S(1)} collective-permute-done((bf16[4,64,512]{2,1,0:T(8,128)(2,1)S(1)}, bf16[4,64,512]{2,1,0:T(8,128)(2,1)S(1)}, u32[]{:S(2)}, u32[]{:S(2)}) %collective-permute-start.10) | collective-permute-done | bytes 262176 | tf_op jit(solution)/shard_map/ppermute | solution.py:549
  61.1 11.9 %collective-permute-done.11 = bf16[4,64,512]{2,1,0:T(8,128)(2,1)S(1)} collective-permute-done((bf16[4,64,512]{2,1,0:T(8,128)(2,1)S(1)}, bf16[4,64,512]{2,1,0:T(8,128)(2,1)S(1)}, u32[]{:S(2)}, u32[]{:S(2)}) %collective-permute-start.11) | collective-permute-done | bytes 262176 | tf_op jit(solution)/shard_map/ppermute | solution.py:549
  73.0 1.2 fusion.19
  74.8 0.7 copy.84.df
  77.2 0.7 dynamic-slice_bitcast_fusion.3.edge
  79.8 0.8 copy.80
  80.5 9.2 %shard_map.511 = (f32[172,512]{1,0:T(8,128)}, bf16[172,512]{1,0:T(8,128)(2,1)}, f32[172,512]{1,0:T(8,128)}, bf16[172,5120]{1,0:T(8,128)(2,1)}, f32[172,5120]{1,0:T(8,128)}) custom-call(f32[172,1024]{1,0:T(8,128)} %bitcast.106, s32[1,512]{1,0:T(1,128)} %constant_dynamic-slice_fusion.2.src, f32[1,512]{1,0:T(1,128)} %bitcast.118, ...), custom_call_target="tpu_custom_call" | custom-call | tf_op jit(solution)/shard_map/pallas_call | solution.py:579
  90.7 0.7 broadcast_select_fusion.bias
  91.5 1.0 collective-permute-done.16.sw_o
  92.5 0.7 copy-done.20
  93.2 3.8 %shard_map.512 = (bf16[2,258,688]{2,1,0:T(8,128)(2,1)}, bf16[2,258,172]{2,1,0:T(8,128)(2,1)}, bf16[2,86,344]{2,1,0:T(8,128)(2,1)}, bf16[352,256]{1,0:T(8,128)(2,...) custom-call(s32[2]{0:T(128)} %pad_add_fusion.meta, ...), custom_call_target="tpu_custom_call" | custom-call | tf_op jit(solution)/shard_map/pallas_call | solution.py:597
  97.0 2.7 pad_maximum_fusion.1.mem_b
  99.7 3.7 %pad_maximum_fusion.mem_a = bf16[2,4,4,112,512]{4,3,2,1,0:T(8,128)(2,1)} fusion(bf16[1,4,4,112,512]{4,3,2,1,0:T(8,128)(2,1)} %bitcast.11, bf16[1,4,4,112,512]{4,3,2,1,0:T(8,128)(2,1)S(1)} %get-tuple-element.178), kind=kLoop, calls=%fused_computation | loop fusion | flops 1835008 | bytes 7340032 | tf_op jit(solution)/shard_map/stack | solution.py:568
  104.0 58.5 %shard_map.513 = (f32[2,86,512]{2,1,0:T(8,128)}, f32[2,640,688]{2,1,0:T(8,128)}) custom-call(s32[2]{0:T(128)} %pad_add_fusion.meta, s32[5632]{0:T(1024)} %add_multiply_fusion.idx, bf16[2,4,4,112,512]{4,3,2,1,0:T(8,128)(2,1)} %pad_maximum_fusion.mem_a, bf16[2,4,4,64,512]{4,3,2,1,0:T(8,128)(2,1)} %pad_maximum_fusion.1.mem_b, ...), custom_call_target="tpu_custom_call" | custom-call | tf_op jit(solution)/shard_map/pallas_call | solution.py:632
  162.5 1.7 slice_bitcast_fusion
  164.2 1.7 copy.86
  166.1 3.9 %collective-permute-done.21 = f32[640,688]{0,1:T(8,128)} collective-permute-done((f32[640,688]{0,1:T(8,128)}, f32[640,688]{0,1:T(8,128)}, u32[]{:S(2)}, u32[]{:S(2)}) %collective-permute-start.21) | collective-permute-done | bytes 1761312 | tf_op jit(solution)/shard_map/ppermute | solution.py:546
  170.0 2.1 copy.87
  172.1 1.8 bitcast_add_fusion
  173.9 1.3 copy-done.2
  175.2 1.6 collective-permute-start.22
  176.8 22.3 %collective-permute-done.22 = f32[320,688]{1,0:T(8,128)S(1)} collective-permute-done((f32[320,688]{1,0:T(8,128)S(1)}, f32[320,688]{1,0:T(8,128)S(1)}, u32[]{:S(2)}, u32[]{:S(2)}) %collective-permute-start.22) | collective-permute-done | bytes 880672 | tf_op jit(solution)/shard_map/ppermute | solution.py:549
  199.1 1.3 dynamic-slice_add_fusion
  200.5 1.2 collective-permute-start.23
  201.6 11.4 %collective-permute-done.23 = f32[160,688]{1,0:T(8,128)S(1)} collective-permute-done((f32[160,688]{1,0:T(8,128)S(1)}, f32[160,688]{1,0:T(8,128)S(1)}, u32[]{:S(2)}, u32[]{:S(2)}) %collective-permute-start.23) | collective-permute-done | bytes 440352 | tf_op jit(solution)/shard_map/ppermute | solution.py:549
  213.0 3.7 %collective-permute-start.24 = (f32[160,688]{1,0:T(8,128)S(1)}, f32[160,688]{1,0:T(8,128)S(1)}, u32[]{:S(2)}, u32[]{:S(2)}) collective-permute-start(f32[160,688]{1,0:T(8,128)S(1)} %dynamic-slice_add_fusion.1), channel_id=1, source_target_pairs={{0,8},{2,10},{4,12},{6,14},{8,0},{10,2},{12,4},{14,6},{16,24},{18,... | collective-permute-start | bytes 1320968 | tf_op jit(solution)/shard_map/ppermute | solution.py:549
  216.8 9.8 %collective-permute-done.24 = f32[160,688]{1,0:T(8,128)S(1)} collective-permute-done((f32[160,688]{1,0:T(8,128)S(1)}, f32[160,688]{1,0:T(8,128)S(1)}, u32[]{:S(2)}, u32[]{:S(2)}) %collective-permute-start.24) | collective-permute-done | bytes 440352 | tf_op jit(solution)/shard_map/ppermute | solution.py:549
  226.6 2.9 collective-permute-start.25
  229.5 19.5 %collective-permute-done.25 = f32[160,688]{1,0:T(8,128)S(1)} collective-permute-done((f32[160,688]{1,0:T(8,128)S(1)}, f32[160,688]{1,0:T(8,128)S(1)}, u32[]{:S(2)}, u32[]{:S(2)}) %collective-permute-start.25) | collective-permute-done | bytes 440352 | tf_op jit(solution)/shard_map/ppermute | solution.py:549
  249.1 1.1 collective-permute-start.26
  250.2 11.1 %collective-permute-done.26 = f32[160,688]{1,0:T(8,128)S(1)} collective-permute-done((f32[160,688]{1,0:T(8,128)S(1)}, f32[160,688]{1,0:T(8,128)S(1)}, u32[]{:S(2)}, u32[]{:S(2)}) %collective-permute-start.26) | collective-permute-done | bytes 440352 | tf_op jit(solution)/shard_map/ppermute | solution.py:549
  261.4 1.6 collective-permute-start.27
  263.1 1.0 copy.85.src
  264.1 0.8 dynamic-slice_bitcast_fusion.mem
  264.9 0.8 maximum_select_fusion.2.fresh
  265.7 3.6 %shard_map.514 = f32[86,1024]{1,0:T(8,128)} custom-call(f32[86,1024]{1,0:T(8,128)} %dynamic-slice_bitcast_fusion.mem, f32[86,1024]{1,0:T(8,128)} %maximum_select_fusion.2.fresh, s32[1024,1]{1,0:T(8,128)} %copy.85.src, s32[1]{0:T(128)} %copy.103.wcount), custom_call_target="tpu_custom_call" | custom-call | tf_op jit(solution)/shard_map/pallas_call | solution.py:651
  269.3 14.0 %collective-permute-done.27 = f32[320,688]{1,0:T(8,128)S(1)} collective-permute-done((f32[320,688]{1,0:T(8,128)S(1)}, f32[320,688]{1,0:T(8,128)S(1)}, u32[]{:S(2)}, u32[]{:S(2)}) %collective-permute-start.27) | collective-permute-done | bytes 880672 | tf_op jit(solution)/shard_map/ppermute | solution.py:549
  284.7 0.8 copy.91
  285.4 0.8 copy.92
  286.2 0.8 copy.93
  287.0 3.2 %fusion.8 = (f32[688,258]{0,1:T(8,128)}, f32[688,258]{0,1:T(8,128)}, f32[688,258]{0,1:T(8,128)}) fusion(f32[640,688]{1,0:T(8,128)S(1)} %maximum_select_fusion, f32[688,258]{0,1:T(8,128)S(1)} %copy-done.6, f32[688,258]{0,1:T(8,128)S(1)} %copy-done.7, f32[688,258]{0,1:T(8,128)} %param.40), kind=kLoop, calls=%fused_computation.46 | loop fusion | flops 2130048 | bytes 4970112 | tf_op jit(solution)/shard_map/transpose | solution.py:706
  290.2 0.7 divide_subtract_fusion.3
  291.0 1.0 divide_subtract_fusion
  292.1 1.3 fusion.16
  295.9 0.9 divide_subtract_fusion.1
  (142 shorter events, 11.2 us)
Async XLA Ops:
  0.7 76.5 %copy-start = (bf16[1024,172]{0,1:T(8,128)(2,1)S(1)}, bf16[1024,172]{0,1:T(8,128)(2,1)}, u32[]{:S(2)}) copy-start(bf16[1024,172]{0,1:T(8,128)(2,1)} %param.38) | copy-start | bytes 1056772
  0.7 20.2 %copy-start.38 = (s32[1024]{0:T(1024)S(1)}, s32[1024]{0:T(1024)}, u32[]{:S(2)}) copy-start(s32[1024]{0:T(1024)} %param.34) | copy-start | bytes 12292
  1.8 6.2 %collective-permute-start = (bf16[1,112,512]{2,1,0:T(8,128)(2,1)S(1)}, bf16[1,112,512]{2,1,0:T(8,128)(2,1)S(1)}, u32[]{:S(2)}, u32[]{:S(2)}) collective-permute-start(bf16[1,112,512]{2,1,0:T(8,128)(2,1)S(1)} %slice_bitcast_fusion.4), channel_id=1, source_target_pairs={{0,8},{2,10},{4,12},{6,14},{8,0},{10,2},{12,4},{14,6},{16,24},{18,... | collective-permute-start | bytes 344072 | tf_op jit(solution)/shard_map/ppermute | solution.py:549
  4.9 11.7 %collective-permute-start.1 = (bf16[1,112,512]{2,1,0:T(8,128)(2,1)S(1)}, bf16[1,112,512]{2,1,0:T(8,128)(2,1)S(1)}, u32[]{:S(2)}, u32[]{:S(2)}) collective-permute-start(bf16[1,112,512]{2,1,0:T(8,128)(2,1)S(1)} %slice_bitcast_fusion.4), channel_id=1, source_target_pairs={{0,16},{2,18},{4,20},{6,22},{8,24},{10,26},{12,28},{14,30},{16,0},... | collective-permute-start | bytes 344072 | tf_op jit(solution)/shard_map/ppermute | solution.py:549
  7.5 9.1 %collective-permute-start.2 = (bf16[1,112,512]{2,1,0:T(8,128)(2,1)S(1)}, bf16[1,112,512]{2,1,0:T(8,128)(2,1)S(1)}, u32[]{:S(2)}, u32[]{:S(2)}) collective-permute-start(bf16[1,112,512]{2,1,0:T(8,128)(2,1)S(1)} %slice_bitcast_fusion.4), channel_id=1, source_target_pairs={{0,24},{2,26},{4,28},{6,30},{8,16},{10,18},{12,20},{14,22},{16,8},... | collective-permute-start | bytes 344072 | tf_op jit(solution)/shard_map/ppermute | solution.py:549
  16.6 13.5 %collective-permute-start.3 = (bf16[4,112,512]{2,1,0:T(8,128)(2,1)S(1)}, bf16[4,112,512]{2,1,0:T(8,128)(2,1)S(1)}, u32[]{:S(2)}, u32[]{:S(2)}) collective-permute-start(bf16[4,112,512]{2,1,0:T(8,128)(2,1)S(1)} %get-tuple-element.186), channel_id=1, source_target_pairs={{0,2},{2,0},{4,6},{6,4},{8,10},{10,8},{12,14},{14,12},{16,18},{18,... | collective-permute-start | bytes 1376264 | tf_op jit(solution)/shard_map/ppermute | solution.py:549
  18.2 19.5 %collective-permute-start.4 = (bf16[4,112,512]{2,1,0:T(8,128)(2,1)S(1)}, bf16[4,112,512]{2,1,0:T(8,128)(2,1)S(1)}, u32[]{:S(2)}, u32[]{:S(2)}) collective-permute-start(bf16[4,112,512]{2,1,0:T(8,128)(2,1)S(1)} %get-tuple-element.186), channel_id=1, source_target_pairs={{0,4},{2,6},{4,0},{6,2},{8,12},{10,14},{12,8},{14,10},{16,20},{18,... | collective-permute-start | bytes 1376264 | tf_op jit(solution)/shard_map/ppermute | solution.py:549
  19.7 18.0 %collective-permute-start.5 = (bf16[4,112,512]{2,1,0:T(8,128)(2,1)S(1)}, bf16[4,112,512]{2,1,0:T(8,128)(2,1)S(1)}, u32[]{:S(2)}, u32[]{:S(2)}) collective-permute-start(bf16[4,112,512]{2,1,0:T(8,128)(2,1)S(1)} %get-tuple-element.186), channel_id=1, source_target_pairs={{0,6},{2,4},{4,2},{6,0},{8,14},{10,12},{12,10},{14,8},{16,22},{18,... | collective-permute-start | bytes 1376264 | tf_op jit(solution)/shard_map/ppermute | solution.py:549
  41.4 58.3 %collective-permute-start.6 = (bf16[4,4,112,512]{3,2,1,0:T(8,128)(2,1)}, bf16[4,4,112,512]{3,2,1,0:T(8,128)(2,1)}, u32[]{:S(2)}, u32[]{:S(2)}) collective-permute-start(bf16[4,4,112,512]{3,2,1,0:T(8,128)(2,1)} %get-tuple-element.179), channel_id=1, source_target_pairs={{0,1},{1,0},{2,3},{3,2},{4,5},{5,4},{6,7},{7,6},{8,9},{9,8},{10,11... | collective-permute-start | bytes 5505032 | tf_op jit(solution)/shard_map/ppermute | solution.py:546
  41.4 33.3 %copy-start.9 = (f32[2,86,172]{2,0,1:T(2,128)S(1)}, f32[2,86,172]{2,0,1:T(2,128)}, u32[]{:S(2)}) copy-start(f32[2,86,172]{2,0,1:T(2,128)} %param.55) | copy-start | bytes 355012
  41.4 34.0 %copy-start.30 = (f32[2,258]{1,0:T(2,128)S(1)}, f32[2,258]{1,0:T(2,128)}, u32[]{:S(2)}) copy-start(f32[2,258]{1,0:T(2,128)} %param.46) | copy-start | bytes 6196
  41.4 34.5 %copy-start.28 = (s32[1024,10]{0,1:T(8,128)S(1)}, s32[1024,10]{0,1:T(8,128)}, u32[]{:S(2)}) copy-start(s32[1024,10]{0,1:T(8,128)} %param.35) | copy-start | bytes 122884
  41.5 4.6 %collective-permute-start.7 = (bf16[1,64,512]{2,1,0:T(8,128)(2,1)S(1)}, bf16[1,64,512]{2,1,0:T(8,128)(2,1)S(1)}, u32[]{:S(2)}, u32[]{:S(2)}) collective-permute-start(bf16[1,64,512]{2,1,0:T(8,128)(2,1)S(1)} %slice_bitcast_fusion.7), channel_id=1, source_target_pairs={{0,2},{2,0},{4,6},{6,4},{8,10},{10,8},{12,14},{14,12},{16,18},{18,... | collective-permute-start | bytes 196616 | tf_op jit(solution)/shard_map/ppermute | solution.py:549
  42.6 4.3 %collective-permute-start.8 = (bf16[1,64,512]{2,1,0:T(8,128)(2,1)S(1)}, bf16[1,64,512]{2,1,0:T(8,128)(2,1)S(1)}, u32[]{:S(2)}, u32[]{:S(2)}) collective-permute-start(bf16[1,64,512]{2,1,0:T(8,128)(2,1)S(1)} %slice_bitcast_fusion.7), channel_id=1, source_target_pairs={{0,4},{2,6},{4,0},{6,2},{8,12},{10,14},{12,8},{14,10},{16,20},{18,... | collective-permute-start | bytes 196616 | tf_op jit(solution)/shard_map/ppermute | solution.py:549
  43.6 5.2 %collective-permute-start.9 = (bf16[1,64,512]{2,1,0:T(8,128)(2,1)S(1)}, bf16[1,64,512]{2,1,0:T(8,128)(2,1)S(1)}, u32[]{:S(2)}, u32[]{:S(2)}) collective-permute-start(bf16[1,64,512]{2,1,0:T(8,128)(2,1)S(1)} %slice_bitcast_fusion.7), channel_id=1, source_target_pairs={{0,6},{2,4},{4,2},{6,0},{8,14},{10,12},{12,10},{14,8},{16,22},{18,... | collective-permute-start | bytes 196616 | tf_op jit(solution)/shard_map/ppermute | solution.py:549
  48.8 27.2 %copy-start.29 = (f32[1024,10]{0,1:T(8,128)S(1)}, f32[1024,10]{0,1:T(8,128)}, u32[]{:S(2)}) copy-start(f32[1024,10]{0,1:T(8,128)} %param.37) | copy-start | bytes 122884
  48.8 12.3 %collective-permute-start.10 = (bf16[4,64,512]{2,1,0:T(8,128)(2,1)S(1)}, bf16[4,64,512]{2,1,0:T(8,128)(2,1)S(1)}, u32[]{:S(2)}, u32[]{:S(2)}) collective-permute-start(bf16[4,64,512]{2,1,0:T(8,128)(2,1)S(1)} %get-tuple-element.190), channel_id=1, source_target_pairs={{0,8},{2,10},{4,12},{6,14},{8,0},{10,2},{12,4},{14,6},{16,24},{18,... | collective-permute-start | bytes 786440 | tf_op jit(solution)/shard_map/ppermute | solution.py:549
  51.6 21.4 %collective-permute-start.11 = (bf16[4,64,512]{2,1,0:T(8,128)(2,1)S(1)}, bf16[4,64,512]{2,1,0:T(8,128)(2,1)S(1)}, u32[]{:S(2)}, u32[]{:S(2)}) collective-permute-start(bf16[4,64,512]{2,1,0:T(8,128)(2,1)S(1)} %get-tuple-element.190), channel_id=1, source_target_pairs={{0,16},{2,18},{4,20},{6,22},{8,24},{10,26},{12,28},{14,30},{16,0},... | collective-permute-start | bytes 786440 | tf_op jit(solution)/shard_map/ppermute | solution.py:549
  52.7 20.3 %collective-permute-start.12 = (bf16[4,64,512]{2,1,0:T(8,128)(2,1)S(1)}, bf16[4,64,512]{2,1,0:T(8,128)(2,1)S(1)}, u32[]{:S(2)}, u32[]{:S(2)}) collective-permute-start(bf16[4,64,512]{2,1,0:T(8,128)(2,1)S(1)} %get-tuple-element.190), channel_id=1, source_target_pairs={{0,24},{2,26},{4,28},{6,30},{8,16},{10,18},{12,20},{14,22},{16,8},... | collective-permute-start | bytes 786440 | tf_op jit(solution)/shard_map/ppermute | solution.py:549
  73.0 4.9 %copy-start.31 = (s32[1,1024]{1,0:T(1,128)S(1)}, s32[1,1024]{1,0:T(1,128)}, u32[]{:S(2)}) copy-start(s32[1,1024]{1,0:T(1,128)} %param.33) | copy-start | bytes 12292
  73.0 5.5 %copy-start.16 = (f32[172,86]{1,0:T(8,128)S(1)}, f32[172,86]{1,0:T(8,128)}, u32[]{:S(2)}) copy-start(f32[172,86]{1,0:T(8,128)} %ds.1) | copy-start | bytes 177508
  73.0 6.1 %copy-start.37 = (f32[1024]{0:T(1024)S(1)}, f32[1024]{0:T(1024)}, u32[]{:S(2)}) copy-start(f32[1024]{0:T(1024)} %param.36) | copy-start | bytes 12292
  73.0 6.7 %copy-start.32 = (f32[2,172]{1,0:T(2,128)S(1)}, f32[2,172]{1,0:T(2,128)}, u32[]{:S(2)}) copy-start(f32[2,172]{1,0:T(2,128)} %param.49) | copy-start | bytes 4132
  74.2 22.8 %collective-permute-start.13 = (bf16[4,4,64,512]{3,2,1,0:T(8,128)(2,1)}, bf16[4,4,64,512]{3,2,1,0:T(8,128)(2,1)}, u32[]{:S(2)}, u32[]{:S(2)}) collective-permute-start(bf16[4,4,64,512]{3,2,1,0:T(8,128)(2,1)} %get-tuple-element.181), channel_id=1, source_target_pairs={{0,1},{1,0},{2,3},{3,2},{4,5},{5,4},{6,7},{7,6},{8,9},{9,8},{10,11... | collective-permute-start | bytes 3145736 | tf_op jit(solution)/shard_map/ppermute | solution.py:546
  74.2 18.2 %collective-permute-start.15 = (f32[258,688]{1,0:T(8,128)}, f32[258,688]{1,0:T(8,128)}, u32[]{:S(2)}, u32[]{:S(2)}) collective-permute-start(f32[258,688]{1,0:T(8,128)} %bitcast.29.mw), channel_id=1, source_target_pairs={{0,1},{1,0},{2,3},{3,2},{4,5},{5,4},{6,7},{7,6},{8,9},{9,8},{10,11... | collective-permute-start | bytes 2130056 | tf_op jit(solution)/shard_map/ppermute | solution.py:546
  75.4 15.2 %collective-permute-start.18 = (f32[2,86,172]{2,1,0:T(8,128)}, f32[2,86,172]{2,1,0:T(8,128)}, u32[]{:S(2)}, u32[]{:S(2)}) collective-permute-start(f32[2,86,172]{2,1,0:T(8,128)} %copy.84.df), channel_id=1, source_target_pairs={{0,1},{1,0},{2,3},{3,2},{4,5},{5,4},{6,7},{7,6},{8,9},{9,8},{10,11... | collective-permute-start | bytes 355016 | tf_op jit(solution)/shard_map/ppermute | solution.py:546
  75.4 3.0 %collective-permute-start.14 = (f32[258,2]{0,1:T(2,128)S(1)}, f32[258,2]{0,1:T(2,128)S(1)}, u32[]{:S(2)}, u32[]{:S(2)}) collective-permute-start(f32[258,2]{0,1:T(2,128)S(1)} %bitcast.120), channel_id=1, source_target_pairs={{0,1},{1,0},{2,3},{3,2},{4,5},{5,4},{6,7},{7,6},{8,9},{9,8},{10,11... | collective-permute-start | bytes 6200 | tf_op jit(solution)/shard_map/ppermute | solution.py:546
  78.5 11.3 %collective-permute-start.19 = (f32[172,86]{1,0:T(8,128)S(1)}, f32[172,86]{1,0:T(8,128)S(1)}, u32[]{:S(2)}, u32[]{:S(2)}) collective-permute-start(f32[172,86]{1,0:T(8,128)S(1)} %copy-done.16), channel_id=1, source_target_pairs={{0,1},{1,0},{2,3},{3,2},{4,5},{5,4},{6,7},{7,6},{8,9},{9,8},{10,11... | collective-permute-start | bytes 177512 | tf_op jit(solution)/shard_map/ppermute | solution.py:546
  89.8 2.7 copy-start.27
  89.8 2.7 collective-permute-start.17
  90.7 1.8 collective-permute-start.16
  165.9 4.0 %collective-permute-start.21 = (f32[640,688]{0,1:T(8,128)}, f32[640,688]{0,1:T(8,128)}, u32[]{:S(2)}, u32[]{:S(2)}) collective-permute-start(f32[640,688]{0,1:T(8,128)} %copy.86), channel_id=1, source_target_pairs={{0,1},{1,0},{2,3},{3,2},{4,5},{5,4},{6,7},{7,6},{8,9},{9,8},{10,11... | collective-permute-start | bytes 5283848 | tf_op jit(solution)/shard_map/ppermute | solution.py:546
  173.9 1.3 copy-start.2
  175.2 23.9 %collective-permute-start.22 = (f32[320,688]{1,0:T(8,128)S(1)}, f32[320,688]{1,0:T(8,128)S(1)}, u32[]{:S(2)}, u32[]{:S(2)}) collective-permute-start(f32[320,688]{1,0:T(8,128)S(1)} %constant_dynamic-slice_fusion.1), channel_id=1, source_target_pairs={{0,2},{2,0},{4,6},{6,4},{8,10},{10,8},{12,14},{14,12},{16,18},{18,... | collective-permute-start | bytes 2641928 | tf_op jit(solution)/shard_map/ppermute | solution.py:549
  200.5 12.5 %collective-permute-start.23 = (f32[160,688]{1,0:T(8,128)S(1)}, f32[160,688]{1,0:T(8,128)S(1)}, u32[]{:S(2)}, u32[]{:S(2)}) collective-permute-start(f32[160,688]{1,0:T(8,128)S(1)} %constant_dynamic-slice_fusion), channel_id=1, source_target_pairs={{0,4},{2,6},{4,0},{6,2},{8,12},{10,14},{12,8},{14,10},{16,20},{18,... | collective-permute-start | bytes 1320968 | tf_op jit(solution)/shard_map/ppermute | solution.py:549
  213.0 13.5 %collective-permute-start.24 = (f32[160,688]{1,0:T(8,128)S(1)}, f32[160,688]{1,0:T(8,128)S(1)}, u32[]{:S(2)}, u32[]{:S(2)}) collective-permute-start(f32[160,688]{1,0:T(8,128)S(1)} %dynamic-slice_add_fusion.1), channel_id=1, source_target_pairs={{0,8},{2,10},{4,12},{6,14},{8,0},{10,2},{12,4},{14,6},{16,24},{18,... | collective-permute-start | bytes 1320968 | tf_op jit(solution)/shard_map/ppermute | solution.py:549
  226.6 36.4 %copy-start.15 = (f32[2,86,512]{2,1,0:T(8,128)S(1)}, f32[2,86,512]{2,1,0:T(8,128)}, u32[]{:S(2)}) copy-start(f32[2,86,512]{2,1,0:T(8,128)} %get-tuple-element.61) | copy-start | bytes 1056772
  226.6 22.4 %collective-permute-start.25 = (f32[160,688]{1,0:T(8,128)S(1)}, f32[160,688]{1,0:T(8,128)S(1)}, u32[]{:S(2)}, u32[]{:S(2)}) collective-permute-start(f32[160,688]{1,0:T(8,128)S(1)} %add.178), channel_id=1, source_target_pairs={{0,16},{2,18},{4,20},{6,22},{8,24},{10,26},{12,28},{14,30},{16,0},... | collective-permute-start | bytes 1320968 | tf_op jit(solution)/shard_map/ppermute | solution.py:549
  249.1 15.0 %copy-start.3 = (f32[1024,172]{0,1:T(8,128)S(1)}, f32[1024,172]{0,1:T(8,128)}, u32[]{:S(2)}) copy-start(f32[1024,172]{0,1:T(8,128)} %param.32) | copy-start | bytes 2113540
  249.1 12.2 %collective-permute-start.26 = (f32[160,688]{1,0:T(8,128)S(1)}, f32[160,688]{1,0:T(8,128)S(1)}, u32[]{:S(2)}, u32[]{:S(2)}) collective-permute-start(f32[160,688]{1,0:T(8,128)S(1)} %add.179), channel_id=1, source_target_pairs={{0,4},{2,6},{4,0},{6,2},{8,12},{10,14},{12,8},{14,10},{16,20},{18,... | collective-permute-start | bytes 1320968 | tf_op jit(solution)/shard_map/ppermute | solution.py:549
  261.4 21.9 %collective-permute-start.27 = (f32[320,688]{1,0:T(8,128)S(1)}, f32[320,688]{1,0:T(8,128)S(1)}, u32[]{:S(2)}, u32[]{:S(2)}) collective-permute-start(f32[320,688]{1,0:T(8,128)S(1)} %maximum_select_fusion.1), channel_id=1, source_target_pairs={{0,2},{2,0},{4,6},{6,4},{8,10},{10,8},{12,14},{14,12},{16,18},{18,... | collective-permute-start | bytes 2641928 | tf_op jit(solution)/shard_map/ppermute | solution.py:549
  263.0 1.9 collective-permute-start.20
  283.4 1.0 copy-start.23
  283.5 1.1 copy-start.24
  283.6 3.4 %copy-start.6 = (f32[688,258]{0,1:T(8,128)S(1)}, f32[688,258]{0,1:T(8,128)}, u32[]{:S(2)}) copy-start(f32[688,258]{0,1:T(8,128)} %param.42) | copy-start | bytes 2130052
  283.6 3.4 %copy-start.7 = (f32[688,258]{0,1:T(8,128)S(1)}, f32[688,258]{0,1:T(8,128)}, u32[]{:S(2)}) copy-start(f32[688,258]{0,1:T(8,128)} %param.41) | copy-start | bytes 2130052
  283.9 10.0 %collective-permute-start.28 = (f32[56,688]{1,0:T(8,128)S(1)}, f32[56,688]{1,0:T(8,128)S(1)}, u32[]{:S(2)}, u32[]{:S(2)}) collective-permute-start(f32[56,688]{1,0:T(8,128)S(1)} %slice.98), channel_id=1, source_target_pairs={{0,1},{1,0},{2,3},{3,2},{4,5},{5,4},{6,7},{7,6},{8,9},{9,8},{10,11... | collective-permute-start | bytes 462344 | tf_op jit(solution)/shard_map/ppermute | solution.py:546
  287.0 3.2 %copy-start.17 = (f32[172,86]{1,0:T(8,128)S(1)}, f32[172,86]{1,0:T(8,128)}, u32[]{:S(2)}) copy-start(f32[172,86]{1,0:T(8,128)} %ds.1) | copy-start | bytes 177508
  287.0 3.2 %copy-start.25 = (f32[172,86]{1,0:T(8,128)S(1)}, f32[172,86]{1,0:T(8,128)}, u32[]{:S(2)}) copy-start(f32[172,86]{1,0:T(8,128)} %param.59) | copy-start | bytes 177508
  287.0 3.2 %copy-start.26 = (f32[172,86]{1,0:T(8,128)S(1)}, f32[172,86]{1,0:T(8,128)}, u32[]{:S(2)}) copy-start(f32[172,86]{1,0:T(8,128)} %param.60) | copy-start | bytes 177508
  287.0 4.0 %copy-start.5 = (f32[172,258]{1,0:T(8,128)S(1)}, f32[172,258]{1,0:T(8,128)}, u32[]{:S(2)}) copy-start(f32[172,258]{1,0:T(8,128)} %sw.1) | copy-start | bytes 532516
  287.0 4.0 %copy-start.18 = (f32[172,258]{1,0:T(8,128)S(1)}, f32[172,258]{1,0:T(8,128)}, u32[]{:S(2)}) copy-start(f32[172,258]{1,0:T(8,128)} %param.44) | copy-start | bytes 532516
  287.0 4.0 %copy-start.19 = (f32[172,258]{1,0:T(8,128)S(1)}, f32[172,258]{1,0:T(8,128)}, u32[]{:S(2)}) copy-start(f32[172,258]{1,0:T(8,128)} %param.45) | copy-start | bytes 532516
  290.2 1.8 copy-start.4
  290.2 1.8 copy-start.13
  290.2 1.8 copy-start.14
  291.0 2.4 copy-start.33
  291.0 2.4 copy-start.34
  292.0 4.8 %copy-start.1 = (bf16[1024,172]{0,1:T(8,128)(2,1)S(1)}, bf16[1024,172]{0,1:T(8,128)(2,1)}, u32[]{:S(2)}) copy-start(bf16[1024,172]{0,1:T(8,128)(2,1)} %param.38) | copy-start | bytes 1056772
  292.0 2.6 copy-start.35
  292.0 2.6 copy-start.36
  292.0 3.9 %copy-start.8 = (f32[172,172]{1,0:T(8,128)S(1)}, f32[172,172]{1,0:T(8,128)}, u32[]{:S(2)}) copy-start(f32[172,172]{1,0:T(8,128)} %tw.1) | copy-start | bytes 355012
  292.0 3.9 %copy-start.21 = (f32[172,172]{1,0:T(8,128)S(1)}, f32[172,172]{1,0:T(8,128)}, u32[]{:S(2)}) copy-start(f32[172,172]{1,0:T(8,128)} %param.62) | copy-start | bytes 355012
  292.0 3.9 %copy-start.22 = (f32[172,172]{1,0:T(8,128)S(1)}, f32[172,172]{1,0:T(8,128)}, u32[]{:S(2)}) copy-start(f32[172,172]{1,0:T(8,128)} %param.63) | copy-start | bytes 355012
  (4 other events, 3.3 us)
where the time goes:
time: 298 us
  waiting for transfers between devices  141 us (47%)
  Pallas kernels  75.2 us (25%)
  starting transfers between devices  32.1 us (11%)
  other arithmetic  25.2 us (8%)
  local copies, waits for them, and re-layouts  20.4 us (7%)
  between operations  3.73 us (1%)
    ppermute x18, waiting for transfers between devices, hop(): return lax.ppermute(x, 'row', flips(n_row, step))  136 us
    pallas_call x1, Pallas kernels, per_device(): vmem_call(functools.partial(step_kernel, planes, use_table), (shape(2, un...  58.5 us
    ppermute x18, starting transfers between devices, hop(): return lax.ppermute(x, 'row', flips(n_row, step))  30.1 us
    pallas_call x1, Pallas kernels, per_device(): vmem_call(codes_kernel, code_shapes, 'vvvvv')  9.24 us
    unnamed x83, local copies, waits for them, and re-layouts  7.31 us
    another operation x2, other arithmetic, per_device(): mem_a = jnp.stack([all_a, swap(all_a)])  6.45 us
  transfers between devices with their start and end apart: 29, of which 17 were waited for; matrix products, arithmetic and copies ran while one was open for 7% of the time, Pallas kernels for 6%

commit v1 on v0

v1 whole, which is shorter than its diff:
```python
import functools
import math

import jax
import jax.numpy as jnp
from jax import lax
from jax.experimental import pallas as pl
from jax.experimental.pallas import tpu as pltpu
from jax.sharding import PartitionSpec as P

STEP = 10
LOGIT_SCALE = 0.25
BETA_ONE = 0.9
BETA_TWO = 0.999
RATE = 0.05
EPSILON = 1e-08
BF = jnp.bfloat16
F32 = jnp.float32
PLANE = 4
PAD = 88
LO_BASE = 256
SAFE_LOGIT = 40.0
VMEM_LIMIT = 58 * 2**20
VMEM_WHOLE = 62 * 2**20
VMEM_SMALL = 12 * 2**20
VMEM_ADAM = 24 * 2**20
TABLE_ROWS_MAX = 16384


def nn(a, b):
    return jnp.dot(a, b, preferred_element_type=F32)


def nt(a, b):
    return lax.dot_general(a, b, (((1,), (1,)), ((), ())), preferred_element_type=F32)


def tn(a, b):
    return lax.dot_general(a, b, (((0,), (0,)), ((), ())), preferred_element_type=F32)


def split3(x):
    first = x.astype(BF)
    rest = x - first.astype(F32)
    second = rest.astype(BF)
    third = (rest - second.astype(F32)).astype(BF)
    return first, second, third


def sin_cos(x):
    turns = jnp.floor(x * (1.0 / math.pi) + 0.5)
    r = ((x - turns * 3.140625) - turns * 0.0009679794311523438) + turns * 3.2584135922775204e-07
    sign = 1.0 - 2.0 * (turns - 2.0 * jnp.floor(turns * 0.5))
    r2 = r * r
    s = SIN[4]
    for k in (3, 2, 1, 0):
        s = s * r2 + SIN[k]
    c = COS[5]
    for k in (4, 3, 2, 1, 0):
        c = c * r2 + COS[k]
    return sign * (r * s), sign * c


SIN = (
    0.9999999956301436,
    -0.16666657831257647,
    0.008333047252581481,
    -0.00019808792312667284,
    2.6045791061554316e-06,
)
COS = (
    0.9999999997746029,
    -0.49999999344091517,
    0.0416666357232742,
    -0.0013888354556677485,
    2.4759808628775167e-05,
    -2.604520000579671e-07,
)


def vmem_call(kernel, out_shape, in_spaces, scratch=(), limit=VMEM_LIMIT, micros=0, in_place=()):
    spaces = {"s": pltpu.SMEM, "v": pltpu.VMEM, "a": pl.ANY}

    def spec(item):
        if isinstance(item, list):
            return tuple(spec(i) for i in item)
        return pl.BlockSpec(memory_space=spaces[item])

    return pl.pallas_call(
        kernel,
        out_shape=out_shape,
        in_specs=[spec(item) for item in in_spaces],
        out_specs=jax.tree.map(
            lambda x: pl.BlockSpec(memory_space=pl.ANY if x in in_place else pltpu.VMEM), out_shape
        ),
        scratch_shapes=list(scratch),
        compiler_params=pltpu.CompilerParams(vmem_limit_bytes=limit),
        cost_estimate=pl.CostEstimate(
            flops=micros * 10**9, bytes_accessed=micros * 10**6, transcendentals=0
        ),
    )


def shape(*dims, dtype=F32):
    return jax.ShapeDtypeStruct(dims, dtype)


def block_kernel(meta, wcount, mem, ids, out):
    width = mem.shape[0]
    events = out.shape[1]
    cols = pl.ds(pl.multiple_of(meta[1] * events, events), events)
    own = ids[:, cols]
    line = lax.broadcasted_iota(jnp.int32, (8, events), 0)
    small = jnp.where(line == 4, own // LO_BASE, own % LO_BASE)
    small = jnp.where(line == 6, wcount[0] // LO_BASE, small)
    small = jnp.where(line == 7, wcount[0] % LO_BASE, small).astype(F32)
    value = mem[:, cols]
    last = jnp.concatenate([value[width - 4 :], small[4:]], 0)
    out[...] = jnp.concatenate([value[: width - 4], last], 0).astype(BF)


def codes_kernel(meta, mem, src, delta, ndelta, tcol, edge, srct, msg, sin_d, code_n, sin_n):
    rows = mem.shape[1]
    events = srct.shape[1]
    nbrs = ndelta.shape[0]
    own = pl.ds(pl.multiple_of(meta[1] * events, events), events)
    pick = (lax.broadcasted_iota(jnp.int32, (rows, events), 0) == src[:, own]).astype(BF)
    parts = split3(mem[...])
    source = nn(parts[0], pick) + nn(parts[1], pick) + nn(parts[2], pick)
    srct[...] = source
    freq, phase = tcol[:, 0:1], tcol[:, 1:2]
    sin_v, cos_v = sin_cos(delta[:, own] * freq + phase)
    sin_d[...] = sin_v
    msg[...] = jnp.concatenate([source, cos_v, edge[:, own].astype(F32)], 0).astype(BF)

    def body(j, carry):
        cols = pl.ds(pl.multiple_of(j * events, events), events)
        s, c = sin_cos(ndelta[pl.ds(j, 1), own] * freq + phase)
        code_n[:, cols] = c.astype(BF)
        sin_n[:, cols] = s.astype(BF)
        return carry

    lax.fori_loop(0, nbrs, body, 0)


WP_QK, WP_VF, WP_SD, WP_B = 272, 368, 464, 736
WP_ROWS, WP_LANES = 752, 768


def pack_weights_kernel(mw, sw, aw, df, ds, gb, out):
    width, units = ds.shape
    out[0 : 3 * units, 0 : 4 * width] = mw[...].astype(BF)
    out[WP_QK : WP_QK + units, 0 : 4 * width] = jnp.concatenate([aw[0], aw[1]], 1).astype(BF)
    out[WP_VF : WP_VF + units, 0 : 4 * width] = jnp.concatenate([aw[2], df[0], df[1]], 1).astype(BF)
    out[WP_SD : WP_SD + 3 * units, 0:width] = sw[...].T.astype(BF)
    out[WP_SD : WP_SD + width, 256 : 256 + units] = ds[...].astype(BF)
    out[WP_SD : WP_SD + units, 384 : 384 + width] = ds[...].T.astype(BF)
    parts = split3(gb[...])
    small = jnp.concatenate([p.astype(F32) for p in parts] + [jnp.zeros((10, gb.shape[1]), F32)], 0)
    out[WP_B : WP_B + 16, 0 : 3 * units] = small.astype(BF)


def weights_kernel(
    meta, own, other, tw, msg,
    o_md, o_mc, o_q, o_kvm, o_kvc, o_kvct, o_f, o_ft, o_d, o_dt, o_tt, o_gin, o_gst,
):
    width = tw.shape[0]
    units = width // 2
    gates = 3 * units

    def put(h, w):
        mw = w[0:gates, 0 : 4 * width].astype(F32)
        o_md[h] = jnp.concatenate(
            [mw[:, width : 2 * width], jnp.zeros((gates, 256 - width), F32)], 1
        ).astype(BF)
        o_mc[h] = mw[:, 2 * width : 3 * width].astype(BF)
        rest = jnp.concatenate([mw[:, :width], mw[:, 2 * width :]], 1).astype(BF)
        small = w[WP_B : WP_B + 16, 0:gates].astype(F32)
        bias = (small[0:2] + small[2:4]) + small[4:6]
        bias = jnp.concatenate([bias, jnp.zeros((6, gates), F32)], 0).T
        o_gin[h] = nn(rest, msg[...]) + bias[:, 0:1]
        o_gst[h] = nn(w[WP_SD : WP_SD + gates, 0:width], msg[0:width]) + bias[:, 1:2]
        o_q[h] = w[WP_QK : WP_QK + units, 0 : 2 * width]
        zero = jnp.zeros((PAD - units, 2 * width), F32)
        key = w[WP_QK : WP_QK + units, 2 * width : 4 * width].astype(F32)
        value = w[WP_VF : WP_VF + units, 0 : 2 * width].astype(F32)
        pair = jnp.concatenate([key, zero, value, zero], 0)
        wide = jnp.concatenate([pair[:, :width], jnp.zeros((2 * PAD, 256 - width), F32)], 1)
        rows = pl.ds(pl.multiple_of(h * 2 * PAD, 2 * PAD), 2 * PAD)
        o_kvm[rows] = wide.astype(BF)
        code = pair[:, width:]
        o_kvc[rows] = code.astype(BF)
        o_kvct[h] = code.T.astype(BF)
        for i in range(2):
            dense = w[WP_VF : WP_VF + units, (2 + i) * width : (3 + i) * width]
            o_f[i, h] = dense
            o_ft[i, h] = dense.astype(F32).T.astype(BF)
        o_d[h] = w[WP_SD : WP_SD + width, 256 : 256 + units]
        o_dt[h] = w[WP_SD : WP_SD + units, 384 : 384 + width]

    put(meta[1], own)
    put(1 - meta[1], other)
    o_tt[...] = tw[...].T.astype(BF)


def step_kernel(
    planes, use_table,
    meta, idx, wcount, own_piece, z_pieces, xy_pieces, far_a, far_b, code_any, sin_any, kvc_any,
    srct, msg, sin_d, delta_all, ndelta_all, tcol,
    w_md, w_mc, w_q, w_kvm, w_kvct, w_f, w_ft, w_d, w_dt, w_tt, gin0, gst, gathered_in,
    o_fresh, o_own, o_other, o_live,
    sems, mem_all, code_n, sin_n, w_kvc, coarse, fine, near, qin, emb, keyt, count, stat, norm,
    scores, probs, fresh_s, att_s, gates, acc_m, tgrad,
):
    width, events = srct.shape
    units = width // 2
    nbrs = ndelta_all.shape[0]
    groups, full, wide_cols = mem_all.shape
    per_group = wide_cols // events
    lookups = (nbrs + 1) * events
    scale = 1.0 / math.sqrt(units)
    row_pos, head = meta[0], meta[1]
    hi_rows = count.shape[0]
    own_cols = pl.ds(pl.multiple_of(head * events, events), events)

    copies = []

    def start(src, dst):
        copy = pltpu.make_async_copy(src, dst, sems.at[len(copies)])
        copy.start()
        copies.append(copy)

    def bring(src, row, half, first, last):
        lanes = pl.ds(pl.multiple_of((lax.rem(row, 2) * 2 + half) * events, events), events)
        start(src, mem_all.at[lax.div(row, 2), pl.ds(first, last - first), lanes])

    cut = z_pieces[0].shape[1]
    for k in range(2):
        half = head ^ k
        bring(own_piece[k], row_pos, half, 0, full)
        for d in range(1, planes):
            bring(z_pieces[k].at[d - 1], row_pos ^ (d * PLANE), half, 0, cut)
        for d in range(1, PLANE):
            bring(xy_pieces[0][d - 1] if k == 0 else xy_pieces[1].at[d - 1], row_pos ^ d, half, 0, full)
            for e in range(1, planes):
                bring(far_a[k][d - 1].at[e - 1], row_pos ^ (e * PLANE + d), half, 0, cut)
        for e in range(1, planes):
            for d in range(PLANE):
                bring(far_b[k][e - 1].at[d], row_pos ^ (e * PLANE + d), half, cut, full)
    n_memory = len(copies)
    start(code_any, code_n)
    start(kvc_any, w_kvc)
    start(sin_any, sin_n)
    for copy in copies[:n_memory]:
        copy.wait()

    count[...] = jnp.zeros_like(count)
    norm[...] = jnp.zeros_like(norm)
    stat[...] = jnp.zeros_like(stat)
    target_t = w_tt[...]

    def keys_of(g):
        return nn(target_t, mem_all[g, 0:width]).astype(BF)

    def per_group_rows(g, table):
        x = mem_all[g]
        wide = x.astype(F32)
        keys = keys_of(g)
        if use_table:
            keyt[g, 0:width] = keys
        keys = keys.astype(F32)
        norm[0:1] = jnp.maximum(norm[0:1], jnp.sum(keys * keys, 0, keepdims=True))
        id_hi = wide[width : width + 1].astype(jnp.int32)
        id_lo = wide[width + 1 : width + 2].astype(jnp.int32)
        hot_hi = (lax.broadcasted_iota(jnp.int32, (hi_rows, wide_cols), 0) == id_hi).astype(BF)
        hot_lo = (lax.broadcasted_iota(jnp.int32, (LO_BASE, wide_cols), 0) == id_lo).astype(BF)
        count[...] += nt(hot_hi, hot_lo)
        here = wide[width + 2 : width + 3] * LO_BASE + wide[width + 3 : width + 4]
        for k in range(0, per_group, 2):
            stat[0:1, :] += here[:, k * events : k * events + 128]
        if table is not None:
            turned = wide.T
            base = pl.multiple_of(g * 2 * wide_cols, 2 * wide_cols)
            table[pl.ds(base, wide_cols, stride=2), :] = turned[:, :128]
            table[pl.ds(base + 1, wide_cols, stride=2), :] = jnp.concatenate(
                [turned[:, 128:], jnp.zeros((wide_cols, 256 - full), F32)], 1
            )

    def gather_rows(table, gathered):
        lax.fori_loop(0, groups, lambda g, s: (per_group_rows(g, table), s)[1], 0)
        unroll = 32

        def body(i, carry):
            for u in range(unroll):
                k = i * unroll + u
                gathered[pl.ds(pl.multiple_of(2 * k, 2), 2), :] = table[
                    pl.ds(pl.multiple_of(idx[k], 2), 2), :
                ]
            return carry

        lax.fori_loop(0, lookups // unroll, body, 0)
        for j in range(nbrs + 1):
            low = gathered[pl.ds(2 * j * events, events, stride=2), :]
            high = gathered[pl.ds(2 * j * events + 1, events, stride=2), :]
            near[pl.ds(j * events, events), :] = jnp.concatenate([low, high], 1).astype(BF)

    if use_table:
        pl.run_scoped(
            gather_rows,
            pltpu.VMEM((2 * groups * wide_cols, 128), F32),
            pltpu.VMEM((2 * lookups, 128), F32),
        )
    else:
        lax.fori_loop(0, groups, lambda g, s: (per_group_rows(g, None), s)[1], 0)
        near = gathered_in

    def count_lines(g, keys):
        at = g * (wide_cols // LO_BASE)
        line = jnp.concatenate(
            [count[pl.ds(at + k, 1), :] for k in range(wide_cols // LO_BASE)], 1
        )
        line = jnp.where(line > 0.5, jnp.log(jnp.maximum(line, 1.0)), -1e30)
        parts = split3(line)
        place = lax.broadcasted_iota(jnp.int32, (16, wide_cols), 0)
        first = full - 16
        tail = jnp.where(place >= width - first, 0.0, keys.astype(F32))
        for k in range(3):
            tail = jnp.where(place == width - first + k, parts[k].astype(F32), tail)
        return tail.astype(BF)

    if use_table:

        def add_lines(g, carry):
            keyt[g, full - 16 : full] = count_lines(g, keyt[g, full - 16 : full])
            return carry

        lax.fori_loop(0, groups, add_lines, 0)

    def keys_with_lines(g):
        if use_table:
            return keyt[g]
        keys = jnp.concatenate([keys_of(g).astype(F32), jnp.zeros((full - width, wide_cols), F32)], 0)
        keys = keys.astype(BF)
        return jnp.concatenate([keys[: full - 16], count_lines(g, keys[full - 16 :])], 0)

    live_rows = stat[0:1, 0:1]

    def rest(kvt, pair):
        dest = near[pl.ds(nbrs * events, events), :]
        dest_t = dest.astype(F32).T[:width]
        dest_key = nn(target_t, dest_t.astype(BF)).astype(BF)
        for h in range(2):
            gate_in = gin0[h] + nt(w_md[h], dest)
            gate_state = gst[h]
            reset = jax.nn.sigmoid(gate_in[:units] + gate_state[:units])
            update = jax.nn.sigmoid(
                gate_in[units : 2 * units] + gate_state[units : 2 * units]
            )
            state_c = gate_state[2 * units :]
            candidate = jnp.tanh(gate_in[2 * units :] + reset * state_c)
            for k, v in enumerate((reset, update, candidate, state_c)):
                gates[h, k] = v
            fresh = (1.0 - update) * candidate + update * srct[h * units : (h + 1) * units]
            o_fresh[h] = fresh
            qin[h * units : (h + 1) * units] = fresh
        zero_sin, zero_cos = sin_cos(tcol[...])
        qin[width : 2 * width] = jnp.broadcast_to(zero_cos[:, 1:2], (width, events))
        query_in = qin[...].astype(BF)
        copies[n_memory].wait()
        copies[n_memory + 1].wait()

        def project(j, carry):
            cols = pl.ds(pl.multiple_of(j * events, events), events)
            kvt[:, cols] = nt(w_kvm[...], near[cols, :]) + nn(w_kvc[...], code_n[:, cols])
            return carry

        lax.fori_loop(0, nbrs, project, 0)
        attended_low = []
        for h in range(2):
            key_at, value_at = h * 2 * PAD, h * 2 * PAD + PAD
            queries = nn(w_q[h], query_in)
            fresh_s[h, :units] = queries
            for j in range(nbrs):
                cols = pl.ds(j * events, events)
                scores[j : j + 1] = (
                    jnp.sum(queries * kvt[key_at : key_at + units, cols], 0, keepdims=True) * scale
                )
            score = scores[0:nbrs]
            grown = jnp.exp(score - jnp.max(score, 0, keepdims=True))
            prob = grown / jnp.sum(grown, 0, keepdims=True)
            probs[h, 0:nbrs] = prob
            total = jnp.zeros((units, events), F32)
            for j in range(nbrs):
                cols = pl.ds(j * events, events)
                total = total + prob[j : j + 1] * kvt[value_at : value_at + units, cols]
            att_s[h, :units] = total
            attended_low.append(total.astype(BF))
        fresh_lows = [qin[h * units : (h + 1) * units].astype(BF) for h in range(2)]
        hidden = (nn(w_ft[0, 0], attended_low[0]) + nn(w_ft[0, 1], attended_low[1])) + (
            nn(w_ft[1, 0], fresh_lows[0]) + nn(w_ft[1, 1], fresh_lows[1])
        )
        sigmoid_h = jax.nn.sigmoid(hidden)
        mixed_low = (hidden * sigmoid_h).astype(BF)
        emb_halves = [nn(w_dt[h], mixed_low) for h in range(2)]
        emb[0:units] = emb_halves[0]
        emb[units:width] = emb_halves[1]
        emb_low = emb[...].astype(BF)
        ones_line = (lax.broadcasted_iota(jnp.int32, (full - width, events), 0) < 3).astype(F32)
        emb_aug = jnp.concatenate([LOGIT_SCALE * emb_low.astype(F32), ones_line], 0)
        emb_rows = emb_aug.T.astype(BF)
        emb_norm = jnp.max(jnp.sum(emb[...] * emb[...], 0, keepdims=True))
        bound = LOGIT_SCALE * LOGIT_SCALE * emb_norm * jnp.max(norm[0:1])
        own_logit = LOGIT_SCALE * jnp.sum(
            emb_low.astype(F32) * dest_key.astype(F32), 0, keepdims=True
        )

        def soft_section(acc, top, total):
            total[...] = jnp.zeros_like(total)
            acc[...] = jnp.zeros_like(acc)
            small = bound < SAFE_LOGIT * SAFE_LOGIT

            @pl.when(small)
            def _():
                top[...] = jnp.zeros_like(top)

                def body(g, carry):
                    grown = jnp.exp(nn(emb_rows, keys_with_lines(g)))
                    lanes = grown[:, 0:128]
                    for k in range(1, wide_cols // 128):
                        lanes = lanes + grown[:, k * 128 : (k + 1) * 128]
                    total[...] += lanes
                    acc[...] += nt(grown.astype(BF), mem_all[g])
                    return carry

                lax.fori_loop(0, groups, body, 0)
                total[...] = jnp.broadcast_to(jnp.sum(total[...], 1, keepdims=True), total.shape)

            @pl.when(jnp.logical_not(small))
            def _():
                top[...] = jnp.full_like(top, -1e30)

                def body(g, carry):
                    logits = nn(emb_rows, keys_with_lines(g))
                    old = top[:, 0:1]
                    new = jnp.maximum(old, jnp.max(logits, 1, keepdims=True))
                    grown = jnp.exp(logits - new)
                    fade = jnp.exp(old - new)
                    total[...] = total[...] * fade + jnp.sum(grown, 1, keepdims=True)
                    top[...] = jnp.broadcast_to(new, top.shape)
                    acc[...] = acc[...] * fade + nt(grown.astype(BF), mem_all[g])
                    return carry

                lax.fori_loop(0, groups, body, 0)

            acc_m[...] = (acc[...] / total[:, 0:1]).T
            probs[2] = jnp.broadcast_to(top[:, 0:1] + jnp.log(total[:, 0:1]), (events, 128)).T[:16]

        pl.run_scoped(
            soft_section,
            pltpu.VMEM((events, full), F32),
            pltpu.VMEM((events, 128), F32),
            pltpu.VMEM((events, 128), F32),
        )
        log_total = probs[2, 0:1]
        position = lax.broadcasted_iota(jnp.int32, (1, events), 1) + head * events
        live = (position < wcount[0]).astype(F32)
        loss = jnp.sum((log_total - own_logit) * live, 1, keepdims=True)
        weight = live / live_rows
        own_prob = jnp.exp(own_logit - log_total)
        own_grad = ((own_prob - 1.0) * weight).astype(BF).astype(F32) - own_prob * weight
        mean_mem = acc_m[:width]
        spread = weight * mean_mem + own_grad * dest_t
        parts = split3(spread)
        target_grad = LOGIT_SCALE * (nt(parts[0], emb_low) + nt(parts[1], emb_low) + nt(parts[2], emb_low))
        parts = split3(mean_mem)
        mean_key = nn(target_t, parts[0]) + nn(target_t, parts[1]) + nn(target_t, parts[2])
        emb_grad = LOGIT_SCALE * (weight * mean_key + own_grad * dest_key.astype(F32))

        coarse[...] = jnp.zeros_like(coarse)
        fine[...] = jnp.zeros_like(fine)
        blocks = state_blocks(units)
        quarter = units // 2

        def slot(h):
            return h ^ head

        emb_grad_low = [emb_grad[h * units : (h + 1) * units].astype(BF) for h in range(2)]
        mixed_grad = nn(w_d[0], emb_grad_low[0]) + nn(w_d[1], emb_grad_low[1])
        hidden_grad = (mixed_grad * sigmoid_h * (1.0 + hidden * (1.0 - sigmoid_h))).astype(BF)
        for h in range(2):
            second = nt(mixed_low, emb_grad_low[h])
            place = slot(h)
            for i, v in enumerate((attended_low[h], fresh_lows[h])):
                fine[place, units:width, (2 + i) * width : (3 + i) * width] = nt(v, hidden_grad)
            for k in range(2):
                fine[place, ROW_T : ROW_T + quarter, k * width : (k + 1) * width] = target_grad[
                    h * units + k * quarter : h * units + (k + 1) * quarter
                ]
            for k in range(4):
                at = 2 * width + k * units
                fine[place, ROW_T : ROW_T + quarter, at : at + units] = second[
                    k * quarter : (k + 1) * quarter
                ]

        copies[n_memory + 2].wait()
        tgrad[...] = jnp.zeros_like(tgrad)
        query_lows = []
        prob_terms = []
        att_grads = []
        for h in range(2):
            value_at = h * 2 * PAD + PAD
            att_grad = nn(w_f[0, h], hidden_grad)
            prob = probs[h, 0:nbrs]
            for j in range(nbrs):
                cols = pl.ds(j * events, events)
                scores[j : j + 1] = jnp.sum(
                    att_grad * kvt[value_at : value_at + units, cols], 0, keepdims=True
                )
            prob_grad = scores[0:nbrs]
            prob_terms.append(prob * (prob_grad - jnp.sum(prob * prob_grad, 0, keepdims=True)))
            att_grads.append(att_grad)
            total = jnp.zeros((units, events), F32)
            key_at = h * 2 * PAD
            for j in range(nbrs):
                cols = pl.ds(j * events, events)
                total = total + prob_terms[h][j : j + 1] * kvt[key_at : key_at + units, cols]
            query_lows.append((total * scale).astype(BF))
        fill = jnp.zeros((PAD - units, events), F32)
        for j in range(nbrs):
            cols = pl.ds(j * events, events)
            pieces = []
            for h in range(2):
                pieces += [
                    (prob_terms[h][j : j + 1] * scale) * fresh_s[h, :units], fill,
                    probs[h, j : j + 1] * att_grads[h], fill,
                ]
            pair_j = jnp.concatenate(pieces, 0).astype(BF)
            pair[:, cols] = pair_j
            code_grad = nn(w_kvct[0], pair_j[: 2 * PAD]) + nn(w_kvct[1], pair_j[2 * PAD :])
            slope = sin_n[:, cols].astype(F32) * code_grad
            tgrad[1, :width] -= slope
            tgrad[0, :width] -= slope * ndelta_all[j : j + 1, own_cols]
        near_grad = nn(pair[...], near[pl.ds(0, nbrs * events), :])
        code_wgrad = nt(pair[...], code_n[...])
        for h in range(2):
            place = slot(h)
            base = h * 2 * PAD
            query_grad = nt(query_lows[h], query_in)
            fine[place, 0:units, 0 : 2 * width] = query_grad
            for k, (row, lane) in enumerate(((0, 2 * width), (units, 0))):
                at = base + k * PAD
                fine[place, row : row + units, lane : lane + width] = near_grad[
                    at : at + units, :width
                ]
                fine[place, row : row + units, lane + width : lane + 2 * width] = code_wgrad[
                    at : at + units
                ]
        query_in_grad = tn(w_q[0], query_lows[0]) + tn(w_q[1], query_lows[1])
        zero_term = zero_sin[:, 1:2] * query_in_grad[width:]
        tgrad[1, :width] -= zero_term

        def send_fine(k):
            for place, out in ((1, o_other), (0, o_own)):
                start(fine.at[place, pl.ds(k * FINE, FINE)], out.at[k, pl.ds(COARSE, FINE)])

        for k in range(3):
            send_fine(k)

        code_dt_grad = jnp.zeros((width, events), F32)
        ones = jnp.ones((8, events), BF)
        for h in range(2):
            place = slot(h)
            reset, update, candidate, state_c = (gates[h, k] for k in range(4))
            fresh_grad = nn(w_f[1, h], hidden_grad) + query_in_grad[h * units : (h + 1) * units]
            own_state = srct[h * units : (h + 1) * units]
            candidate_pre = fresh_grad * (1.0 - update) * (1.0 - candidate * candidate)
            update_pre = fresh_grad * (own_state - candidate) * update * (1.0 - update)
            reset_pre = candidate_pre * state_c * reset * (1.0 - reset)
            in_grad = jnp.concatenate([reset_pre, update_pre, candidate_pre], 0).astype(BF)
            state_grad = jnp.concatenate([reset_pre, update_pre, candidate_pre * reset], 0).astype(BF)
            gate_rows = 3 * units
            coarse[place, 0:gate_rows, width : 2 * width] = nn(in_grad, dest)[:, :width]
            rest_grad = nt(in_grad, msg[...])
            coarse[place, 0:gate_rows, 0:width] = rest_grad[:, :width]
            coarse[place, 0:gate_rows, 2 * width : 4 * width] = rest_grad[:, width:]
            state_w = nt(msg[0:width], state_grad)
            coarse[place, 0:width, 4 * width : 4 * width + gate_rows - 256] = state_w[:, 256:]
            for k, (first, last) in enumerate(blocks):
                coarse[place, gate_rows : gate_rows + last - first, k * 256 : (k + 1) * 256] = state_w[
                    first:last, 0:256
                ]
            fine[place, ROW_B : ROW_B + 1, 0:gate_rows] = nt(ones, in_grad)[0:1]
            fine[place, ROW_B + 1 : ROW_B + 2, 0:gate_rows] = nt(ones, state_grad)[0:1]
            code_dt_grad = code_dt_grad + tn(w_mc[h], in_grad)
        slope = sin_d[...] * code_dt_grad
        tgrad[1, :width] -= slope
        tgrad[0, :width] -= slope * delta_all[:, own_cols]
        ones_f = jnp.ones((8, events), F32)
        for i in range(2):
            line = lax.dot_general(
                ones_f, tgrad[i, :width], (((1,), (1,)), ((), ())),
                precision=lax.Precision.HIGHEST, preferred_element_type=F32,
            )[0:1]
            for place in range(2):
                fine[place, ROW_B + 2 + i : ROW_B + 3 + i, 0:width] = line
        for place in range(2):
            fine[place, ROW_B + 4 : ROW_B + 5, 0:128] = jnp.broadcast_to(loss, (1, 128))
        o_live[...] = jnp.broadcast_to(stat[0:1, :], o_live.shape)
        send_fine(3)
        for k in range(4):
            for place, out in ((1, o_other), (0, o_own)):
                start(coarse.at[place, pl.ds(k * COARSE, COARSE)], out.at[k, pl.ds(0, COARSE)])
        for copy in copies[n_memory + 3 :]:
            copy.wait()

    pl.run_scoped(
        rest,
        pltpu.VMEM((4 * PAD, nbrs * events), F32),
        pltpu.VMEM((4 * PAD, nbrs * events), BF),
    )


COARSE, FINE, LANES = 80, 64, 768
ROWS = COARSE + FINE
EXTRA = 16
ROW_T, ROW_B = 192, 240


def state_blocks(units):
    room = 4 * COARSE - 3 * units
    return [(k * room, min((k + 1) * room, 2 * units)) for k in range(3)]


def to_half_wire(out, value):
    high = value.astype(BF)
    out[0:ROWS] = high
    out[ROWS:] = (value - high.astype(F32))[ROWS - EXTRA :].astype(BF)


def from_half_wire(w):
    high = w[0:ROWS].astype(F32)
    last = high[ROWS - EXTRA :] + w[ROWS:].astype(F32)
    return jnp.concatenate([high[: ROWS - EXTRA], last], 0)


def to_wire(out, value):
    high = value.astype(BF)
    out[0:ROWS] = high
    out[ROWS:] = (value - high.astype(F32)).astype(BF)


def from_wire(w):
    return w[0:ROWS].astype(F32) + w[ROWS:].astype(F32)


def first_sum_kernel(bits, own, got, o_keep, o_send):
    for k in range(2):
        q = bits[0] * 2 + k
        o_keep[k] = own[q] + got[q]
        q = (1 - bits[0]) * 2 + k
        to_half_wire(o_send.at[k], own[q] + got[q])


def second_sum_kernel(bits, keep, got, o_keep, o_send):
    q = bits[1]
    o_keep[...] = keep[q] + from_half_wire(got[q])
    q = 1 - bits[1]
    to_half_wire(o_send, keep[q] + from_half_wire(got[q]))


def third_sum_kernel(keep, got, o_send):
    to_wire(o_send, keep[...] + from_half_wire(got[...]))


def wire_sum_kernel(one, two, o_send):
    to_wire(o_send, from_wire(one[...]) + from_wire(two[...]))


def quarter_of(bits, k):
    one = bits[0] if k < 2 else 1 - bits[0]
    two = bits[1] if k % 2 == 0 else 1 - bits[1]
    return one * 2 + two


def shared_kernel(bits, w0, w1, w2, w3, out):
    for k, w in enumerate((w0, w1, w2, w3)):

        @pl.when(quarter_of(bits, k) == 3)
        def _(w=w):
            out[0:FINE] = w[COARSE:ROWS]
            out[FINE:] = w[ROWS + COARSE :]


def adam_kernel(bits, w0, w1, w2, w3, *refs):
    params, outs = refs[:18], refs[18:36]
    coarse, fine = refs[36:]
    for k, w in enumerate((w0, w1, w2, w3)):
        q = quarter_of(bits, k)
        value = from_wire(w[...])
        coarse[pl.ds(pl.multiple_of(q * COARSE, COARSE), COARSE)] = value[0:COARSE]
        fine[pl.ds(pl.multiple_of(q * FINE, FINE), FINE)] = value[COARSE:]
    units, gates = params[15].shape[1], params[3].shape[1]
    width = 2 * units

    def step(which, at, gradient):
        values = [params[3 * which + i][at] for i in range(3)]
        for i, v in enumerate(adam_step(*values, gradient)):
            outs[3 * which + i][at] = v

    every = (slice(None), slice(None))
    step(0, every, coarse[0:gates, 0 : 4 * width])
    for k, (first, last) in enumerate(state_blocks(units)):
        step(
            1, (slice(first, last), slice(0, 256)),
            coarse[gates : gates + last - first, k * 256 : (k + 1) * 256],
        )
    step(1, (slice(None), slice(256, gates)), coarse[0:width, 4 * width : 4 * width + gates - 256])
    step(2, every, fine[ROW_B : ROW_B + 2, 0:gates])
    step(3, 0, fine[0:units, 0 : 2 * width])
    step(3, 1, fine[0:units, 2 * width : 4 * width])
    step(3, 2, fine[units:width, 0 : 2 * width])
    for i in range(2):
        step(4, (slice(None), i), fine[units:width, (2 + i) * width : (3 + i) * width])
    quarter = units // 2
    for k in range(4):
        at = 2 * width + k * units
        step(5, (slice(k * quarter, (k + 1) * quarter), slice(None)), fine[ROW_T : ROW_T + quarter, at : at + units])


def shared_adam_kernel(meta, own, other, *refs):
    params, outs, o_loss = refs[:6], refs[6:12], refs[12]
    width = params[0].shape[0]
    quarter = width // 4

    def step(which, at, gradient):
        values = [params[3 * which + i][at] for i in range(3)]
        for i, v in enumerate(adam_step(*values, gradient)):
            outs[3 * which + i][at] = v

    def run(first, second):
        parts = [w[0:FINE].astype(F32) + w[FINE:].astype(F32) for w in (first, second)]
        for h in range(2):
            for k in range(2):
                at = (h * 2 + k) * quarter
                step(
                    0, (slice(at, at + quarter), slice(None)),
                    parts[h][0:quarter, k * width : (k + 1) * width],
                )
        row = ROW_B - 3 * FINE
        step(1, (slice(None), slice(None)), parts[0][row + 2 : row + 4, 0:width])
        o_loss[...] = jnp.broadcast_to(parts[0][row + 4 : row + 5, 0:128], o_loss.shape)

    @pl.when(meta[1] == 0)
    def _():
        run(own, other)

    @pl.when(meta[1] == 1)
    def _():
        run(other, own)


def memory_kernel(mem, fresh, src, wcount, out):
    units, rows = mem.shape
    pick = (lax.broadcasted_iota(jnp.int32, (rows, rows), 1) == src[...]).astype(BF)
    parts = split3(fresh[...])
    moved = nn(parts[0], pick) + nn(parts[1], pick) + nn(parts[2], pick)
    alive = (lax.broadcasted_iota(jnp.int32, (16, rows), 1) < wcount[0]).astype(BF)
    hit = nn(alive, pick)[0:1] > 0.5
    out[...] = jnp.where(hit, moved, mem[...])


def adam_step(master, moment, square, gradient):
    moment_new = BETA_ONE * moment + (1.0 - BETA_ONE) * gradient
    square_new = BETA_TWO * square + (1.0 - BETA_TWO) * gradient * gradient
    master_new = master - RATE * (moment_new / (1.0 - BETA_ONE**STEP)) / (
        jnp.sqrt(square_new / (1.0 - BETA_TWO**STEP)) + EPSILON
    )
    return (master_new, moment_new, square_new)


def axis_orders(n_row):
    bits = []
    step = PLANE
    while step < n_row:
        bits.append(step)
        step *= 2
    first = [1, 2] + bits
    second = bits[:2] + [1, 2] + bits[2:]
    return list(zip(first, second))


def flips(count, step):
    return [(i, i ^ step) for i in range(count)]


def per_device(
    n_row,
    memory, sources, dest_ids, neighbours, delta_t, nbr_delta, edge_feat, window_count,
    message_weight, message_weight_moment, message_weight_square,
    state_weight, state_weight_moment, state_weight_square,
    gate_bias, gate_bias_moment, gate_bias_square,
    time_param, time_param_moment, time_param_square,
    attend_weight, attend_weight_moment, attend_weight_square,
    dense_first, dense_first_moment, dense_first_square,
    dense_second, dense_second_moment, dense_second_square,
    target_weight, target_weight_moment, target_weight_square,
):
    rows, width = memory.shape
    units = width // 2
    events = rows // 2
    nbrs = neighbours.shape[1]
    planes = n_row // PLANE
    total_rows = n_row * rows
    head = lax.axis_index("head")
    row = lax.axis_index("row")
    meta = jnp.stack([row, head]).astype(jnp.int32)

    def own(x, axis):
        return lax.dynamic_slice_in_dim(x, head * events, events, axis)

    def swap(x):
        return lax.ppermute(x, "head", [(0, 1), (1, 0)])

    def hop(x, step):
        return lax.ppermute(x, "row", flips(n_row, step))

    bf = functools.partial(shape, dtype=BF)
    full = -(-(width + 4) // 16) * 16

    mem_t = memory.T
    block = vmem_call(block_kernel, bf(full, events), "ssvv", micros=1)(
        meta, window_count, mem_t, dest_ids[None]
    )
    cut = 128
    near_z = [hop(block[:cut], e * PLANE) for e in range(1, planes)]
    near_xy = [hop(block, d) for d in range(1, PLANE)]
    mw, aw, gb = message_weight.T, attend_weight.transpose(0, 2, 1), gate_bias
    packed = vmem_call(pack_weights_kernel, bf(WP_ROWS, WP_LANES), "vvvvvv", limit=VMEM_SMALL, micros=2)(
        mw, state_weight, aw, dense_first, dense_second, gb
    )
    line_a = jnp.stack(near_z)
    plane_b = jnp.stack([block[cut:]] + [p[cut:] for p in near_xy])
    line_a, plane_b = lax.optimization_barrier((line_a, plane_b))
    packed, _ = lax.optimization_barrier((packed, line_a))
    packed_o = swap(packed)
    far_a = tuple(hop(line_a, d) for d in range(1, PLANE))
    far_b = tuple(hop(plane_b, e * PLANE) for e in range(1, planes))
    delta, ndelta, edge, tcol, packed_o, _ = lax.optimization_barrier(
        (delta_t[None], nbr_delta.T, edge_feat.T, time_param.T, packed_o, plane_b)
    )
    code_shapes = (
        shape(width, events), bf(3 * width, events), shape(width, events),
        bf(width, nbrs * events), bf(width, nbrs * events),
    )
    srct, msg, sin_d, code_n, sin_n = vmem_call(codes_kernel, code_shapes, "svvvvvv", micros=9)(
        meta, mem_t, sources, delta, ndelta, tcol, edge
    )
    w_shapes = (
        bf(2, 3 * units, 256), bf(2, 3 * units, width), bf(2, units, 2 * width),
        bf(4 * PAD, 256), bf(4 * PAD, width), bf(2, width, 2 * PAD),
        bf(2, 2, units, width), bf(2, 2, width, units), bf(2, width, units), bf(2, units, width),
        bf(width, width), shape(2, 3 * units, events), shape(2, 3 * units, events),
    )
    w_md, w_mc, w_q, w_kvm, w_kvc, *w_more = vmem_call(weights_kernel, w_shapes, "svvvv", micros=6)(
        meta, packed, packed_o, target_weight, msg
    )

    far_a, far_b, _ = lax.optimization_barrier((far_a, far_b, w_md))
    block, line_a, near_xy, _ = lax.optimization_barrier((block, line_a, near_xy, srct))
    own_piece = (block, swap(block))
    z_pieces = (line_a, swap(line_a))
    xy_pieces = (tuple(near_xy), swap(jnp.stack(near_xy)))
    far_a = (far_a, tuple(swap(p) for p in far_a))
    far_b = (far_b, tuple(swap(p) for p in far_b))

    index = jnp.concatenate([own(neighbours.T, 1).reshape(-1), own(dest_ids, 0)])
    use_table = total_rows <= TABLE_ROWS_MAX
    lookups = (nbrs + 1) * events
    if use_table:
        gathered = tcol
    else:
        parts = {}
        for k in range(2):
            parts[0, 0, k] = own_piece[k]
            for e in range(1, planes):
                parts[e, 0, k] = jnp.concatenate([z_pieces[k][e - 1], far_b[k][e - 1][0]], 0)
            for d in range(1, PLANE):
                parts[0, d, k] = xy_pieces[k][d - 1]
                for e in range(1, planes):
                    parts[e, d, k] = jnp.concatenate([far_a[k][d - 1][e - 1], far_b[k][e - 1][d]], 0)
        table = jnp.stack([parts[e, d, k].T for e in range(planes) for d in range(PLANE) for k in range(2)])
        half = (index % rows) // events
        gathered = table[((index // rows) ^ row) * 2 + (half ^ head), index % events]
        gathered = jnp.pad(gathered, ((0, 0), (0, 256 - full)))
    hi_rows = total_rows // LO_BASE
    wide_cols = 4 * events
    groups = total_rows // wide_cols
    n_copies = 2 * (1 + (planes - 1) + (PLANE - 1) * planes + (planes - 1) * PLANE) + 3 + 16
    scratch = [
        pltpu.SemaphoreType.DMA((n_copies,)),
        pltpu.VMEM((groups, full, wide_cols), BF),
        pltpu.VMEM((width, nbrs * events), BF),
        pltpu.VMEM((width, nbrs * events), BF),
        pltpu.VMEM((4 * PAD, width), BF),
        pltpu.VMEM((2, 4 * COARSE, LANES), F32),
        pltpu.VMEM((2, 4 * FINE, LANES), F32),
        pltpu.VMEM((lookups if use_table else 16, 256), BF),
        pltpu.VMEM((2 * width, events), F32),
        pltpu.VMEM((width, events), F32),
        pltpu.VMEM((groups if use_table else 1, full, wide_cols), BF),
        pltpu.VMEM((hi_rows, LO_BASE), F32),
        pltpu.VMEM((8, 128), F32),
        pltpu.VMEM((8, wide_cols), F32),
        pltpu.VMEM((16, events), F32),
        pltpu.VMEM((3, 16, events), F32),
        pltpu.VMEM((2, PAD, events), F32),
        pltpu.VMEM((2, PAD, events), F32),
        pltpu.VMEM((2, 4, units, events), F32),
        pltpu.VMEM((full, events), F32),
        pltpu.VMEM((2, PAD * 2, events), F32),
    ]
    spaces = [
        "s", "s", "s", ["a", "a"], ["a", "a"], [["a"] * (PLANE - 1), "a"],
        [["a"] * (PLANE - 1)] * 2, [["a"] * (planes - 1)] * 2, "a", "a", "a",
    ] + ["v"] * 19
    fresh, pack_own, pack_other, live = vmem_call(
        functools.partial(step_kernel, planes, use_table),
        (
            shape(2, units, events), shape(4, ROWS, LANES), shape(4, ROWS, LANES), shape(8, 128),
        ),
        spaces,
        scratch,
        VMEM_LIMIT if use_table else VMEM_WHOLE,
        micros=40,
        in_place=(shape(4, ROWS, LANES),),
    )(
        meta, 2 * index, window_count, own_piece, z_pieces, xy_pieces, far_a, far_b, code_n, sin_n, w_kvc,
        srct, msg, sin_d, delta, ndelta, tcol, w_md, w_mc, w_q, w_kvm, *w_more, gathered,
    )

    fresh_own = lax.dynamic_index_in_dim(fresh, head, 0, False)
    fresh_sent = swap(lax.dynamic_index_in_dim(fresh, 1 - head, 0, False))
    both = jnp.where(
        head == 0,
        jnp.concatenate([fresh_own, fresh_sent], 1),
        jnp.concatenate([fresh_sent, fresh_own], 1),
    )
    base_cols = lax.dynamic_slice_in_dim(mem_t, head * units, units, 0)
    new_memory = vmem_call(memory_kernel, shape(units, rows), "vvvs", limit=VMEM_SMALL, micros=3)(
        base_cols, both, sources.reshape(rows, 1), window_count
    ).T

    orders = axis_orders(n_row)

    def joint_hop(x, steps):
        pairs = [(2 * i + c, 2 * (i ^ steps[c]) + c) for i in range(n_row) for c in range(2)]
        return lax.ppermute(x, ("row", "head"), pairs)

    bits = jnp.stack(
        [jnp.where(head == 0, (row // steps[0]) % 2, (row // steps[1]) % 2) for steps in orders[:2]]
    ).astype(jnp.int32)
    wire = bf(2 * ROWS, LANES)
    keep, send = vmem_call(
        first_sum_kernel, (shape(2, ROWS, LANES), bf(2, ROWS + EXTRA, LANES)), "svv", limit=VMEM_SMALL, micros=1
    )(bits, pack_own, swap(pack_other))
    keep, send = vmem_call(
        second_sum_kernel, (shape(ROWS, LANES), bf(ROWS + EXTRA, LANES)), "svv", limit=VMEM_SMALL, micros=1
    )(bits, keep, joint_hop(send, orders[0]))
    total = vmem_call(third_sum_kernel, wire, "vv", limit=VMEM_SMALL, micros=1)(keep, joint_hop(send, orders[1]))
    for steps in orders[2:]:
        total = vmem_call(wire_sum_kernel, wire, "vv", limit=VMEM_SMALL, micros=1)(total, joint_hop(total, steps))
    second_q = joint_hop(total, orders[1])
    first_q = joint_hop(total, orders[0])
    last_q = joint_hop(second_q, orders[0])
    quarters = (total, second_q, first_q, last_q)
    shared = vmem_call(shared_kernel, bf(2 * FINE, LANES), "svvvv", limit=VMEM_SMALL, micros=1)(bits, *quarters)
    shared_o = swap(shared)

    def turned(x):
        return x.transpose(0, 2, 1)

    def middle(x):
        return x.transpose(1, 0, 2)

    views = (lambda x: x.T, lambda x: x, lambda x: x, turned, middle, lambda x: x)
    params = (
        message_weight, message_weight_moment, message_weight_square,
        state_weight, state_weight_moment, state_weight_square,
        gate_bias, gate_bias_moment, gate_bias_square,
        attend_weight, attend_weight_moment, attend_weight_square,
        dense_first, dense_first_moment, dense_first_square,
        dense_second, dense_second_moment, dense_second_square,
    )
    params = [views[i // 3](p) for i, p in enumerate(params)]
    stepped = vmem_call(
        adam_kernel, tuple(shape(*p.shape) for p in params), "svvvv" + "v" * 18,
        [pltpu.VMEM((4 * COARSE, LANES), F32), pltpu.VMEM((4 * FINE, LANES), F32)], limit=VMEM_ADAM, micros=4,
    )(bits, *quarters, *params)
    back = (lambda x: x.T, lambda x: x, lambda x: x, turned, middle, lambda x: x)
    stepped = [back[i // 3](p) for i, p in enumerate(stepped)]
    rest = (
        target_weight, target_weight_moment, target_weight_square,
        time_param, time_param_moment, time_param_square,
    )
    *others, loss = vmem_call(
        shared_adam_kernel, tuple(shape(*p.shape) for p in rest) + (shape(8, 128),), "svv" + "v" * 6, limit=VMEM_SMALL, micros=2
    )(meta, shared, shared_o, *rest)
    return (
        new_memory, loss[0, 0], live[0, 0], *stepped[:9], *others[3:], *stepped[9:], *others[:3],
    )


def solution(mesh):
    cols = P(None, "head")
    third = P(None, None, "head")
    middle = P(None, "head", None)
    by_row = P("row", None)
    in_specs = (
        (by_row, by_row, P("row"), by_row, P("row"), by_row, by_row, P("row"))
        + (cols,) * 9 + (P(),) * 3 + (third,) * 3 + (middle,) * 3 + (cols,) * 3 + (P(),) * 3
    )
    out_specs = (
        (P("row", "head"), P(), P())
        + (cols,) * 9 + (P(),) * 3 + (third,) * 3 + (middle,) * 3 + (cols,) * 3 + (P(),) * 3
    )
    return jax.shard_map(
        functools.partial(per_device, mesh.shape["row"]),
        mesh=mesh, in_specs=in_specs, out_specs=out_specs, check_vma=False,
    )
```

time: 298 us -> 192 us (0.64)
  waiting for transfers between devices: 141 us -> 61.3 us
  other arithmetic: 25.2 us -> 2.65 us
  local copies, waits for them, and re-layouts: 20.4 us -> 10.3 us
  Pallas kernels: 75.2 us -> 84.9 us
    ppermute x18 -> x12, waiting for transfers between devices: 136 us -> 10 us  [hop(): return lax.ppermute(x, 'row', flips(n_row, step))]
    ppermute x0 -> x7, waiting for transfers between devices: none -> 45.9 us  [joint_hop(): return lax.ppermute(x, ('row', 'head'), pairs)]
    ppermute x18 -> x12, starting transfers between devices: 30.1 us -> 16.9 us  [hop(): return lax.ppermute(x, 'row', flips(n_row, step))]
    ppermute x0 -> x7, starting transfers between devices: none -> 10.9 us  [joint_hop(): return lax.ppermute(x, ('row', 'head'), pairs)]
    pallas_call x3 -> x13, Pallas kernels: 16.7 us -> 27.6 us  [the longest x1 8.98 us: per_device(): vmem_call(codes_kernel, code_shapes, 'svvvvvv', micros=9)]
    another operation x9 -> x4, other arithmetic: 10.6 us -> 0.21 us  [the longest x1 0.07 us: per_device(): jnp.stack([jnp.where(head == 0, row // steps[0] % 2, row // steps[1] % 2)...]
    transpose x2 -> x0, other arithmetic: 4.47 us -> none  [the longest x1 3.17 us: per_device(): message_out = tuple((x.T for x in message_out))]
    sub x6 -> x0, other arithmetic: 3.94 us -> none  [adam_step(): master - RATE * (moment_new / (1.0 - BETA_ONE ** STEP)) / (jnp.sqrt(squar...]
  transfers between devices with their start and end apart: 29 -> 32, of which waited for: 17 -> 12; matrix products, arithmetic and copies ran while one was open for 7% -> 4% of each run, Pallas kernels for 6% -> 11%
where the time goes in v1:
time: 192 us
  Pallas kernels  84.9 us (44%)
  waiting for transfers between devices  61.3 us (32%)
  starting transfers between devices  30.6 us (16%)
  local copies, waits for them, and re-layouts  10.3 us (5%)
  other arithmetic  2.65 us (1%)
  between operations  2.12 us (1%)
    pallas_call x1, Pallas kernels, per_device(): vmem_call(functools.partial(step_kernel, planes, use_table), (shape(2, un...  57.3 us
    ppermute x7, waiting for transfers between devices, joint_hop(): return lax.ppermute(x, ('row', 'head'), pairs)  45.9 us
    ppermute x12, starting transfers between devices, hop(): return lax.ppermute(x, 'row', flips(n_row, step))  16.9 us
    ppermute x7, starting transfers between devices, joint_hop(): return lax.ppermute(x, ('row', 'head'), pairs)  10.9 us
    ppermute x12, waiting for transfers between devices, hop(): return lax.ppermute(x, 'row', flips(n_row, step))  10 us
    pallas_call x1, Pallas kernels, per_device(): vmem_call(codes_kernel, code_shapes, 'svvvvvv', micros=9)  8.98 us
    ppermute x13, waiting for transfers between devices, swap(): return lax.ppermute(x, 'head', [(0, 1), (1, 0)])  5.41 us
    pallas_call x1, Pallas kernels, per_device(): vmem_call(adam_kernel, tuple((shape(*p.shape) for p in params)), 'svvvv'...  4.98 us
  transfers between devices with their start and end apart: 32, of which 12 were waited for; matrix products, arithmetic and copies ran while one was open for 4% of the time, Pallas kernels for 11%

profile of v1, /device:TPU:0, one launch (start us, length us, event | category | flops | bytes accessed | tf_op | source)
XLA Modules:
  0.0 191.8 jit_solution(12097179867148740997)
XLA Ops:
  1.4 0.6 pad_add_fusion.meta
  2.0 1.9 %shard_map.511.own_piece_0_ = bf16[176,512]{1,0:T(8,128)(2,1)} custom-call(s32[2]{0:T(128)} %pad_add_fusion.meta, s32[1]{0:T(128)S(6)} %copy.64.wcount, f32[172,1024]{1,0:T(8,128)} %bitcast.68, s32[1,1024]{1,0:T(1,128)} %bitcast.77), custom_call_target="tpu_custom_call" | custom-call | flops 1000000000 | bytes 1000000 | tf_op jit(solution)/shard_map/pallas_call | solution.py:831
  3.9 3.9 %collective-permute-start.5 = (bf16[176,512]{1,0:T(8,128)(2,1)}, bf16[176,512]{1,0:T(8,128)(2,1)S(1)}, u32[]{:S(2)}, u32[]{:S(2)}) collective-permute-start(bf16[176,512]{1,0:T(8,128)(2,1)} %shard_map.511.own_piece_0_), channel_id=1, source_target_pairs={{0,6},{2,4},{4,2},{6,0},{8,14},{10,12},{12,10},{14,8},{16,22},{18,... | collective-permute-start | bytes 540680 | tf_op jit(solution)/shard_map/ppermute | solution.py:825
  7.8 0.5 collective-permute-start.4
  8.3 0.9 slice.30
  9.3 1.6 collective-permute-start
  10.9 2.6 %collective-permute-start.1 = (bf16[128,512]{1,0:T(8,128)(2,1)S(1)}, bf16[128,512]{1,0:T(8,128)(2,1)S(1)}, u32[]{:S(2)}, u32[]{:S(2)}) collective-permute-start(bf16[128,512]{1,0:T(8,128)(2,1)S(1)} %slice.30), channel_id=1, source_target_pairs={{0,16},{2,18},{4,20},{6,22},{8,24},{10,26},{12,28},{14,30},{16,0},... | collective-permute-start | bytes 393224 | tf_op jit(solution)/shard_map/ppermute | solution.py:825
  13.5 0.2 collective-permute-start.2
  13.7 0.8 slice_bitcast_fusion.3
  14.6 0.2 shard_map.512.own
  14.9 0.9 collective-permute-done
  15.9 7.4 %collective-permute-done.1 = bf16[128,512]{1,0:T(8,128)(2,1)S(1)} collective-permute-done((bf16[128,512]{1,0:T(8,128)(2,1)S(1)}, bf16[128,512]{1,0:T(8,128)(2,1)S(1)}, u32[]{:S(2)}, u32[]{:S(2)}) %collective-permute-start.1) | collective-permute-done | bytes 131104 | tf_op jit(solution)/shard_map/ppermute | solution.py:825
  23.6 0.8 copy.61
  24.4 0.5 collective-permute-start.10
  24.9 1.5 collective-permute-start.11
  26.4 1.4 collective-permute-start.12
  27.8 2.0 %collective-permute-start.13 = (bf16[4,48,512]{2,1,0:T(8,128)(2,1)S(1)}, bf16[4,48,512]{2,1,0:T(8,128)(2,1)S(1)}, u32[]{:S(2)}, u32[]{:S(2)}) collective-permute-start(bf16[4,48,512]{2,1,0:T(8,128)(2,1)S(1)} %pad_maximum_fusion.2), channel_id=1, source_target_pairs={{0,8},{2,10},{4,12},{6,14},{8,0},{10,2},{12,4},{14,6},{16,24},{18,... | collective-permute-start | bytes 589832 | tf_op jit(solution)/shard_map/ppermute | solution.py:825
  29.8 1.1 collective-permute-start.14
  30.9 9.0 %shard_map.513 = (f32[172,512]{1,0:T(8,128)}, bf16[516,512]{1,0:T(8,128)(2,1)}, f32[172,512]{1,0:T(8,128)}, bf16[172,5120]{1,0:T(8,128)(2,1)}, bf16[172,5120]{1,0:T(8,128)(2,1)}) custom-call(s32[2]{0:T(128)} %pad_add_fusion.meta, f32[172,1024]{1,0:T(8,128)} %bitcast.69, s32[1,1024]{1,0:T(1,128)} %src.1, f32[1,1024]{1,0:T(1,128)} %bitcast.81, ...), custom_call_target="tpu_custom_call" | custom-call | flops 8999999488 | bytes 9000000 | tf_op jit(solution)/shard_map/pallas_call | solution.py:855
  39.9 1.5 collective-permute-start.15
  41.4 5.0 %shard_map.514 = (bf16[2,258,256]{2,1,0:T(8,128)(2,1)}, bf16[2,258,172]{2,1,0:T(8,128)(2,1)}, bf16[2,86,344]{2,1,0:T(8,128)(2,1)}, bf16[352,256]{1,0:T(8,128)(2,...) custom-call(s32[2]{0:T(128)} %pad_add_fusion.meta, ...), custom_call_target="tpu_custom_call" | custom-call | flops 6000000000 | bytes 6000000 | tf_op jit(solution)/shard_map/pallas_call | solution.py:864
  46.3 1.6 collective-permute-done.15.far_b_0__2_
  48.1 0.5 collective-permute-start.20
  48.7 0.4 collective-permute-start.7
  49.3 1.0 collective-permute-done.7.own_piece_1_
  50.3 0.2 collective-permute-start.16
  50.6 0.4 copy-done.47
  51.0 0.2 collective-permute-start.17
  51.2 0.3 collective-permute-start.18
  51.5 0.4 copy-done.45
  51.9 0.7 copy-done.46
  52.6 0.3 collective-permute-start.8
  53.0 0.6 add_multiply_fusion.idx
  53.6 0.8 collective-permute-done.8.z_pieces_1_
  54.6 0.7 copy-done.38
  55.2 57.3 %shard_map.515 = (f32[2,86,512]{2,1,0:T(8,128)}, f32[4,144,768]{2,1,0:T(8,128)}, f32[4,144,768]{2,1,0:T(8,128)}, f32[8,128]{1,0:T(8,128)}) custom-call(s32[2]{0:T(128)} %pad_add_fusion.meta, s32[5632]{0:T(1024)} %add_multiply_fusion.idx, s32[1]{0:T(128)S(6)} %copy.64.wcount, bf16[176,512]{1,0:T(8,128)(2,1)} %shard_map.511.own_piece_0_, ...), custom_call_target="tpu_custom_call" | custom-call | flops 40000000000 | bytes 40000000 | tf_op jit(solution)/shard_map/pallas_call | solution.py:926
  112.6 0.3 collective-permute-start.23
  113.0 3.5 %collective-permute-done.23.got = f32[4,144,768]{2,1,0:T(8,128)S(1)} collective-permute-done((f32[4,144,768]{2,1,0:T(8,128)}, f32[4,144,768]{2,1,0:T(8,128)S(1)}, u32[]{:S(2)}, u32[]{:S(2)}) %collective-permute-start.23) | collective-permute-done | bytes 1769504 | tf_op jit(solution)/shard_map/ppermute | solution.py:822
  116.5 1.5 copy-done.29
  118.0 0.7 shard_map.517
  118.7 0.6 collective-permute-start.24
  119.3 8.3 %collective-permute-done.24.got = bf16[2,160,768]{2,1,0:T(8,128)(2,1)S(1)} collective-permute-done((bf16[2,160,768]{2,1,0:T(8,128)(2,1)S(1)}, bf16[2,160,768]{2,1,0:T(8,128)(2,1)S(1)}, u32[]{:S(2)}, u32[]{:S(2)}) %collective-permute-start.24) | collective-permute-done | bytes 491552 | tf_op jit(solution)/shard_map/ppermute | solution.py:957
  127.6 0.6 shard_map.518
  128.3 1.6 collective-permute-start.25
  129.8 4.7 %collective-permute-done.25.got = bf16[160,768]{1,0:T(8,128)(2,1)S(1)} collective-permute-done((bf16[160,768]{1,0:T(8,128)(2,1)S(1)}, bf16[160,768]{1,0:T(8,128)(2,1)S(1)}, u32[]{:S(2)}, u32[]{:S(2)}) %collective-permute-start.25) | collective-permute-done | bytes 245792 | tf_op jit(solution)/shard_map/ppermute | solution.py:957
  134.6 4.1 %collective-permute-start.26 = (bf16[288,768]{1,0:T(8,128)(2,1)S(1)}, bf16[288,768]{1,0:T(8,128)(2,1)S(1)}, u32[]{:S(2)}, u32[]{:S(2)}) collective-permute-start(bf16[288,768]{1,0:T(8,128)(2,1)S(1)} %shard_map.519.one), channel_id=1, source_target_pairs={{0,8},{1,3},{2,10},{3,1},{4,12},{5,7},{6,14},{7,5},{8,0},{9,11},{1... | collective-permute-start | bytes 1327112 | tf_op jit(solution)/shard_map/ppermute | solution.py:957
  138.7 6.3 %collective-permute-done.26.two = bf16[288,768]{1,0:T(8,128)(2,1)S(1)} collective-permute-done((bf16[288,768]{1,0:T(8,128)(2,1)S(1)}, bf16[288,768]{1,0:T(8,128)(2,1)S(1)}, u32[]{:S(2)}, u32[]{:S(2)}) %collective-permute-start.26) | collective-permute-done | bytes 442400 | tf_op jit(solution)/shard_map/ppermute | solution.py:957
  145.2 2.0 %collective-permute-start.27 = (bf16[288,768]{1,0:T(8,128)(2,1)S(1)}, bf16[288,768]{1,0:T(8,128)(2,1)S(1)}, u32[]{:S(2)}, u32[]{:S(2)}) collective-permute-start(bf16[288,768]{1,0:T(8,128)(2,1)S(1)} %shard_map.520.one), channel_id=1, source_target_pairs={{0,16},{1,5},{2,18},{3,7},{4,20},{5,1},{6,22},{7,3},{8,24},{9,13},... | collective-permute-start | bytes 1327112 | tf_op jit(solution)/shard_map/ppermute | solution.py:957
  147.2 19.6 %collective-permute-done.27.two = bf16[288,768]{1,0:T(8,128)(2,1)S(1)} collective-permute-done((bf16[288,768]{1,0:T(8,128)(2,1)S(1)}, bf16[288,768]{1,0:T(8,128)(2,1)S(1)}, u32[]{:S(2)}, u32[]{:S(2)}) %collective-permute-start.27) | collective-permute-done | bytes 442400 | tf_op jit(solution)/shard_map/ppermute | solution.py:957
  166.9 1.6 collective-permute-start.28
  168.5 0.8 dynamic-slice_bitcast_fusion.2
  169.3 0.5 collective-permute-start.29
  169.8 5.5 %collective-permute-done.28.w1 = bf16[288,768]{1,0:T(8,128)(2,1)S(1)} collective-permute-done((bf16[288,768]{1,0:T(8,128)(2,1)S(1)}, bf16[288,768]{1,0:T(8,128)(2,1)S(1)}, u32[]{:S(2)}, u32[]{:S(2)}) %collective-permute-start.28) | collective-permute-done | bytes 442400 | tf_op jit(solution)/shard_map/ppermute | solution.py:957
  175.3 0.5 collective-permute-start.30
  175.8 1.0 dynamic-slice_bitcast_fusion.mem
  176.9 0.2 copy.63.src
  177.1 1.2 slice.29
  178.3 1.2 maximum_select_fusion.fresh
  179.6 2.4 %shard_map.516 = f32[86,1024]{1,0:T(8,128)} custom-call(f32[86,1024]{1,0:T(8,128)S(1)} %dynamic-slice_bitcast_fusion.mem, f32[86,1024]{1,0:T(8,128)S(1)} %maximum_select_fusion.fresh, s32[1024,1]{1,0:T(8,128)S(1)} %copy.63.src, s32[1]{0:T(128)S(6)} %copy.64.wcount), custom_call_target="tpu_custom_call" | custom-call | flops 3000000000 | bytes 3000000 | tf_op jit(solution)/shard_map/pallas_call | solution.py:949
  182.1 1.5 collective-permute-done.30.w3
  183.6 0.8 shard_map.522.own
  184.7 5.0 %shard_map.524 = (f32[258,688]{1,0:T(8,128)}, f32[258,688]{1,0:T(8,128)}, f32[258,688]{1,0:T(8,128)}, f32[172,258]{1,0:T(8,128)}, f32[172,258]{1,0:T(8,128)}, /*...) custom-call(s32[2]{0:T(128)S(1)} %pad_add_fusion.1.bits, ...), custom_call_target="tpu_custom_call" | custom-call | flops 4000000000 | bytes 4000000 | tf_op jit(solution)/shard_map/pallas_call | solution.py:995
  189.8 1.6 shard_map.523
  191.3 0.5 slice.28
  (132 shorter events, 1.6 us)
Async XLA Ops:
  0.7 52.3 %copy-start = (s32[1024,10]{0,1:T(8,128)S(1)}, s32[1024,10]{0,1:T(8,128)}, u32[]{:S(2)}) copy-start(s32[1024,10]{0,1:T(8,128)} %param.35) | copy-start | bytes 122884
  2.0 12.6 %copy-start.1 = (f32[2,86,172]{2,0,1:T(2,128)S(1)}, f32[2,86,172]{2,0,1:T(2,128)}, u32[]{:S(2)}) copy-start(f32[2,86,172]{2,0,1:T(2,128)} %param.55) | copy-start | bytes 355012
  2.0 12.6 %copy-start.4 = (f32[688,258]{0,1:T(8,128)S(1)}, f32[688,258]{0,1:T(8,128)}, u32[]{:S(2)}) copy-start(f32[688,258]{0,1:T(8,128)} %param.40) | copy-start | bytes 2130052
  2.0 12.6 %copy-start.8 = (f32[3,344,86]{1,2,0:T(8,128)S(1)}, f32[3,344,86]{1,2,0:T(8,128)}, u32[]{:S(2)}) copy-start(f32[3,344,86]{1,2,0:T(8,128)} %param.52) | copy-start | bytes 1065028
  2.0 12.6 %copy-start.11 = (f32[172,258]{1,0:T(8,128)S(1)}, f32[172,258]{1,0:T(8,128)}, u32[]{:S(2)}) copy-start(f32[172,258]{1,0:T(8,128)} %refs_3_.3) | copy-start | bytes 532516
  2.0 12.6 %copy-start.20 = (f32[172,86]{1,0:T(8,128)S(1)}, f32[172,86]{1,0:T(8,128)}, u32[]{:S(2)}) copy-start(f32[172,86]{1,0:T(8,128)} %refs_15_.1) | copy-start | bytes 177508
  2.0 12.6 %copy-start.23 = (f32[2,258]{1,0:T(2,128)S(1)}, f32[2,258]{1,0:T(2,128)}, u32[]{:S(2)}) copy-start(f32[2,258]{1,0:T(2,128)} %refs_6_.1) | copy-start | bytes 6196
  3.9 19.4 %collective-permute-start.5 = (bf16[176,512]{1,0:T(8,128)(2,1)}, bf16[176,512]{1,0:T(8,128)(2,1)S(1)}, u32[]{:S(2)}, u32[]{:S(2)}) collective-permute-start(bf16[176,512]{1,0:T(8,128)(2,1)} %shard_map.511.own_piece_0_), channel_id=1, source_target_pairs={{0,6},{2,4},{4,2},{6,0},{8,14},{10,12},{12,10},{14,8},{16,22},{18,... | collective-permute-start | bytes 540680 | tf_op jit(solution)/shard_map/ppermute | solution.py:825
  7.8 15.6 %collective-permute-start.4 = (bf16[176,512]{1,0:T(8,128)(2,1)}, bf16[176,512]{1,0:T(8,128)(2,1)S(1)}, u32[]{:S(2)}, u32[]{:S(2)}) collective-permute-start(bf16[176,512]{1,0:T(8,128)(2,1)} %shard_map.511.own_piece_0_), channel_id=1, source_target_pairs={{0,4},{2,6},{4,0},{6,2},{8,12},{10,14},{12,8},{14,10},{16,20},{18,... | collective-permute-start | bytes 540680 | tf_op jit(solution)/shard_map/ppermute | solution.py:825
  9.3 6.5 %collective-permute-start = (bf16[128,512]{1,0:T(8,128)(2,1)S(1)}, bf16[128,512]{1,0:T(8,128)(2,1)S(1)}, u32[]{:S(2)}, u32[]{:S(2)}) collective-permute-start(bf16[128,512]{1,0:T(8,128)(2,1)S(1)} %slice.30), channel_id=1, source_target_pairs={{0,8},{2,10},{4,12},{6,14},{8,0},{10,2},{12,4},{14,6},{16,24},{18,... | collective-permute-start | bytes 393224 | tf_op jit(solution)/shard_map/ppermute | solution.py:825
  10.9 12.4 %collective-permute-start.1 = (bf16[128,512]{1,0:T(8,128)(2,1)S(1)}, bf16[128,512]{1,0:T(8,128)(2,1)S(1)}, u32[]{:S(2)}, u32[]{:S(2)}) collective-permute-start(bf16[128,512]{1,0:T(8,128)(2,1)S(1)} %slice.30), channel_id=1, source_target_pairs={{0,16},{2,18},{4,20},{6,22},{8,24},{10,26},{12,28},{14,30},{16,0},... | collective-permute-start | bytes 393224 | tf_op jit(solution)/shard_map/ppermute | solution.py:825
  13.5 9.8 %collective-permute-start.2 = (bf16[128,512]{1,0:T(8,128)(2,1)S(1)}, bf16[128,512]{1,0:T(8,128)(2,1)S(1)}, u32[]{:S(2)}, u32[]{:S(2)}) collective-permute-start(bf16[128,512]{1,0:T(8,128)(2,1)S(1)} %slice.30), channel_id=1, source_target_pairs={{0,24},{2,26},{4,28},{6,30},{8,16},{10,18},{12,20},{14,22},{16,8},... | collective-permute-start | bytes 393224 | tf_op jit(solution)/shard_map/ppermute | solution.py:825
  14.6 9.0 %copy-start.2 = (f32[2,172]{1,0:T(2,128)S(1)}, f32[2,172]{1,0:T(2,128)}, u32[]{:S(2)}) copy-start(f32[2,172]{1,0:T(2,128)} %refs_3_.2) | copy-start | bytes 4132
  14.9 25.0 %copy-start.3 = (bf16[752,768]{1,0:T(8,128)(2,1)}, bf16[752,768]{1,0:T(8,128)(2,1)S(1)}, u32[]{:S(2)}) copy-start(bf16[752,768]{1,0:T(8,128)(2,1)S(1)} %shard_map.512.own) | copy-start | bytes 3465220
  15.8 7.6 %collective-permute-start.3 = (bf16[176,512]{1,0:T(8,128)(2,1)S(1)}, bf16[176,512]{1,0:T(8,128)(2,1)S(1)}, u32[]{:S(2)}, u32[]{:S(2)}) collective-permute-start(bf16[176,512]{1,0:T(8,128)(2,1)S(1)} %copy-done.35), channel_id=1, source_target_pairs={{0,2},{2,0},{4,6},{6,4},{8,10},{10,8},{12,14},{14,12},{16,18},{18,... | collective-permute-start | bytes 540680 | tf_op jit(solution)/shard_map/ppermute | solution.py:825
  23.3 28.2 %copy-start.30 = (bf16[3,128,512]{2,1,0:T(8,128)(2,1)}, bf16[3,128,512]{2,1,0:T(8,128)(2,1)S(1)}, u32[]{:S(2)}) copy-start(bf16[3,128,512]{2,1,0:T(8,128)(2,1)S(1)} %pad_maximum_fusion.1.z_pieces_0_) | copy-start | bytes 1179652
  23.4 25.7 %copy-start.32 = (bf16[176,512]{1,0:T(8,128)(2,1)}, bf16[176,512]{1,0:T(8,128)(2,1)S(1)}, u32[]{:S(2)}) copy-start(bf16[176,512]{1,0:T(8,128)(2,1)S(1)} %collective-permute-done.5.xy_pieces_0__2_) | copy-start | bytes 540676
  23.4 25.7 %copy-start.33 = (bf16[176,512]{1,0:T(8,128)(2,1)}, bf16[176,512]{1,0:T(8,128)(2,1)S(1)}, u32[]{:S(2)}) copy-start(bf16[176,512]{1,0:T(8,128)(2,1)S(1)} %collective-permute-done.4.xy_pieces_0__1_) | copy-start | bytes 540676
  23.4 25.7 %copy-start.34 = (bf16[176,512]{1,0:T(8,128)(2,1)}, bf16[176,512]{1,0:T(8,128)(2,1)S(1)}, u32[]{:S(2)}) copy-start(bf16[176,512]{1,0:T(8,128)(2,1)S(1)} %collective-permute-done.3.xy_pieces_0__0_) | copy-start | bytes 540676
  23.5 6.3 %collective-permute-start.6 = (bf16[752,768]{1,0:T(8,128)(2,1)S(1)}, bf16[752,768]{1,0:T(8,128)(2,1)}, u32[]{:S(2)}, u32[]{:S(2)}) collective-permute-start(bf16[752,768]{1,0:T(8,128)(2,1)S(1)} %shard_map.512.own), channel_id=1, source_target_pairs={{0,1},{1,0},{2,3},{3,2},{4,5},{5,4},{6,7},{7,6},{8,9},{9,8},{10,11... | collective-permute-start | bytes 3465224 | tf_op jit(solution)/shard_map/ppermute | solution.py:822
  24.4 23.6 %collective-permute-start.10 = (bf16[3,128,512]{2,1,0:T(8,128)(2,1)S(1)}, bf16[3,128,512]{2,1,0:T(8,128)(2,1)}, u32[]{:S(2)}, u32[]{:S(2)}) collective-permute-start(bf16[3,128,512]{2,1,0:T(8,128)(2,1)S(1)} %pad_maximum_fusion.1.z_pieces_0_), channel_id=1, source_target_pairs={{0,2},{2,0},{4,6},{6,4},{8,10},{10,8},{12,14},{14,12},{16,18},{18,... | collective-permute-start | bytes 1179656 | tf_op jit(solution)/shard_map/ppermute | solution.py:825
  24.9 23.1 %collective-permute-start.11 = (bf16[3,128,512]{2,1,0:T(8,128)(2,1)S(1)}, bf16[3,128,512]{2,1,0:T(8,128)(2,1)}, u32[]{:S(2)}, u32[]{:S(2)}) collective-permute-start(bf16[3,128,512]{2,1,0:T(8,128)(2,1)S(1)} %pad_maximum_fusion.1.z_pieces_0_), channel_id=1, source_target_pairs={{0,4},{2,6},{4,0},{6,2},{8,12},{10,14},{12,8},{14,10},{16,20},{18,... | collective-permute-start | bytes 1179656 | tf_op jit(solution)/shard_map/ppermute | solution.py:825
  26.4 21.6 %collective-permute-start.12 = (bf16[3,128,512]{2,1,0:T(8,128)(2,1)S(1)}, bf16[3,128,512]{2,1,0:T(8,128)(2,1)}, u32[]{:S(2)}, u32[]{:S(2)}) collective-permute-start(bf16[3,128,512]{2,1,0:T(8,128)(2,1)S(1)} %pad_maximum_fusion.1.z_pieces_0_), channel_id=1, source_target_pairs={{0,6},{2,4},{4,2},{6,0},{8,14},{10,12},{12,10},{14,8},{16,22},{18,... | collective-permute-start | bytes 1179656 | tf_op jit(solution)/shard_map/ppermute | solution.py:825
  27.8 12.0 %collective-permute-start.13 = (bf16[4,48,512]{2,1,0:T(8,128)(2,1)S(1)}, bf16[4,48,512]{2,1,0:T(8,128)(2,1)S(1)}, u32[]{:S(2)}, u32[]{:S(2)}) collective-permute-start(bf16[4,48,512]{2,1,0:T(8,128)(2,1)S(1)} %pad_maximum_fusion.2), channel_id=1, source_target_pairs={{0,8},{2,10},{4,12},{6,14},{8,0},{10,2},{12,4},{14,6},{16,24},{18,... | collective-permute-start | bytes 589832 | tf_op jit(solution)/shard_map/ppermute | solution.py:825
  29.8 16.5 %collective-permute-start.14 = (bf16[4,48,512]{2,1,0:T(8,128)(2,1)S(1)}, bf16[4,48,512]{2,1,0:T(8,128)(2,1)S(1)}, u32[]{:S(2)}, u32[]{:S(2)}) collective-permute-start(bf16[4,48,512]{2,1,0:T(8,128)(2,1)S(1)} %pad_maximum_fusion.2), channel_id=1, source_target_pairs={{0,16},{2,18},{4,20},{6,22},{8,24},{10,26},{12,28},{14,30},{16,0},... | collective-permute-start | bytes 589832 | tf_op jit(solution)/shard_map/ppermute | solution.py:825
  39.9 8.1 %copy-start.42 = (bf16[4,48,512]{2,1,0:T(8,128)(2,1)}, bf16[4,48,512]{2,1,0:T(8,128)(2,1)S(1)}, u32[]{:S(2)}) copy-start(bf16[4,48,512]{2,1,0:T(8,128)(2,1)S(1)} %collective-permute-done.13.far_b_0__0_) | copy-start | bytes 589828
  39.9 8.1 %collective-permute-start.15 = (bf16[4,48,512]{2,1,0:T(8,128)(2,1)S(1)}, bf16[4,48,512]{2,1,0:T(8,128)(2,1)S(1)}, u32[]{:S(2)}, u32[]{:S(2)}) collective-permute-start(bf16[4,48,512]{2,1,0:T(8,128)(2,1)S(1)} %pad_maximum_fusion.2), channel_id=1, source_target_pairs={{0,24},{2,26},{4,28},{6,30},{8,16},{10,18},{12,20},{14,22},{16,8},... | collective-permute-start | bytes 589832 | tf_op jit(solution)/shard_map/ppermute | solution.py:825
  41.4 11.5 %copy-start.37 = (s32[1024]{0:T(1024)S(1)}, s32[1024]{0:T(1024)}, u32[]{:S(2)}) copy-start(s32[1024]{0:T(1024)} %param.34) | copy-start | bytes 12292
  46.3 5.2 %copy-start.43 = (bf16[4,48,512]{2,1,0:T(8,128)(2,1)}, bf16[4,48,512]{2,1,0:T(8,128)(2,1)S(1)}, u32[]{:S(2)}) copy-start(bf16[4,48,512]{2,1,0:T(8,128)(2,1)S(1)} %collective-permute-done.14.far_b_0__1_) | copy-start | bytes 589828
  48.0 3.6 %copy-start.44 = (bf16[4,48,512]{2,1,0:T(8,128)(2,1)}, bf16[4,48,512]{2,1,0:T(8,128)(2,1)S(1)}, u32[]{:S(2)}) copy-start(bf16[4,48,512]{2,1,0:T(8,128)(2,1)S(1)} %collective-permute-done.15.far_b_0__2_) | copy-start | bytes 589828
  48.0 3.0 %collective-permute-start.19 = (bf16[4,48,512]{2,1,0:T(8,128)(2,1)S(1)}, bf16[4,48,512]{2,1,0:T(8,128)(2,1)}, u32[]{:S(2)}, u32[]{:S(2)}) collective-permute-start(bf16[4,48,512]{2,1,0:T(8,128)(2,1)S(1)} %collective-permute-done.13.far_b_0__0_), channel_id=1, source_target_pairs={{0,1},{1,0},{2,3},{3,2},{4,5},{5,4},{6,7},{7,6},{8,9},{9,8},{10,11... | collective-permute-start | bytes 589832 | tf_op jit(solution)/shard_map/ppermute | solution.py:822
  48.1 3.2 %collective-permute-start.20 = (bf16[4,48,512]{2,1,0:T(8,128)(2,1)S(1)}, bf16[4,48,512]{2,1,0:T(8,128)(2,1)S(1)}, u32[]{:S(2)}, u32[]{:S(2)}) collective-permute-start(bf16[4,48,512]{2,1,0:T(8,128)(2,1)S(1)} %collective-permute-done.14.far_b_0__1_), channel_id=1, source_target_pairs={{0,1},{1,0},{2,3},{3,2},{4,5},{5,4},{6,7},{7,6},{8,9},{9,8},{10,11... | collective-permute-start | bytes 589832 | tf_op jit(solution)/shard_map/ppermute | solution.py:822
  48.6 2.9 %collective-permute-start.21 = (bf16[4,48,512]{2,1,0:T(8,128)(2,1)S(1)}, bf16[4,48,512]{2,1,0:T(8,128)(2,1)S(1)}, u32[]{:S(2)}, u32[]{:S(2)}) collective-permute-start(bf16[4,48,512]{2,1,0:T(8,128)(2,1)S(1)} %collective-permute-done.15.far_b_0__2_), channel_id=1, source_target_pairs={{0,1},{1,0},{2,3},{3,2},{4,5},{5,4},{6,7},{7,6},{8,9},{9,8},{10,11... | collective-permute-start | bytes 589832 | tf_op jit(solution)/shard_map/ppermute | solution.py:822
  48.7 1.7 collective-permute-start.7
  49.2 5.3 %collective-permute-start.9 = (bf16[3,176,512]{2,1,0:T(8,128)(2,1)S(1)}, bf16[3,176,512]{2,1,0:T(8,128)(2,1)S(1)}, u32[]{:S(2)}, u32[]{:S(2)}) collective-permute-start(bf16[3,176,512]{2,1,0:T(8,128)(2,1)S(1)} %pad_maximum_fusion), channel_id=1, source_target_pairs={{0,1},{1,0},{2,3},{3,2},{4,5},{5,4},{6,7},{7,6},{8,9},{9,8},{10,11... | collective-permute-start | bytes 1622024 | tf_op jit(solution)/shard_map/ppermute | solution.py:822
  50.3 3.2 %collective-permute-start.16 = (bf16[3,128,512]{2,1,0:T(8,128)(2,1)}, bf16[3,128,512]{2,1,0:T(8,128)(2,1)S(1)}, u32[]{:S(2)}, u32[]{:S(2)}) collective-permute-start(bf16[3,128,512]{2,1,0:T(8,128)(2,1)} %collective-permute-done.10.far_a_0__0_), channel_id=1, source_target_pairs={{0,1},{1,0},{2,3},{3,2},{4,5},{5,4},{6,7},{7,6},{8,9},{9,8},{10,11... | collective-permute-start | bytes 1179656 | tf_op jit(solution)/shard_map/ppermute | solution.py:822
  51.0 2.6 %collective-permute-start.17 = (bf16[3,128,512]{2,1,0:T(8,128)(2,1)}, bf16[3,128,512]{2,1,0:T(8,128)(2,1)S(1)}, u32[]{:S(2)}, u32[]{:S(2)}) collective-permute-start(bf16[3,128,512]{2,1,0:T(8,128)(2,1)} %collective-permute-done.11.far_a_0__1_), channel_id=1, source_target_pairs={{0,1},{1,0},{2,3},{3,2},{4,5},{5,4},{6,7},{7,6},{8,9},{9,8},{10,11... | collective-permute-start | bytes 1179656 | tf_op jit(solution)/shard_map/ppermute | solution.py:822
  51.2 2.4 %collective-permute-start.18 = (bf16[3,128,512]{2,1,0:T(8,128)(2,1)}, bf16[3,128,512]{2,1,0:T(8,128)(2,1)S(1)}, u32[]{:S(2)}, u32[]{:S(2)}) collective-permute-start(bf16[3,128,512]{2,1,0:T(8,128)(2,1)} %collective-permute-done.12.far_a_0__2_), channel_id=1, source_target_pairs={{0,1},{1,0},{2,3},{3,2},{4,5},{5,4},{6,7},{7,6},{8,9},{9,8},{10,11... | collective-permute-start | bytes 1179656 | tf_op jit(solution)/shard_map/ppermute | solution.py:822
  52.6 1.9 collective-permute-start.8
  112.6 4.0 %collective-permute-start.23 = (f32[4,144,768]{2,1,0:T(8,128)}, f32[4,144,768]{2,1,0:T(8,128)S(1)}, u32[]{:S(2)}, u32[]{:S(2)}) collective-permute-start(f32[4,144,768]{2,1,0:T(8,128)} %get-tuple-element.136), channel_id=1, source_target_pairs={{0,1},{1,0},{2,3},{3,2},{4,5},{5,4},{6,7},{7,6},{8,9},{9,8},{10,11... | collective-permute-start | bytes 5308424 | tf_op jit(solution)/shard_map/ppermute | solution.py:822
  118.7 8.9 %collective-permute-start.24 = (bf16[2,160,768]{2,1,0:T(8,128)(2,1)S(1)}, bf16[2,160,768]{2,1,0:T(8,128)(2,1)S(1)}, u32[]{:S(2)}, u32[]{:S(2)}) collective-permute-start(bf16[2,160,768]{2,1,0:T(8,128)(2,1)S(1)} %get-tuple-element.138), channel_id=1, source_target_pairs={{0,2},{1,9},{2,0},{3,11},{4,6},{5,13},{6,4},{7,15},{8,10},{9,1},{1... | collective-permute-start | bytes 1474568 | tf_op jit(solution)/shard_map/ppermute | solution.py:957
  128.3 6.3 %collective-permute-start.25 = (bf16[160,768]{1,0:T(8,128)(2,1)S(1)}, bf16[160,768]{1,0:T(8,128)(2,1)S(1)}, u32[]{:S(2)}, u32[]{:S(2)}) collective-permute-start(bf16[160,768]{1,0:T(8,128)(2,1)S(1)} %get-tuple-element.140), channel_id=1, source_target_pairs={{0,4},{1,17},{2,6},{3,19},{4,0},{5,21},{6,2},{7,23},{8,12},{9,25},... | collective-permute-start | bytes 737288 | tf_op jit(solution)/shard_map/ppermute | solution.py:957
  134.6 10.4 %collective-permute-start.26 = (bf16[288,768]{1,0:T(8,128)(2,1)S(1)}, bf16[288,768]{1,0:T(8,128)(2,1)S(1)}, u32[]{:S(2)}, u32[]{:S(2)}) collective-permute-start(bf16[288,768]{1,0:T(8,128)(2,1)S(1)} %shard_map.519.one), channel_id=1, source_target_pairs={{0,8},{1,3},{2,10},{3,1},{4,12},{5,7},{6,14},{7,5},{8,0},{9,11},{1... | collective-permute-start | bytes 1327112 | tf_op jit(solution)/shard_map/ppermute | solution.py:957
  145.2 23.3 %copy-start.31 = (f32[2,86,512]{2,1,0:T(8,128)S(1)}, f32[2,86,512]{2,1,0:T(8,128)}, u32[]{:S(2)}) copy-start(f32[2,86,512]{2,1,0:T(8,128)} %get-tuple-element.134) | copy-start | bytes 1056772
  145.2 31.7 %copy-start.36 = (s32[1,1024]{1,0:T(1,128)S(1)}, s32[1,1024]{1,0:T(1,128)}, u32[]{:S(2)}) copy-start(s32[1,1024]{1,0:T(1,128)} %src.1) | copy-start | bytes 12292
  145.2 21.6 %collective-permute-start.27 = (bf16[288,768]{1,0:T(8,128)(2,1)S(1)}, bf16[288,768]{1,0:T(8,128)(2,1)S(1)}, u32[]{:S(2)}, u32[]{:S(2)}) collective-permute-start(bf16[288,768]{1,0:T(8,128)(2,1)S(1)} %shard_map.520.one), channel_id=1, source_target_pairs={{0,16},{1,5},{2,18},{3,7},{4,20},{5,1},{6,22},{7,3},{8,24},{9,13},... | collective-permute-start | bytes 1327112 | tf_op jit(solution)/shard_map/ppermute | solution.py:957
  166.9 8.4 %collective-permute-start.28 = (bf16[288,768]{1,0:T(8,128)(2,1)S(1)}, bf16[288,768]{1,0:T(8,128)(2,1)S(1)}, u32[]{:S(2)}, u32[]{:S(2)}) collective-permute-start(bf16[288,768]{1,0:T(8,128)(2,1)S(1)} %shard_map.521.w0), channel_id=1, source_target_pairs={{0,4},{1,17},{2,6},{3,19},{4,0},{5,21},{6,2},{7,23},{8,12},{9,25},... | collective-permute-start | bytes 1327112 | tf_op jit(solution)/shard_map/ppermute | solution.py:957
  169.3 9.0 %collective-permute-start.22 = (f32[86,512]{1,0:T(8,128)}, f32[86,512]{1,0:T(8,128)}, u32[]{:S(2)}, u32[]{:S(2)}) collective-permute-start(f32[86,512]{1,0:T(8,128)} %get-tuple-element.168), channel_id=1, source_target_pairs={{0,1},{1,0},{2,3},{3,2},{4,5},{5,4},{6,7},{7,6},{8,9},{9,8},{10,11... | collective-permute-start | bytes 528392 | tf_op jit(solution)/shard_map/ppermute | solution.py:822
  169.3 12.8 %collective-permute-start.29 = (bf16[288,768]{1,0:T(8,128)(2,1)S(1)}, bf16[288,768]{1,0:T(8,128)(2,1)S(1)}, u32[]{:S(2)}, u32[]{:S(2)}) collective-permute-start(bf16[288,768]{1,0:T(8,128)(2,1)S(1)} %shard_map.521.w0), channel_id=1, source_target_pairs={{0,2},{1,9},{2,0},{3,11},{4,6},{5,13},{6,4},{7,15},{8,10},{9,1},{1... | collective-permute-start | bytes 1327112 | tf_op jit(solution)/shard_map/ppermute | solution.py:957
  175.3 8.3 %collective-permute-start.30 = (bf16[288,768]{1,0:T(8,128)(2,1)S(1)}, bf16[288,768]{1,0:T(8,128)(2,1)S(1)}, u32[]{:S(2)}, u32[]{:S(2)}) collective-permute-start(bf16[288,768]{1,0:T(8,128)(2,1)S(1)} %collective-permute-done.28.w1), channel_id=1, source_target_pairs={{0,2},{1,9},{2,0},{3,11},{4,6},{5,13},{6,4},{7,15},{8,10},{9,1},{1... | collective-permute-start | bytes 1327112 | tf_op jit(solution)/shard_map/ppermute | solution.py:957
  179.5 5.0 %copy-start.13 = (f32[172,258]{1,0:T(8,128)S(1)}, f32[172,258]{1,0:T(8,128)}, u32[]{:S(2)}) copy-start(f32[172,258]{1,0:T(8,128)} %refs_4_.3) | copy-start | bytes 532516
  179.6 5.0 %copy-start.14 = (f32[172,258]{1,0:T(8,128)S(1)}, f32[172,258]{1,0:T(8,128)}, u32[]{:S(2)}) copy-start(f32[172,258]{1,0:T(8,128)} %refs_5_.3) | copy-start | bytes 532516
  179.6 5.0 %copy-start.19 = (f32[2,86,172]{2,0,1:T(2,128)S(1)}, f32[2,86,172]{2,0,1:T(2,128)}, u32[]{:S(2)}) copy-start(f32[2,86,172]{2,0,1:T(2,128)} %param.57) | copy-start | bytes 355012
  179.6 4.9 %copy-start.21 = (f32[172,86]{1,0:T(8,128)S(1)}, f32[172,86]{1,0:T(8,128)}, u32[]{:S(2)}) copy-start(f32[172,86]{1,0:T(8,128)} %refs_16_.1) | copy-start | bytes 177508
  179.6 4.9 %copy-start.22 = (f32[172,86]{1,0:T(8,128)S(1)}, f32[172,86]{1,0:T(8,128)}, u32[]{:S(2)}) copy-start(f32[172,86]{1,0:T(8,128)} %refs_17_.1) | copy-start | bytes 177508
  182.0 2.6 %copy-start.10 = (f32[3,344,86]{1,2,0:T(8,128)S(1)}, f32[3,344,86]{1,2,0:T(8,128)}, u32[]{:S(2)}) copy-start(f32[3,344,86]{1,2,0:T(8,128)} %param.54) | copy-start | bytes 1065028
  182.0 2.6 %copy-start.12 = (f32[172,258]{1,0:T(8,128)S(1)}, f32[172,258]{1,0:T(8,128)}, u32[]{:S(2)}) copy-start(f32[172,258]{1,0:T(8,128)} %refs_3_.3) | copy-start | bytes 532516
  184.4 5.3 %collective-permute-start.31 = (bf16[128,768]{1,0:T(8,128)(2,1)S(1)}, bf16[128,768]{1,0:T(8,128)(2,1)S(1)}, u32[]{:S(2)}, u32[]{:S(2)}) collective-permute-start(bf16[128,768]{1,0:T(8,128)(2,1)S(1)} %shard_map.522.own), channel_id=1, source_target_pairs={{0,1},{1,0},{2,3},{3,2},{4,5},{5,4},{6,7},{7,6},{8,9},{9,8},{10,11... | collective-permute-start | bytes 589832 | tf_op jit(solution)/shard_map/ppermute | solution.py:822
  184.6 5.1 %copy-start.15 = (f32[172,172]{1,0:T(8,128)S(1)}, f32[172,172]{1,0:T(8,128)}, u32[]{:S(2)}) copy-start(f32[172,172]{1,0:T(8,128)} %refs_0_.1) | copy-start | bytes 355012
  184.6 5.1 %copy-start.16 = (f32[172,172]{1,0:T(8,128)S(1)}, f32[172,172]{1,0:T(8,128)}, u32[]{:S(2)}) copy-start(f32[172,172]{1,0:T(8,128)} %refs_1_.1) | copy-start | bytes 355012
  184.7 5.1 %copy-start.17 = (f32[172,172]{1,0:T(8,128)S(1)}, f32[172,172]{1,0:T(8,128)}, u32[]{:S(2)}) copy-start(f32[172,172]{1,0:T(8,128)} %refs_2_.1) | copy-start | bytes 355012
  184.7 5.1 %copy-start.26 = (f32[2,172]{1,0:T(2,128)S(1)}, f32[2,172]{1,0:T(2,128)}, u32[]{:S(2)}) copy-start(f32[2,172]{1,0:T(2,128)} %refs_4_.2) | copy-start | bytes 4132
  184.7 5.1 %copy-start.27 = (f32[2,172]{1,0:T(2,128)S(1)}, f32[2,172]{1,0:T(2,128)}, u32[]{:S(2)}) copy-start(f32[2,172]{1,0:T(2,128)} %refs_5_.2) | copy-start | bytes 4132
  184.7 5.1 %copy-start.28 = (s32[2]{0:T(128)S(1)}, s32[2]{0:T(128)}, u32[]{:S(2)}) copy-start(s32[2]{0:T(128)} %pad_add_fusion.meta) | copy-start | bytes 28
  (16 other events, 26.1 us)

commit v2 on v1

--- a/solution.py
+++ b/solution.py
@@ -19,6 +19,7 @@
 PLANE = 4
 PAD = 88
 LO_BASE = 256
+COLS = 128
 SAFE_LOGIT = 40.0
 VMEM_LIMIT = 58 * 2**20
 VMEM_WHOLE = 62 * 2**20
@@ -37,6 +38,10 @@
 
 def tn(a, b):
     return lax.dot_general(a, b, (((0,), (0,)), ((), ())), preferred_element_type=F32)
+
+
+def sigmoid(x):
+    return 0.5 * jnp.tanh(0.5 * x) + 0.5
 
 
 def split3(x):
@@ -121,13 +126,16 @@
 
 def codes_kernel(meta, mem, src, delta, ndelta, tcol, edge, srct, msg, sin_d, code_n, sin_n):
     rows = mem.shape[1]
-    events = srct.shape[1]
+    events = srct.shape[2]
     nbrs = ndelta.shape[0]
     own = pl.ds(pl.multiple_of(meta[1] * events, events), events)
     pick = (lax.broadcasted_iota(jnp.int32, (rows, events), 0) == src[:, own]).astype(BF)
     parts = split3(mem[...])
     source = nn(parts[0], pick) + nn(parts[1], pick) + nn(parts[2], pick)
-    srct[...] = source
+    units = source.shape[0] // 2
+    fill = jnp.zeros((PAD - units, events), F32)
+    for h in range(2):
+        srct[h] = jnp.concatenate([source[h * units : (h + 1) * units], fill], 0)
     freq, phase = tcol[:, 0:1], tcol[:, 1:2]
     sin_v, cos_v = sin_cos(delta[:, own] * freq + phase)
     sin_d[...] = sin_v
@@ -168,23 +176,36 @@
     units = width // 2
     gates = 3 * units
 
+    def rows_padded(x):
+        zero = jnp.zeros((PAD - units, x.shape[1]), F32)
+        parts = []
+        for k in range(x.shape[0] // units):
+            parts += [x[k * units : (k + 1) * units], zero]
+        return jnp.concatenate(parts, 0)
+
     def put(h, w):
         mw = w[0:gates, 0 : 4 * width].astype(F32)
+        o_mc[h] = mw[:, 2 * width : 3 * width].astype(BF)
+        mw = rows_padded(mw)
         o_md[h] = jnp.concatenate(
-            [mw[:, width : 2 * width], jnp.zeros((gates, 256 - width), F32)], 1
+            [mw[:, width : 2 * width], jnp.zeros((3 * PAD, 256 - width), F32)], 1
         ).astype(BF)
-        o_mc[h] = mw[:, 2 * width : 3 * width].astype(BF)
         rest = jnp.concatenate([mw[:, :width], mw[:, 2 * width :]], 1).astype(BF)
         small = w[WP_B : WP_B + 16, 0:gates].astype(F32)
         bias = (small[0:2] + small[2:4]) + small[4:6]
         bias = jnp.concatenate([bias, jnp.zeros((6, gates), F32)], 0).T
+        bias = rows_padded(bias)
+        state = rows_padded(w[WP_SD : WP_SD + gates, 0:width].astype(F32)).astype(BF)
         o_gin[h] = nn(rest, msg[...]) + bias[:, 0:1]
-        o_gst[h] = nn(w[WP_SD : WP_SD + gates, 0:width], msg[0:width]) + bias[:, 1:2]
-        o_q[h] = w[WP_QK : WP_QK + units, 0 : 2 * width]
-        zero = jnp.zeros((PAD - units, 2 * width), F32)
+        o_gst[h] = nn(state, msg[0:width]) + bias[:, 1:2]
+        query = rows_padded(w[WP_QK : WP_QK + units, 0 : 2 * width].astype(F32))
+        zero = jnp.zeros((PAD, PAD - units), F32)
+        o_q[h] = jnp.concatenate(
+            [query[:, :units], zero, query[:, units:width], zero, query[:, width:]], 1
+        ).astype(BF)
         key = w[WP_QK : WP_QK + units, 2 * width : 4 * width].astype(F32)
         value = w[WP_VF : WP_VF + units, 0 : 2 * width].astype(F32)
-        pair = jnp.concatenate([key, zero, value, zero], 0)
+        pair = rows_padded(jnp.concatenate([key, value], 0))
         wide = jnp.concatenate([pair[:, :width], jnp.zeros((2 * PAD, 256 - width), F32)], 1)
         rows = pl.ds(pl.multiple_of(h * 2 * PAD, 2 * PAD), 2 * PAD)
         o_kvm[rows] = wide.astype(BF)
@@ -192,11 +213,26 @@
         o_kvc[rows] = code.astype(BF)
         o_kvct[h] = code.T.astype(BF)
         for i in range(2):
-            dense = w[WP_VF : WP_VF + units, (2 + i) * width : (3 + i) * width]
-            o_f[i, h] = dense
-            o_ft[i, h] = dense.astype(F32).T.astype(BF)
-        o_d[h] = w[WP_SD : WP_SD + width, 256 : 256 + units]
-        o_dt[h] = w[WP_SD : WP_SD + units, 384 : 384 + width]
+            dense = w[WP_VF : WP_VF + units, (2 + i) * width : (3 + i) * width].astype(F32)
+            dense = rows_padded(dense)
+            o_f[i, h] = dense.astype(BF)
+            o_ft[i, h] = dense.T.astype(BF)
+
+    def second(one, two):
+        o_d[...] = jnp.concatenate(
+            [w[WP_SD : WP_SD + width, 256 : 256 + units].astype(F32) for w in (one, two)], 1
+        ).astype(BF)
+        o_dt[...] = jnp.concatenate(
+            [w[WP_SD : WP_SD + units, 384 : 384 + width].astype(F32) for w in (one, two)], 0
+        ).astype(BF)
+
+    @pl.when(meta[1] == 0)
+    def _():
+        second(own, other)
+
+    @pl.when(meta[1] == 1)
+    def _():
+        second(other, own)
 
     put(meta[1], own)
     put(1 - meta[1], other)
@@ -205,14 +241,17 @@
 
 def step_kernel(
     planes, use_table,
-    meta, idx, wcount, own_piece, z_pieces, xy_pieces, far_a, far_b, code_any, sin_any, kvc_any,
-    srct, msg, sin_d, delta_all, ndelta_all, tcol,
-    w_md, w_mc, w_q, w_kvm, w_kvct, w_f, w_ft, w_d, w_dt, w_tt, gin0, gst, gathered_in,
+    meta, idx, wcount, own_piece, z_pieces, xy_pieces, far_a, far_b, late_in,
+    delta_all, ndelta_all, tcol, w_tt, gathered_in,
     o_fresh, o_own, o_other, o_live,
-    sems, mem_all, code_n, sin_n, w_kvc, coarse, fine, near, qin, emb, keyt, count, stat, norm,
-    scores, probs, fresh_s, att_s, gates, acc_m, tgrad,
+    sems, mem_all, late, coarse, fine, near, qin, emb, keyt, count, stat, norm,
+    scores, probs, fresh_s, gates, acc_m, tgrad,
 ):
-    width, events = srct.shape
+    (
+        srct, msg, sin_d, w_md, w_mc, w_q, w_kvm, w_kvct, w_f, w_ft, w_d, w_dt, gin0, gst,
+        code_n, w_kvc, sin_n,
+    ) = late
+    width, events = sin_d.shape
     units = width // 2
     nbrs = ndelta_all.shape[0]
     groups, full, wide_cols = mem_all.shape
@@ -235,24 +274,39 @@
         start(src, mem_all.at[lax.div(row, 2), pl.ds(first, last - first), lanes])
 
     cut = z_pieces[0].shape[1]
-    for k in range(2):
-        half = head ^ k
-        bring(own_piece[k], row_pos, half, 0, full)
-        for d in range(1, planes):
-            bring(z_pieces[k].at[d - 1], row_pos ^ (d * PLANE), half, 0, cut)
-        for d in range(1, PLANE):
-            bring(xy_pieces[0][d - 1] if k == 0 else xy_pieces[1].at[d - 1], row_pos ^ d, half, 0, full)
-            for e in range(1, planes):
-                bring(far_a[k][d - 1].at[e - 1], row_pos ^ (e * PLANE + d), half, 0, cut)
-        for e in range(1, planes):
-            for d in range(PLANE):
-                bring(far_b[k][e - 1].at[d], row_pos ^ (e * PLANE + d), half, cut, full)
+    first_copy = []
+    for r in range(groups):
+        first_copy.append(len(copies))
+        for e, d in (divmod(2 * r, PLANE), divmod(2 * r + 1, PLANE)):
+            row = row_pos ^ (e * PLANE + d)
+            for k in range(2):
+                half = head ^ k
+                if e == 0 and d == 0:
+                    bring(own_piece[k], row, half, 0, full)
+                elif e == 0:
+                    bring(xy_pieces[0][d - 1] if k == 0 else xy_pieces[1].at[d - 1], row, half, 0, full)
+                else:
+                    bring(z_pieces[k].at[e - 1] if d == 0 else far_a[k][d - 1].at[e - 1], row, half, 0, cut)
+                    bring(far_b[k][e - 1].at[d], row, half, cut, full)
     n_memory = len(copies)
-    start(code_any, code_n)
-    start(kvc_any, w_kvc)
-    start(sin_any, sin_n)
-    for copy in copies[:n_memory]:
-        copy.wait()
+    first_copy.append(n_memory)
+    for src, dst in zip(late_in, late):
+        start(src, dst)
+    n_late = len(copies)
+
+    def group_here(r):
+        for copy in copies[first_copy[r] : first_copy[r + 1]]:
+            copy.wait()
+        return lax.div(row_pos, 2) ^ r
+
+    def each_group(work):
+        if groups <= 8:
+            for r in range(groups):
+                work(group_here(r))
+        else:
+            for r in range(groups):
+                group_here(r)
+            lax.fori_loop(0, groups, lambda g, s: (work(g), s)[1], 0)
 
     count[...] = jnp.zeros_like(count)
     norm[...] = jnp.zeros_like(norm)
@@ -270,11 +324,12 @@
             keyt[g, 0:width] = keys
         keys = keys.astype(F32)
         norm[0:1] = jnp.maximum(norm[0:1], jnp.sum(keys * keys, 0, keepdims=True))
-        id_hi = wide[width : width + 1].astype(jnp.int32)
-        id_lo = wide[width + 1 : width + 2].astype(jnp.int32)
-        hot_hi = (lax.broadcasted_iota(jnp.int32, (hi_rows, wide_cols), 0) == id_hi).astype(BF)
-        hot_lo = (lax.broadcasted_iota(jnp.int32, (LO_BASE, wide_cols), 0) == id_lo).astype(BF)
-        count[...] += nt(hot_hi, hot_lo)
+        ids = (wide[width : width + 1] * LO_BASE + wide[width + 1 : width + 2]).astype(jnp.int32)
+        hot = []
+        for size, part in ((hi_rows, ids // COLS), (COLS, ids % COLS)):
+            place = lax.broadcasted_iota(jnp.int32, (size, wide_cols), 0).astype(F32)
+            hot.append(jnp.where(place == part.astype(F32), 1.0, 0.0).astype(BF))
+        count[...] += nt(hot[0], hot[1])
         here = wide[width + 2 : width + 3] * LO_BASE + wide[width + 3 : width + 4]
         for k in range(0, per_group, 2):
             stat[0:1, :] += here[:, k * events : k * events + 128]
@@ -287,7 +342,7 @@
             )
 
     def gather_rows(table, gathered):
-        lax.fori_loop(0, groups, lambda g, s: (per_group_rows(g, table), s)[1], 0)
+        each_group(lambda g: per_group_rows(g, table))
         unroll = 32
 
         def body(i, carry):
@@ -311,14 +366,12 @@
             pltpu.VMEM((2 * lookups, 128), F32),
         )
     else:
-        lax.fori_loop(0, groups, lambda g, s: (per_group_rows(g, None), s)[1], 0)
+        each_group(lambda g: per_group_rows(g, None))
         near = gathered_in
 
     def count_lines(g, keys):
-        at = g * (wide_cols // LO_BASE)
-        line = jnp.concatenate(
-            [count[pl.ds(at + k, 1), :] for k in range(wide_cols // LO_BASE)], 1
-        )
+        at = g * (wide_cols // COLS)
+        line = jnp.concatenate([count[pl.ds(at + k, 1), :] for k in range(wide_cols // COLS)], 1)
         line = jnp.where(line > 0.5, jnp.log(jnp.maximum(line, 1.0)), -1e30)
         parts = split3(line)
         place = lax.broadcasted_iota(jnp.int32, (16, wide_cols), 0)
@@ -346,28 +399,28 @@
     live_rows = stat[0:1, 0:1]
 
     def rest(kvt, pair):
+        for copy in copies[n_memory : n_late - 3]:
+            copy.wait()
         dest = near[pl.ds(nbrs * events, events), :]
         dest_t = dest.astype(F32).T[:width]
         dest_key = nn(target_t, dest_t.astype(BF)).astype(BF)
         for h in range(2):
             gate_in = gin0[h] + nt(w_md[h], dest)
             gate_state = gst[h]
-            reset = jax.nn.sigmoid(gate_in[:units] + gate_state[:units])
-            update = jax.nn.sigmoid(
-                gate_in[units : 2 * units] + gate_state[units : 2 * units]
-            )
-            state_c = gate_state[2 * units :]
-            candidate = jnp.tanh(gate_in[2 * units :] + reset * state_c)
+            reset = sigmoid(gate_in[:PAD] + gate_state[:PAD])
+            update = sigmoid(gate_in[PAD : 2 * PAD] + gate_state[PAD : 2 * PAD])
+            state_c = gate_state[2 * PAD :]
+            candidate = jnp.tanh(gate_in[2 * PAD :] + reset * state_c)
             for k, v in enumerate((reset, update, candidate, state_c)):
                 gates[h, k] = v
-            fresh = (1.0 - update) * candidate + update * srct[h * units : (h + 1) * units]
+            fresh = (1.0 - update) * candidate + update * srct[h]
             o_fresh[h] = fresh
-            qin[h * units : (h + 1) * units] = fresh
+            qin[h * PAD : (h + 1) * PAD] = fresh
         zero_sin, zero_cos = sin_cos(tcol[...])
-        qin[width : 2 * width] = jnp.broadcast_to(zero_cos[:, 1:2], (width, events))
+        qin[2 * PAD :] = jnp.broadcast_to(zero_cos[:, 1:2], (width, events))
         query_in = qin[...].astype(BF)
-        copies[n_memory].wait()
-        copies[n_memory + 1].wait()
+        copies[n_late - 3].wait()
+        copies[n_late - 2].wait()
 
         def project(j, carry):
             cols = pl.ds(pl.multiple_of(j * events, events), events)
@@ -379,31 +432,28 @@
         for h in range(2):
             key_at, value_at = h * 2 * PAD, h * 2 * PAD + PAD
             queries = nn(w_q[h], query_in)
-            fresh_s[h, :units] = queries
+            fresh_s[h] = queries
             for j in range(nbrs):
                 cols = pl.ds(j * events, events)
                 scores[j : j + 1] = (
-                    jnp.sum(queries * kvt[key_at : key_at + units, cols], 0, keepdims=True) * scale
+                    jnp.sum(queries * kvt[key_at : key_at + PAD, cols], 0, keepdims=True) * scale
                 )
             score = scores[0:nbrs]
             grown = jnp.exp(score - jnp.max(score, 0, keepdims=True))
             prob = grown / jnp.sum(grown, 0, keepdims=True)
             probs[h, 0:nbrs] = prob
-            total = jnp.zeros((units, events), F32)
+            total = jnp.zeros((PAD, events), F32)
             for j in range(nbrs):
                 cols = pl.ds(j * events, events)
-                total = total + prob[j : j + 1] * kvt[value_at : value_at + units, cols]
-            att_s[h, :units] = total
+                total = total + prob[j : j + 1] * kvt[value_at : value_at + PAD, cols]
             attended_low.append(total.astype(BF))
-        fresh_lows = [qin[h * units : (h + 1) * units].astype(BF) for h in range(2)]
+        fresh_lows = [qin[h * PAD : (h + 1) * PAD].astype(BF) for h in range(2)]
         hidden = (nn(w_ft[0, 0], attended_low[0]) + nn(w_ft[0, 1], attended_low[1])) + (
             nn(w_ft[1, 0], fresh_lows[0]) + nn(w_ft[1, 1], fresh_lows[1])
         )
-        sigmoid_h = jax.nn.sigmoid(hidden)
+        sigmoid_h = sigmoid(hidden)
         mixed_low = (hidden * sigmoid_h).astype(BF)
-        emb_halves = [nn(w_dt[h], mixed_low) for h in range(2)]
-        emb[0:units] = emb_halves[0]
-        emb[units:width] = emb_halves[1]
+        emb[...] = nn(w_dt[...], mixed_low)
         emb_low = emb[...].astype(BF)
         ones_line = (lax.broadcasted_iota(jnp.int32, (full - width, events), 0) < 3).astype(F32)
         emb_aug = jnp.concatenate([LOGIT_SCALE * emb_low.astype(F32), ones_line], 0)
@@ -484,14 +534,14 @@
         def slot(h):
             return h ^ head
 
-        emb_grad_low = [emb_grad[h * units : (h + 1) * units].astype(BF) for h in range(2)]
-        mixed_grad = nn(w_d[0], emb_grad_low[0]) + nn(w_d[1], emb_grad_low[1])
+        emb_grad_low = emb_grad.astype(BF)
+        mixed_grad = nn(w_d[...], emb_grad_low)
+        second = nt(mixed_low, emb_grad_low)
         hidden_grad = (mixed_grad * sigmoid_h * (1.0 + hidden * (1.0 - sigmoid_h))).astype(BF)
         for h in range(2):
-            second = nt(mixed_low, emb_grad_low[h])
             place = slot(h)
             for i, v in enumerate((attended_low[h], fresh_lows[h])):
-                fine[place, units:width, (2 + i) * width : (3 + i) * width] = nt(v, hidden_grad)
+                fine[place, units:width, (2 + i) * width : (3 + i) * width] = nt(v, hidden_grad)[:units]
             for k in range(2):
                 fine[place, ROW_T : ROW_T + quarter, k * width : (k + 1) * width] = target_grad[
                     h * units + k * quarter : h * units + (k + 1) * quarter
@@ -499,10 +549,10 @@
             for k in range(4):
                 at = 2 * width + k * units
                 fine[place, ROW_T : ROW_T + quarter, at : at + units] = second[
-                    k * quarter : (k + 1) * quarter
+                    k * quarter : (k + 1) * quarter, h * units : (h + 1) * units
                 ]
 
-        copies[n_memory + 2].wait()
+        copies[n_late - 1].wait()
         tgrad[...] = jnp.zeros_like(tgrad)
         query_lows = []
         prob_terms = []
@@ -514,25 +564,23 @@
             for j in range(nbrs):
                 cols = pl.ds(j * events, events)
                 scores[j : j + 1] = jnp.sum(
-                    att_grad * kvt[value_at : value_at + units, cols], 0, keepdims=True
+                    att_grad * kvt[value_at : value_at + PAD, cols], 0, keepdims=True
                 )
             prob_grad = scores[0:nbrs]
             prob_terms.append(prob * (prob_grad - jnp.sum(prob * prob_grad, 0, keepdims=True)))
             att_grads.append(att_grad)
-            total = jnp.zeros((units, events), F32)
+            total = jnp.zeros((PAD, events), F32)
             key_at = h * 2 * PAD
             for j in range(nbrs):
                 cols = pl.ds(j * events, events)
-                total = total + prob_terms[h][j : j + 1] * kvt[key_at : key_at + units, cols]
+                total = total + prob_terms[h][j : j + 1] * kvt[key_at : key_at + PAD, cols]
             query_lows.append((total * scale).astype(BF))
-        fill = jnp.zeros((PAD - units, events), F32)
         for j in range(nbrs):
             cols = pl.ds(j * events, events)
             pieces = []
             for h in range(2):
                 pieces += [
-                    (prob_terms[h][j : j + 1] * scale) * fresh_s[h, :units], fill,
-                    probs[h, j : j + 1] * att_grads[h], fill,
+                    (prob_terms[h][j : j + 1] * scale) * fresh_s[h], probs[h, j : j + 1] * att_grads[h],
                 ]
             pair_j = jnp.concatenate(pieces, 0).astype(BF)
             pair[:, cols] = pair_j
@@ -546,7 +594,9 @@
             place = slot(h)
             base = h * 2 * PAD
             query_grad = nt(query_lows[h], query_in)
-            fine[place, 0:units, 0 : 2 * width] = query_grad
+            fine[place, 0:units, 0:units] = query_grad[:units, 0:units]
+            fine[place, 0:units, units:width] = query_grad[:units, PAD : PAD + units]
+            fine[place, 0:units, width : 2 * width] = query_grad[:units, 2 * PAD :]
             for k, (row, lane) in enumerate(((0, 2 * width), (units, 0))):
                 at = base + k * PAD
                 fine[place, row : row + units, lane : lane + width] = near_grad[
@@ -556,7 +606,7 @@
                     at : at + units
                 ]
         query_in_grad = tn(w_q[0], query_lows[0]) + tn(w_q[1], query_lows[1])
-        zero_term = zero_sin[:, 1:2] * query_in_grad[width:]
+        zero_term = zero_sin[:, 1:2] * query_in_grad[2 * PAD :]
         tgrad[1, :width] -= zero_term
 
         def send_fine(k):
@@ -571,13 +621,15 @@
         for h in range(2):
             place = slot(h)
             reset, update, candidate, state_c = (gates[h, k] for k in range(4))
-            fresh_grad = nn(w_f[1, h], hidden_grad) + query_in_grad[h * units : (h + 1) * units]
-            own_state = srct[h * units : (h + 1) * units]
+            fresh_grad = nn(w_f[1, h], hidden_grad) + query_in_grad[h * PAD : (h + 1) * PAD]
+            own_state = srct[h]
             candidate_pre = fresh_grad * (1.0 - update) * (1.0 - candidate * candidate)
             update_pre = fresh_grad * (own_state - candidate) * update * (1.0 - update)
             reset_pre = candidate_pre * state_c * reset * (1.0 - reset)
-            in_grad = jnp.concatenate([reset_pre, update_pre, candidate_pre], 0).astype(BF)
-            state_grad = jnp.concatenate([reset_pre, update_pre, candidate_pre * reset], 0).astype(BF)
+            last_pre = candidate_pre * reset
+            shared = [reset_pre[:units], update_pre[:units]]
+            in_grad = jnp.concatenate(shared + [candidate_pre[:units]], 0).astype(BF)
+            state_grad = jnp.concatenate(shared + [last_pre[:units]], 0).astype(BF)
             gate_rows = 3 * units
             coarse[place, 0:gate_rows, width : 2 * width] = nn(in_grad, dest)[:, :width]
             rest_grad = nt(in_grad, msg[...])
@@ -610,7 +662,7 @@
         for k in range(4):
             for place, out in ((1, o_other), (0, o_own)):
                 start(coarse.at[place, pl.ds(k * COARSE, COARSE)], out.at[k, pl.ds(0, COARSE)])
-        for copy in copies[n_memory + 3 :]:
+        for copy in copies[n_late:]:
             copy.wait()
 
     pl.run_scoped(
@@ -668,12 +720,41 @@
     to_half_wire(o_send, keep[q] + from_half_wire(got[q]))
 
 
-def third_sum_kernel(keep, got, o_send):
-    to_wire(o_send, keep[...] + from_half_wire(got[...]))
-
-
-def wire_sum_kernel(one, two, o_send):
-    to_wire(o_send, from_wire(one[...]) + from_wire(two[...]))
+def third_sum_kernel(bits, keep, got, o_keep, o_send):
+    half = ROWS // 2
+    total = keep[...] + from_half_wire(got[...])
+    for b in range(2):
+
+        @pl.when(bits[2] == b)
+        def _(b=b):
+            o_keep[...] = total[b * half : (b + 1) * half]
+            eighth_wire(o_send, total[(1 - b) * half : (2 - b) * half])
+
+
+def eighth_wire(out, value):
+    half = ROWS // 2
+    high = value.astype(BF).astype(F32)
+    out[...] = jnp.concatenate([high, value - high], 0).astype(BF)
+
+
+def fourth_sum_kernel(keep, got, o_send):
+    half = ROWS // 2
+    wide = got[...].astype(F32)
+    eighth_wire(o_send, keep[...] + (wide[0:half] + wide[half:]))
+
+
+def eighth_sum_kernel(one, two, o_send):
+    half = ROWS // 2
+    a, b = one[...].astype(F32), two[...].astype(F32)
+    eighth_wire(o_send, (a[0:half] + a[half:]) + (b[0:half] + b[half:]))
+
+
+def join_kernel(bits, one, two, o_send):
+    half = ROWS // 2
+    a, b = one[...].astype(F32), two[...].astype(F32)
+    first = jnp.where(bits[2] == 0, a, b)
+    second = jnp.where(bits[2] == 0, b, a)
+    o_send[...] = jnp.concatenate([first[:half], second[:half], first[half:], second[half:]], 0).astype(BF)
 
 
 def quarter_of(bits, k):
@@ -762,7 +843,7 @@
 def memory_kernel(mem, fresh, src, wcount, out):
     units, rows = mem.shape
     pick = (lax.broadcasted_iota(jnp.int32, (rows, rows), 1) == src[...]).astype(BF)
-    parts = split3(fresh[...])
+    parts = split3(fresh[0:units])
     moved = nn(parts[0], pick) + nn(parts[1], pick) + nn(parts[2], pick)
     alive = (lax.broadcasted_iota(jnp.int32, (16, rows), 1) < wcount[0]).astype(BF)
     hit = nn(alive, pick)[0:1] > 0.5
@@ -849,19 +930,19 @@
         (delta_t[None], nbr_delta.T, edge_feat.T, time_param.T, packed_o, plane_b)
     )
     code_shapes = (
-        shape(width, events), bf(3 * width, events), shape(width, events),
+        shape(2, PAD, events), bf(3 * width, events), shape(width, events),
         bf(width, nbrs * events), bf(width, nbrs * events),
     )
     srct, msg, sin_d, code_n, sin_n = vmem_call(codes_kernel, code_shapes, "svvvvvv", micros=9)(
         meta, mem_t, sources, delta, ndelta, tcol, edge
     )
     w_shapes = (
-        bf(2, 3 * units, 256), bf(2, 3 * units, width), bf(2, units, 2 * width),
+        bf(2, 3 * PAD, 256), bf(2, 3 * units, width), bf(2, PAD, 2 * PAD + width),
         bf(4 * PAD, 256), bf(4 * PAD, width), bf(2, width, 2 * PAD),
-        bf(2, 2, units, width), bf(2, 2, width, units), bf(2, width, units), bf(2, units, width),
-        bf(width, width), shape(2, 3 * units, events), shape(2, 3 * units, events),
-    )
-    w_md, w_mc, w_q, w_kvm, w_kvc, *w_more = vmem_call(weights_kernel, w_shapes, "svvvv", micros=6)(
+        bf(2, 2, PAD, width), bf(2, 2, width, PAD), bf(width, width), bf(width, width),
+        bf(width, width), shape(2, 3 * PAD, events), shape(2, 3 * PAD, events),
+    )
+    w_md, w_mc, w_q, w_kvm, w_kvc, w_kvct, w_f, w_ft, w_d, w_dt, w_tt, gin0, gst = vmem_call(weights_kernel, w_shapes, "svvvv", micros=6)(
         meta, packed, packed_o, target_weight, msg
     )
 
@@ -892,41 +973,41 @@
         half = (index % rows) // events
         gathered = table[((index // rows) ^ row) * 2 + (half ^ head), index % events]
         gathered = jnp.pad(gathered, ((0, 0), (0, 256 - full)))
-    hi_rows = total_rows // LO_BASE
+    hi_rows = total_rows // COLS
     wide_cols = 4 * events
     groups = total_rows // wide_cols
-    n_copies = 2 * (1 + (planes - 1) + (PLANE - 1) * planes + (planes - 1) * PLANE) + 3 + 16
+    late = (
+        srct, msg, sin_d, w_md, w_mc, w_q, w_kvm, w_kvct, w_f, w_ft, w_d, w_dt, gin0, gst, code_n, w_kvc, sin_n,
+    )
+    n_copies = 2 * (1 + (planes - 1) + (PLANE - 1) * planes + (planes - 1) * PLANE) + len(late) + 16
     scratch = [
         pltpu.SemaphoreType.DMA((n_copies,)),
         pltpu.VMEM((groups, full, wide_cols), BF),
-        pltpu.VMEM((width, nbrs * events), BF),
-        pltpu.VMEM((width, nbrs * events), BF),
-        pltpu.VMEM((4 * PAD, width), BF),
+        tuple(pltpu.VMEM(x.shape, x.dtype) for x in late),
         pltpu.VMEM((2, 4 * COARSE, LANES), F32),
         pltpu.VMEM((2, 4 * FINE, LANES), F32),
         pltpu.VMEM((lookups if use_table else 16, 256), BF),
-        pltpu.VMEM((2 * width, events), F32),
+        pltpu.VMEM((2 * PAD + width, events), F32),
         pltpu.VMEM((width, events), F32),
         pltpu.VMEM((groups if use_table else 1, full, wide_cols), BF),
-        pltpu.VMEM((hi_rows, LO_BASE), F32),
+        pltpu.VMEM((hi_rows, COLS), F32),
         pltpu.VMEM((8, 128), F32),
         pltpu.VMEM((8, wide_cols), F32),
         pltpu.VMEM((16, events), F32),
         pltpu.VMEM((3, 16, events), F32),
         pltpu.VMEM((2, PAD, events), F32),
-        pltpu.VMEM((2, PAD, events), F32),
-        pltpu.VMEM((2, 4, units, events), F32),
+        pltpu.VMEM((2, 4, PAD, events), F32),
         pltpu.VMEM((full, events), F32),
         pltpu.VMEM((2, PAD * 2, events), F32),
     ]
     spaces = [
         "s", "s", "s", ["a", "a"], ["a", "a"], [["a"] * (PLANE - 1), "a"],
-        [["a"] * (PLANE - 1)] * 2, [["a"] * (planes - 1)] * 2, "a", "a", "a",
-    ] + ["v"] * 19
+        [["a"] * (PLANE - 1)] * 2, [["a"] * (planes - 1)] * 2, ["a"] * len(late),
+    ] + ["v"] * 5
     fresh, pack_own, pack_other, live = vmem_call(
         functools.partial(step_kernel, planes, use_table),
         (
-            shape(2, units, events), shape(4, ROWS, LANES), shape(4, ROWS, LANES), shape(8, 128),
+            shape(2, PAD, events), shape(4, ROWS, LANES), shape(4, ROWS, LANES), shape(8, 128),
         ),
         spaces,
         scratch,
@@ -934,8 +1015,8 @@
         micros=40,
         in_place=(shape(4, ROWS, LANES),),
     )(
-        meta, 2 * index, window_count, own_piece, z_pieces, xy_pieces, far_a, far_b, code_n, sin_n, w_kvc,
-        srct, msg, sin_d, delta, ndelta, tcol, w_md, w_mc, w_q, w_kvm, *w_more, gathered,
+        meta, 2 * index, window_count, own_piece, z_pieces, xy_pieces, far_a, far_b, late,
+        delta, ndelta, tcol, w_tt, gathered,
     )
 
     fresh_own = lax.dynamic_index_in_dim(fresh, head, 0, False)
@@ -957,7 +1038,7 @@
         return lax.ppermute(x, ("row", "head"), pairs)
 
     bits = jnp.stack(
-        [jnp.where(head == 0, (row // steps[0]) % 2, (row // steps[1]) % 2) for steps in orders[:2]]
+        [jnp.where(head == 0, (row // steps[0]) % 2, (row // steps[1]) % 2) for steps in orders[:3]]
     ).astype(jnp.int32)
     wire = bf(2 * ROWS, LANES)
     keep, send = vmem_call(
@@ -966,9 +1047,20 @@
     keep, send = vmem_call(
         second_sum_kernel, (shape(ROWS, LANES), bf(ROWS + EXTRA, LANES)), "svv", limit=VMEM_SMALL, micros=1
     )(bits, keep, joint_hop(send, orders[0]))
-    total = vmem_call(third_sum_kernel, wire, "vv", limit=VMEM_SMALL, micros=1)(keep, joint_hop(send, orders[1]))
-    for steps in orders[2:]:
-        total = vmem_call(wire_sum_kernel, wire, "vv", limit=VMEM_SMALL, micros=1)(total, joint_hop(total, steps))
+    keep, send = vmem_call(
+        third_sum_kernel, (shape(ROWS // 2, LANES), bf(ROWS, LANES)), "svv", limit=VMEM_SMALL, micros=1
+    )(bits, keep, joint_hop(send, orders[1]))
+    eighth = bf(ROWS, LANES)
+    part = vmem_call(fourth_sum_kernel, eighth, "vv", limit=VMEM_SMALL, micros=1)(
+        keep, joint_hop(send, orders[2])
+    )
+    for steps in orders[3:]:
+        part = vmem_call(eighth_sum_kernel, eighth, "vv", limit=VMEM_SMALL, micros=1)(
+            part, joint_hop(part, steps)
+        )
+    total = vmem_call(join_kernel, wire, "svv", limit=VMEM_SMALL, micros=1)(
+        bits, part, joint_hop(part, orders[2])
+    )
     second_q = joint_hop(total, orders[1])
     first_q = joint_hop(total, orders[0])
     last_q = joint_hop(second_q, orders[0])

time: 192 us -> 181 us (0.943)
  waiting for transfers between devices: 61.3 us -> 52.8 us
  Pallas kernels: 84.9 us -> 82.2 us
    ppermute x7 -> x8, waiting for transfers between devices: 45.9 us -> 37.6 us  [joint_hop(): return lax.ppermute(x, ('row', 'head'), pairs)]
    pallas_call x4 -> x5, Pallas kernels: 57.7 us -> 55 us  [the longest x1 53.3 us: per_device(): vmem_call(functools.partial(step_kernel, planes, use_table), (shape(2, PA...]
    ppermute x7 -> x8, starting transfers between devices: 10.9 us -> 10.9 us  [joint_hop(): return lax.ppermute(x, ('row', 'head'), pairs)]
  transfers between devices with their start and end apart: 32 -> 33, of which waited for: 12 -> 13; matrix products, arithmetic and copies ran while one was open for 4% -> 4% of each run, Pallas kernels for 11% -> 12%
where the time goes in v2:
time: 181 us
  Pallas kernels  82.2 us (45%)
  waiting for transfers between devices  52.8 us (29%)
  starting transfers between devices  30.8 us (17%)
  local copies, waits for them, and re-layouts  10.3 us (6%)
  other arithmetic  2.64 us (1%)
  between operations  2.1 us (1%)
    pallas_call x1, Pallas kernels, per_device(): vmem_call(functools.partial(step_kernel, planes, use_table), (shape(2, PA...  53.3 us
    ppermute x8, waiting for transfers between devices, joint_hop(): return lax.ppermute(x, ('row', 'head'), pairs)  37.6 us
    ppermute x12, starting transfers between devices, hop(): return lax.ppermute(x, 'row', flips(n_row, step))  16.9 us
    ppermute x8, starting transfers between devices, joint_hop(): return lax.ppermute(x, ('row', 'head'), pairs)  10.9 us
    ppermute x12, waiting for transfers between devices, hop(): return lax.ppermute(x, 'row', flips(n_row, step))  9.85 us
    pallas_call x1, Pallas kernels, per_device(): vmem_call(codes_kernel, code_shapes, 'svvvvvv', micros=9)  9 us
    ppermute x13, waiting for transfers between devices, swap(): return lax.ppermute(x, 'head', [(0, 1), (1, 0)])  5.41 us
    pallas_call x1, Pallas kernels, per_device(): vmem_call(weights_kernel, w_shapes, 'svvvv', micros=6)  5.13 us
  transfers between devices with their start and end apart: 33, of which 13 were waited for; matrix products, arithmetic and copies ran while one was open for 4% of the time, Pallas kernels for 12%

profile of v2, /device:TPU:0, one launch (start us, length us, event | category | flops | bytes accessed | tf_op | source)
XLA Modules:
  0.0 180.8 jit_solution(17459172138981087347)
XLA Ops:
  1.4 0.6 pad_add_fusion.meta
  2.0 1.9 %shard_map.511.own_piece_0_ = bf16[176,512]{1,0:T(8,128)(2,1)} custom-call(s32[2]{0:T(128)} %pad_add_fusion.meta, s32[1]{0:T(128)S(6)} %copy.64.wcount, f32[172,1024]{1,0:T(8,128)} %bitcast.69, s32[1,1024]{1,0:T(1,128)} %bitcast.78), custom_call_target="tpu_custom_call" | custom-call | flops 1000000000 | bytes 1000000 | tf_op jit(solution)/shard_map/pallas_call | solution.py:912
  3.9 3.9 %collective-permute-start.5 = (bf16[176,512]{1,0:T(8,128)(2,1)}, bf16[176,512]{1,0:T(8,128)(2,1)S(1)}, u32[]{:S(2)}, u32[]{:S(2)}) collective-permute-start(bf16[176,512]{1,0:T(8,128)(2,1)} %shard_map.511.own_piece_0_), channel_id=1, source_target_pairs={{0,6},{2,4},{4,2},{6,0},{8,14},{10,12},{12,10},{14,8},{16,22},{18,... | collective-permute-start | bytes 540680 | tf_op jit(solution)/shard_map/ppermute | solution.py:906
  7.8 0.5 collective-permute-start.4
  8.3 0.9 slice.30
  9.3 1.6 collective-permute-start
  10.9 2.6 %collective-permute-start.1 = (bf16[128,512]{1,0:T(8,128)(2,1)S(1)}, bf16[128,512]{1,0:T(8,128)(2,1)S(1)}, u32[]{:S(2)}, u32[]{:S(2)}) collective-permute-start(bf16[128,512]{1,0:T(8,128)(2,1)S(1)} %slice.30), channel_id=1, source_target_pairs={{0,16},{2,18},{4,20},{6,22},{8,24},{10,26},{12,28},{14,30},{16,0},... | collective-permute-start | bytes 393224 | tf_op jit(solution)/shard_map/ppermute | solution.py:906
  13.7 0.8 slice_bitcast_fusion.3
  14.9 0.9 collective-permute-done
  15.9 7.4 %collective-permute-done.1 = bf16[128,512]{1,0:T(8,128)(2,1)S(1)} collective-permute-done((bf16[128,512]{1,0:T(8,128)(2,1)S(1)}, bf16[128,512]{1,0:T(8,128)(2,1)S(1)}, u32[]{:S(2)}, u32[]{:S(2)}) %collective-permute-start.1) | collective-permute-done | bytes 131104 | tf_op jit(solution)/shard_map/ppermute | solution.py:906
  23.6 0.8 copy.61
  24.4 0.5 collective-permute-start.10
  24.9 1.5 collective-permute-start.11
  26.4 1.4 collective-permute-start.12
  27.8 2.0 %collective-permute-start.13 = (bf16[4,48,512]{2,1,0:T(8,128)(2,1)S(1)}, bf16[4,48,512]{2,1,0:T(8,128)(2,1)S(1)}, u32[]{:S(2)}, u32[]{:S(2)}) collective-permute-start(bf16[4,48,512]{2,1,0:T(8,128)(2,1)S(1)} %pad_maximum_fusion.2), channel_id=1, source_target_pairs={{0,8},{2,10},{4,12},{6,14},{8,0},{10,2},{12,4},{14,6},{16,24},{18,... | collective-permute-start | bytes 589832 | tf_op jit(solution)/shard_map/ppermute | solution.py:906
  29.8 1.1 collective-permute-start.14
  30.9 9.0 %shard_map.513 = (f32[2,88,512]{2,1,0:T(8,128)}, bf16[516,512]{1,0:T(8,128)(2,1)}, f32[172,512]{1,0:T(8,128)}, bf16[172,5120]{1,0:T(8,128)(2,1)}, bf16[172,5120]{1,0:T(8,128)(2,1)}) custom-call(s32[2]{0:T(128)} %pad_add_fusion.meta, f32[172,1024]{1,0:T(8,128)} %bitcast.70, s32[1,1024]{1,0:T(1,128)} %src.1, f32[1,1024]{1,0:T(1,128)} %bitcast.82, ...), custom_call_target="tpu_custom_call" | custom-call | flops 8999999488 | bytes 9000000 | tf_op jit(solution)/shard_map/pallas_call | solution.py:936
  39.9 1.5 collective-permute-start.15
  41.4 5.1 %shard_map.514 = (bf16[2,264,256]{2,1,0:T(8,128)(2,1)}, bf16[2,258,172]{2,1,0:T(8,128)(2,1)}, bf16[2,88,348]{2,1,0:T(8,128)(2,1)}, bf16[352,256]{1,0:T(8,128)(2,...) custom-call(s32[2]{0:T(128)} %pad_add_fusion.meta, ...), custom_call_target="tpu_custom_call" | custom-call | flops 6000000000 | bytes 6000000 | tf_op jit(solution)/shard_map/pallas_call | solution.py:945
  46.5 1.5 collective-permute-done.15.far_b_0__2_
  48.1 0.5 collective-permute-start.20
  48.7 0.4 collective-permute-start.7
  49.3 1.0 collective-permute-done.7.own_piece_1_
  50.6 0.4 copy-done.47
  51.0 0.2 collective-permute-start.17
  51.3 0.3 collective-permute-start.18
  51.6 0.4 copy-done.45
  51.9 0.7 copy-done.46
  52.6 0.3 collective-permute-start.8
  53.0 0.6 add_multiply_fusion.idx
  53.6 0.8 collective-permute-done.8.z_pieces_1_
  54.6 0.7 copy-done.38
  55.2 53.3 %shard_map.515 = (f32[2,88,512]{2,1,0:T(8,128)}, f32[4,144,768]{2,1,0:T(8,128)}, f32[4,144,768]{2,1,0:T(8,128)}, f32[8,128]{1,0:T(8,128)}) custom-call(s32[2]{0:T(128)} %pad_add_fusion.meta, s32[5632]{0:T(1024)} %add_multiply_fusion.idx, s32[1]{0:T(128)S(6)} %copy.64.wcount, bf16[176,512]{1,0:T(8,128)(2,1)} %shard_map.511.own_piece_0_, ...), custom_call_target="tpu_custom_call" | custom-call | flops 40000000000 | bytes 40000000 | tf_op jit(solution)/shard_map/pallas_call | solution.py:1007
  108.6 0.3 collective-permute-start.23
  109.0 3.5 %collective-permute-done.23.got = f32[4,144,768]{2,1,0:T(8,128)S(1)} collective-permute-done((f32[4,144,768]{2,1,0:T(8,128)}, f32[4,144,768]{2,1,0:T(8,128)S(1)}, u32[]{:S(2)}, u32[]{:S(2)}) %collective-permute-start.23) | collective-permute-done | bytes 1769504 | tf_op jit(solution)/shard_map/ppermute | solution.py:903
  112.5 1.5 copy-done.29
  114.0 0.7 shard_map.517
  114.7 0.6 collective-permute-start.24
  115.3 8.3 %collective-permute-done.24.got = bf16[2,160,768]{2,1,0:T(8,128)(2,1)S(1)} collective-permute-done((bf16[2,160,768]{2,1,0:T(8,128)(2,1)S(1)}, bf16[2,160,768]{2,1,0:T(8,128)(2,1)S(1)}, u32[]{:S(2)}, u32[]{:S(2)}) %collective-permute-start.24) | collective-permute-done | bytes 491552 | tf_op jit(solution)/shard_map/ppermute | solution.py:1038
  123.6 0.6 shard_map.518
  124.3 1.6 collective-permute-start.25
  125.9 4.7 %collective-permute-done.25.got = bf16[160,768]{1,0:T(8,128)(2,1)S(1)} collective-permute-done((bf16[160,768]{1,0:T(8,128)(2,1)S(1)}, bf16[160,768]{1,0:T(8,128)(2,1)S(1)}, u32[]{:S(2)}, u32[]{:S(2)}) %collective-permute-start.25) | collective-permute-done | bytes 245792 | tf_op jit(solution)/shard_map/ppermute | solution.py:1038
  130.5 0.9 shard_map.519
  131.4 4.1 %collective-permute-start.26 = (bf16[144,768]{1,0:T(8,128)(2,1)S(1)}, bf16[144,768]{1,0:T(8,128)(2,1)S(1)}, u32[]{:S(2)}, u32[]{:S(2)}) collective-permute-start(bf16[144,768]{1,0:T(8,128)(2,1)S(1)} %get-tuple-element.144), channel_id=1, source_target_pairs={{0,8},{1,3},{2,10},{3,1},{4,12},{5,7},{6,14},{7,5},{8,0},{9,11},{1... | collective-permute-start | bytes 663560 | tf_op jit(solution)/shard_map/ppermute | solution.py:1038
  135.6 3.9 %collective-permute-done.26.got = bf16[144,768]{1,0:T(8,128)(2,1)S(1)} collective-permute-done((bf16[144,768]{1,0:T(8,128)(2,1)S(1)}, bf16[144,768]{1,0:T(8,128)(2,1)S(1)}, u32[]{:S(2)}, u32[]{:S(2)}) %collective-permute-start.26) | collective-permute-done | bytes 221216 | tf_op jit(solution)/shard_map/ppermute | solution.py:1038
  139.6 2.0 %collective-permute-start.27 = (bf16[144,768]{1,0:T(8,128)(2,1)S(1)}, bf16[144,768]{1,0:T(8,128)(2,1)S(1)}, u32[]{:S(2)}, u32[]{:S(2)}) collective-permute-start(bf16[144,768]{1,0:T(8,128)(2,1)S(1)} %shard_map.520.one), channel_id=1, source_target_pairs={{0,16},{1,5},{2,18},{3,7},{4,20},{5,1},{6,22},{7,3},{8,24},{9,13},... | collective-permute-start | bytes 663560 | tf_op jit(solution)/shard_map/ppermute | solution.py:1038
  141.5 7.3 %collective-permute-done.27.two = bf16[144,768]{1,0:T(8,128)(2,1)S(1)} collective-permute-done((bf16[144,768]{1,0:T(8,128)(2,1)S(1)}, bf16[144,768]{1,0:T(8,128)(2,1)S(1)}, u32[]{:S(2)}, u32[]{:S(2)}) %collective-permute-start.27) | collective-permute-done | bytes 221216 | tf_op jit(solution)/shard_map/ppermute | solution.py:1038
  149.0 6.3 %collective-permute-done.28.two = bf16[144,768]{1,0:T(8,128)(2,1)S(1)} collective-permute-done((bf16[144,768]{1,0:T(8,128)(2,1)S(1)}, bf16[144,768]{1,0:T(8,128)(2,1)S(1)}, u32[]{:S(2)}, u32[]{:S(2)}) %collective-permute-start.28) | collective-permute-done | bytes 221216 | tf_op jit(solution)/shard_map/ppermute | solution.py:1038
  155.3 0.6 shard_map.522.w0
  156.0 1.6 collective-permute-start.29
  157.5 0.8 dynamic-slice_bitcast_fusion.2
  158.3 0.5 collective-permute-start.30
  158.8 5.5 %collective-permute-done.29.w1 = bf16[288,768]{1,0:T(8,128)(2,1)S(1)} collective-permute-done((bf16[288,768]{1,0:T(8,128)(2,1)S(1)}, bf16[288,768]{1,0:T(8,128)(2,1)S(1)}, u32[]{:S(2)}, u32[]{:S(2)}) %collective-permute-start.29) | collective-permute-done | bytes 442400 | tf_op jit(solution)/shard_map/ppermute | solution.py:1038
  164.3 0.5 collective-permute-start.31
  164.8 1.0 dynamic-slice_bitcast_fusion.mem
  166.1 1.2 slice.29
  167.3 1.2 maximum_select_fusion.fresh
  168.6 2.4 %shard_map.516 = f32[86,1024]{1,0:T(8,128)} custom-call(f32[86,1024]{1,0:T(8,128)S(1)} %dynamic-slice_bitcast_fusion.mem, f32[88,1024]{1,0:T(8,128)S(1)} %maximum_select_fusion.fresh, s32[1024,1]{1,0:T(8,128)S(1)} %copy.63.src, s32[1]{0:T(128)S(6)} %copy.64.wcount), custom_call_target="tpu_custom_call" | custom-call | flops 3000000000 | bytes 3000000 | tf_op jit(solution)/shard_map/pallas_call | solution.py:1030
  171.1 1.6 collective-permute-done.31.w3
  172.6 0.6 shard_map.523.own
  173.2 0.3 collective-permute-start.32
  173.7 5.0 %shard_map.525 = (f32[258,688]{1,0:T(8,128)}, f32[258,688]{1,0:T(8,128)}, f32[258,688]{1,0:T(8,128)}, f32[172,258]{1,0:T(8,128)}, f32[172,258]{1,0:T(8,128)}, /*...) custom-call(s32[3]{0:T(128)S(1)} %pad_add_fusion.1.bits, ...), custom_call_target="tpu_custom_call" | custom-call | flops 4000000000 | bytes 4000000 | tf_op jit(solution)/shard_map/pallas_call | solution.py:1087
  178.8 1.6 shard_map.524
  180.3 0.5 slice.28
  (135 shorter events, 2.3 us)
Async XLA Ops:
  0.7 52.3 %copy-start = (s32[1024,10]{0,1:T(8,128)S(1)}, s32[1024,10]{0,1:T(8,128)}, u32[]{:S(2)}) copy-start(s32[1024,10]{0,1:T(8,128)} %param.35) | copy-start | bytes 122884
  2.0 12.6 %copy-start.1 = (f32[2,86,172]{2,0,1:T(2,128)S(1)}, f32[2,86,172]{2,0,1:T(2,128)}, u32[]{:S(2)}) copy-start(f32[2,86,172]{2,0,1:T(2,128)} %param.55) | copy-start | bytes 355012
  2.0 12.6 %copy-start.4 = (f32[688,258]{0,1:T(8,128)S(1)}, f32[688,258]{0,1:T(8,128)}, u32[]{:S(2)}) copy-start(f32[688,258]{0,1:T(8,128)} %param.40) | copy-start | bytes 2130052
  2.0 12.6 %copy-start.8 = (f32[3,344,86]{1,2,0:T(8,128)S(1)}, f32[3,344,86]{1,2,0:T(8,128)}, u32[]{:S(2)}) copy-start(f32[3,344,86]{1,2,0:T(8,128)} %param.52) | copy-start | bytes 1065028
  2.0 12.6 %copy-start.11 = (f32[172,258]{1,0:T(8,128)S(1)}, f32[172,258]{1,0:T(8,128)}, u32[]{:S(2)}) copy-start(f32[172,258]{1,0:T(8,128)} %refs_3_.3) | copy-start | bytes 532516
  2.0 12.6 %copy-start.20 = (f32[172,86]{1,0:T(8,128)S(1)}, f32[172,86]{1,0:T(8,128)}, u32[]{:S(2)}) copy-start(f32[172,86]{1,0:T(8,128)} %refs_15_.1) | copy-start | bytes 177508
  2.0 12.6 %copy-start.23 = (f32[2,258]{1,0:T(2,128)S(1)}, f32[2,258]{1,0:T(2,128)}, u32[]{:S(2)}) copy-start(f32[2,258]{1,0:T(2,128)} %refs_6_.1) | copy-start | bytes 6196
  3.9 19.4 %collective-permute-start.5 = (bf16[176,512]{1,0:T(8,128)(2,1)}, bf16[176,512]{1,0:T(8,128)(2,1)S(1)}, u32[]{:S(2)}, u32[]{:S(2)}) collective-permute-start(bf16[176,512]{1,0:T(8,128)(2,1)} %shard_map.511.own_piece_0_), channel_id=1, source_target_pairs={{0,6},{2,4},{4,2},{6,0},{8,14},{10,12},{12,10},{14,8},{16,22},{18,... | collective-permute-start | bytes 540680 | tf_op jit(solution)/shard_map/ppermute | solution.py:906
  7.8 15.6 %collective-permute-start.4 = (bf16[176,512]{1,0:T(8,128)(2,1)}, bf16[176,512]{1,0:T(8,128)(2,1)S(1)}, u32[]{:S(2)}, u32[]{:S(2)}) collective-permute-start(bf16[176,512]{1,0:T(8,128)(2,1)} %shard_map.511.own_piece_0_), channel_id=1, source_target_pairs={{0,4},{2,6},{4,0},{6,2},{8,12},{10,14},{12,8},{14,10},{16,20},{18,... | collective-permute-start | bytes 540680 | tf_op jit(solution)/shard_map/ppermute | solution.py:906
  9.3 6.5 %collective-permute-start = (bf16[128,512]{1,0:T(8,128)(2,1)S(1)}, bf16[128,512]{1,0:T(8,128)(2,1)S(1)}, u32[]{:S(2)}, u32[]{:S(2)}) collective-permute-start(bf16[128,512]{1,0:T(8,128)(2,1)S(1)} %slice.30), channel_id=1, source_target_pairs={{0,8},{2,10},{4,12},{6,14},{8,0},{10,2},{12,4},{14,6},{16,24},{18,... | collective-permute-start | bytes 393224 | tf_op jit(solution)/shard_map/ppermute | solution.py:906
  10.9 12.4 %collective-permute-start.1 = (bf16[128,512]{1,0:T(8,128)(2,1)S(1)}, bf16[128,512]{1,0:T(8,128)(2,1)S(1)}, u32[]{:S(2)}, u32[]{:S(2)}) collective-permute-start(bf16[128,512]{1,0:T(8,128)(2,1)S(1)} %slice.30), channel_id=1, source_target_pairs={{0,16},{2,18},{4,20},{6,22},{8,24},{10,26},{12,28},{14,30},{16,0},... | collective-permute-start | bytes 393224 | tf_op jit(solution)/shard_map/ppermute | solution.py:906
  13.5 9.8 %collective-permute-start.2 = (bf16[128,512]{1,0:T(8,128)(2,1)S(1)}, bf16[128,512]{1,0:T(8,128)(2,1)S(1)}, u32[]{:S(2)}, u32[]{:S(2)}) collective-permute-start(bf16[128,512]{1,0:T(8,128)(2,1)S(1)} %slice.30), channel_id=1, source_target_pairs={{0,24},{2,26},{4,28},{6,30},{8,16},{10,18},{12,20},{14,22},{16,8},... | collective-permute-start | bytes 393224 | tf_op jit(solution)/shard_map/ppermute | solution.py:906
  14.6 9.0 %copy-start.2 = (f32[2,172]{1,0:T(2,128)S(1)}, f32[2,172]{1,0:T(2,128)}, u32[]{:S(2)}) copy-start(f32[2,172]{1,0:T(2,128)} %refs_3_.2) | copy-start | bytes 4132
  14.9 25.0 %copy-start.3 = (bf16[752,768]{1,0:T(8,128)(2,1)}, bf16[752,768]{1,0:T(8,128)(2,1)S(1)}, u32[]{:S(2)}) copy-start(bf16[752,768]{1,0:T(8,128)(2,1)S(1)} %shard_map.512.own) | copy-start | bytes 3465220
  15.8 7.6 %collective-permute-start.3 = (bf16[176,512]{1,0:T(8,128)(2,1)S(1)}, bf16[176,512]{1,0:T(8,128)(2,1)S(1)}, u32[]{:S(2)}, u32[]{:S(2)}) collective-permute-start(bf16[176,512]{1,0:T(8,128)(2,1)S(1)} %copy-done.35), channel_id=1, source_target_pairs={{0,2},{2,0},{4,6},{6,4},{8,10},{10,8},{12,14},{14,12},{16,18},{18,... | collective-permute-start | bytes 540680 | tf_op jit(solution)/shard_map/ppermute | solution.py:906
  23.3 28.2 %copy-start.30 = (bf16[3,128,512]{2,1,0:T(8,128)(2,1)}, bf16[3,128,512]{2,1,0:T(8,128)(2,1)S(1)}, u32[]{:S(2)}) copy-start(bf16[3,128,512]{2,1,0:T(8,128)(2,1)S(1)} %pad_maximum_fusion.1.z_pieces_0_) | copy-start | bytes 1179652
  23.4 25.7 %copy-start.32 = (bf16[176,512]{1,0:T(8,128)(2,1)}, bf16[176,512]{1,0:T(8,128)(2,1)S(1)}, u32[]{:S(2)}) copy-start(bf16[176,512]{1,0:T(8,128)(2,1)S(1)} %collective-permute-done.5.xy_pieces_0__2_) | copy-start | bytes 540676
  23.4 25.7 %copy-start.33 = (bf16[176,512]{1,0:T(8,128)(2,1)}, bf16[176,512]{1,0:T(8,128)(2,1)S(1)}, u32[]{:S(2)}) copy-start(bf16[176,512]{1,0:T(8,128)(2,1)S(1)} %collective-permute-done.4.xy_pieces_0__1_) | copy-start | bytes 540676
  23.4 25.7 %copy-start.34 = (bf16[176,512]{1,0:T(8,128)(2,1)}, bf16[176,512]{1,0:T(8,128)(2,1)S(1)}, u32[]{:S(2)}) copy-start(bf16[176,512]{1,0:T(8,128)(2,1)S(1)} %collective-permute-done.3.xy_pieces_0__0_) | copy-start | bytes 540676
  23.5 6.3 %collective-permute-start.6 = (bf16[752,768]{1,0:T(8,128)(2,1)S(1)}, bf16[752,768]{1,0:T(8,128)(2,1)}, u32[]{:S(2)}, u32[]{:S(2)}) collective-permute-start(bf16[752,768]{1,0:T(8,128)(2,1)S(1)} %shard_map.512.own), channel_id=1, source_target_pairs={{0,1},{1,0},{2,3},{3,2},{4,5},{5,4},{6,7},{7,6},{8,9},{9,8},{10,11... | collective-permute-start | bytes 3465224 | tf_op jit(solution)/shard_map/ppermute | solution.py:903
  24.4 23.6 %collective-permute-start.10 = (bf16[3,128,512]{2,1,0:T(8,128)(2,1)S(1)}, bf16[3,128,512]{2,1,0:T(8,128)(2,1)}, u32[]{:S(2)}, u32[]{:S(2)}) collective-permute-start(bf16[3,128,512]{2,1,0:T(8,128)(2,1)S(1)} %pad_maximum_fusion.1.z_pieces_0_), channel_id=1, source_target_pairs={{0,2},{2,0},{4,6},{6,4},{8,10},{10,8},{12,14},{14,12},{16,18},{18,... | collective-permute-start | bytes 1179656 | tf_op jit(solution)/shard_map/ppermute | solution.py:906
  24.9 23.1 %collective-permute-start.11 = (bf16[3,128,512]{2,1,0:T(8,128)(2,1)S(1)}, bf16[3,128,512]{2,1,0:T(8,128)(2,1)}, u32[]{:S(2)}, u32[]{:S(2)}) collective-permute-start(bf16[3,128,512]{2,1,0:T(8,128)(2,1)S(1)} %pad_maximum_fusion.1.z_pieces_0_), channel_id=1, source_target_pairs={{0,4},{2,6},{4,0},{6,2},{8,12},{10,14},{12,8},{14,10},{16,20},{18,... | collective-permute-start | bytes 1179656 | tf_op jit(solution)/shard_map/ppermute | solution.py:906
  26.4 21.6 %collective-permute-start.12 = (bf16[3,128,512]{2,1,0:T(8,128)(2,1)S(1)}, bf16[3,128,512]{2,1,0:T(8,128)(2,1)}, u32[]{:S(2)}, u32[]{:S(2)}) collective-permute-start(bf16[3,128,512]{2,1,0:T(8,128)(2,1)S(1)} %pad_maximum_fusion.1.z_pieces_0_), channel_id=1, source_target_pairs={{0,6},{2,4},{4,2},{6,0},{8,14},{10,12},{12,10},{14,8},{16,22},{18,... | collective-permute-start | bytes 1179656 | tf_op jit(solution)/shard_map/ppermute | solution.py:906
  27.8 12.0 %collective-permute-start.13 = (bf16[4,48,512]{2,1,0:T(8,128)(2,1)S(1)}, bf16[4,48,512]{2,1,0:T(8,128)(2,1)S(1)}, u32[]{:S(2)}, u32[]{:S(2)}) collective-permute-start(bf16[4,48,512]{2,1,0:T(8,128)(2,1)S(1)} %pad_maximum_fusion.2), channel_id=1, source_target_pairs={{0,8},{2,10},{4,12},{6,14},{8,0},{10,2},{12,4},{14,6},{16,24},{18,... | collective-permute-start | bytes 589832 | tf_op jit(solution)/shard_map/ppermute | solution.py:906
  29.8 16.7 %collective-permute-start.14 = (bf16[4,48,512]{2,1,0:T(8,128)(2,1)S(1)}, bf16[4,48,512]{2,1,0:T(8,128)(2,1)S(1)}, u32[]{:S(2)}, u32[]{:S(2)}) collective-permute-start(bf16[4,48,512]{2,1,0:T(8,128)(2,1)S(1)} %pad_maximum_fusion.2), channel_id=1, source_target_pairs={{0,16},{2,18},{4,20},{6,22},{8,24},{10,26},{12,28},{14,30},{16,0},... | collective-permute-start | bytes 589832 | tf_op jit(solution)/shard_map/ppermute | solution.py:906
  39.9 8.1 %copy-start.42 = (bf16[4,48,512]{2,1,0:T(8,128)(2,1)}, bf16[4,48,512]{2,1,0:T(8,128)(2,1)S(1)}, u32[]{:S(2)}) copy-start(bf16[4,48,512]{2,1,0:T(8,128)(2,1)S(1)} %collective-permute-done.13.far_b_0__0_) | copy-start | bytes 589828
  39.9 8.1 %collective-permute-start.15 = (bf16[4,48,512]{2,1,0:T(8,128)(2,1)S(1)}, bf16[4,48,512]{2,1,0:T(8,128)(2,1)S(1)}, u32[]{:S(2)}, u32[]{:S(2)}) collective-permute-start(bf16[4,48,512]{2,1,0:T(8,128)(2,1)S(1)} %pad_maximum_fusion.2), channel_id=1, source_target_pairs={{0,24},{2,26},{4,28},{6,30},{8,16},{10,18},{12,20},{14,22},{16,8},... | collective-permute-start | bytes 589832 | tf_op jit(solution)/shard_map/ppermute | solution.py:906
  41.4 11.5 %copy-start.37 = (s32[1024]{0:T(1024)S(1)}, s32[1024]{0:T(1024)}, u32[]{:S(2)}) copy-start(s32[1024]{0:T(1024)} %param.34) | copy-start | bytes 12292
  46.5 5.0 %copy-start.43 = (bf16[4,48,512]{2,1,0:T(8,128)(2,1)}, bf16[4,48,512]{2,1,0:T(8,128)(2,1)S(1)}, u32[]{:S(2)}) copy-start(bf16[4,48,512]{2,1,0:T(8,128)(2,1)S(1)} %collective-permute-done.14.far_b_0__1_) | copy-start | bytes 589828
  48.0 3.6 %copy-start.44 = (bf16[4,48,512]{2,1,0:T(8,128)(2,1)}, bf16[4,48,512]{2,1,0:T(8,128)(2,1)S(1)}, u32[]{:S(2)}) copy-start(bf16[4,48,512]{2,1,0:T(8,128)(2,1)S(1)} %collective-permute-done.15.far_b_0__2_) | copy-start | bytes 589828
  48.0 3.0 %collective-permute-start.19 = (bf16[4,48,512]{2,1,0:T(8,128)(2,1)S(1)}, bf16[4,48,512]{2,1,0:T(8,128)(2,1)}, u32[]{:S(2)}, u32[]{:S(2)}) collective-permute-start(bf16[4,48,512]{2,1,0:T(8,128)(2,1)S(1)} %collective-permute-done.13.far_b_0__0_), channel_id=1, source_target_pairs={{0,1},{1,0},{2,3},{3,2},{4,5},{5,4},{6,7},{7,6},{8,9},{9,8},{10,11... | collective-permute-start | bytes 589832 | tf_op jit(solution)/shard_map/ppermute | solution.py:903
  48.1 3.2 %collective-permute-start.20 = (bf16[4,48,512]{2,1,0:T(8,128)(2,1)S(1)}, bf16[4,48,512]{2,1,0:T(8,128)(2,1)S(1)}, u32[]{:S(2)}, u32[]{:S(2)}) collective-permute-start(bf16[4,48,512]{2,1,0:T(8,128)(2,1)S(1)} %collective-permute-done.14.far_b_0__1_), channel_id=1, source_target_pairs={{0,1},{1,0},{2,3},{3,2},{4,5},{5,4},{6,7},{7,6},{8,9},{9,8},{10,11... | collective-permute-start | bytes 589832 | tf_op jit(solution)/shard_map/ppermute | solution.py:903
  48.6 2.9 %collective-permute-start.21 = (bf16[4,48,512]{2,1,0:T(8,128)(2,1)S(1)}, bf16[4,48,512]{2,1,0:T(8,128)(2,1)S(1)}, u32[]{:S(2)}, u32[]{:S(2)}) collective-permute-start(bf16[4,48,512]{2,1,0:T(8,128)(2,1)S(1)} %collective-permute-done.15.far_b_0__2_), channel_id=1, source_target_pairs={{0,1},{1,0},{2,3},{3,2},{4,5},{5,4},{6,7},{7,6},{8,9},{9,8},{10,11... | collective-permute-start | bytes 589832 | tf_op jit(solution)/shard_map/ppermute | solution.py:903
  48.7 1.7 collective-permute-start.7
  49.2 5.3 %collective-permute-start.9 = (bf16[3,176,512]{2,1,0:T(8,128)(2,1)S(1)}, bf16[3,176,512]{2,1,0:T(8,128)(2,1)S(1)}, u32[]{:S(2)}, u32[]{:S(2)}) collective-permute-start(bf16[3,176,512]{2,1,0:T(8,128)(2,1)S(1)} %pad_maximum_fusion), channel_id=1, source_target_pairs={{0,1},{1,0},{2,3},{3,2},{4,5},{5,4},{6,7},{7,6},{8,9},{9,8},{10,11... | collective-permute-start | bytes 1622024 | tf_op jit(solution)/shard_map/ppermute | solution.py:903
  50.3 3.2 %collective-permute-start.16 = (bf16[3,128,512]{2,1,0:T(8,128)(2,1)}, bf16[3,128,512]{2,1,0:T(8,128)(2,1)S(1)}, u32[]{:S(2)}, u32[]{:S(2)}) collective-permute-start(bf16[3,128,512]{2,1,0:T(8,128)(2,1)} %collective-permute-done.10.far_a_0__0_), channel_id=1, source_target_pairs={{0,1},{1,0},{2,3},{3,2},{4,5},{5,4},{6,7},{7,6},{8,9},{9,8},{10,11... | collective-permute-start | bytes 1179656 | tf_op jit(solution)/shard_map/ppermute | solution.py:903
  51.0 2.6 %collective-permute-start.17 = (bf16[3,128,512]{2,1,0:T(8,128)(2,1)}, bf16[3,128,512]{2,1,0:T(8,128)(2,1)S(1)}, u32[]{:S(2)}, u32[]{:S(2)}) collective-permute-start(bf16[3,128,512]{2,1,0:T(8,128)(2,1)} %collective-permute-done.11.far_a_0__1_), channel_id=1, source_target_pairs={{0,1},{1,0},{2,3},{3,2},{4,5},{5,4},{6,7},{7,6},{8,9},{9,8},{10,11... | collective-permute-start | bytes 1179656 | tf_op jit(solution)/shard_map/ppermute | solution.py:903
  51.3 2.3 %collective-permute-start.18 = (bf16[3,128,512]{2,1,0:T(8,128)(2,1)}, bf16[3,128,512]{2,1,0:T(8,128)(2,1)S(1)}, u32[]{:S(2)}, u32[]{:S(2)}) collective-permute-start(bf16[3,128,512]{2,1,0:T(8,128)(2,1)} %collective-permute-done.12.far_a_0__2_), channel_id=1, source_target_pairs={{0,1},{1,0},{2,3},{3,2},{4,5},{5,4},{6,7},{7,6},{8,9},{9,8},{10,11... | collective-permute-start | bytes 1179656 | tf_op jit(solution)/shard_map/ppermute | solution.py:903
  52.6 1.9 %collective-permute-start.8 = (bf16[3,128,512]{2,1,0:T(8,128)(2,1)S(1)}, bf16[3,128,512]{2,1,0:T(8,128)(2,1)}, u32[]{:S(2)}, u32[]{:S(2)}) collective-permute-start(bf16[3,128,512]{2,1,0:T(8,128)(2,1)S(1)} %pad_maximum_fusion.1.z_pieces_0_), channel_id=1, source_target_pairs={{0,1},{1,0},{2,3},{3,2},{4,5},{5,4},{6,7},{7,6},{8,9},{9,8},{10,11... | collective-permute-start | bytes 1179656 | tf_op jit(solution)/shard_map/ppermute | solution.py:903
  108.6 4.0 %collective-permute-start.23 = (f32[4,144,768]{2,1,0:T(8,128)}, f32[4,144,768]{2,1,0:T(8,128)S(1)}, u32[]{:S(2)}, u32[]{:S(2)}) collective-permute-start(f32[4,144,768]{2,1,0:T(8,128)} %get-tuple-element.138), channel_id=1, source_target_pairs={{0,1},{1,0},{2,3},{3,2},{4,5},{5,4},{6,7},{7,6},{8,9},{9,8},{10,11... | collective-permute-start | bytes 5308424 | tf_op jit(solution)/shard_map/ppermute | solution.py:903
  114.7 8.9 %collective-permute-start.24 = (bf16[2,160,768]{2,1,0:T(8,128)(2,1)S(1)}, bf16[2,160,768]{2,1,0:T(8,128)(2,1)S(1)}, u32[]{:S(2)}, u32[]{:S(2)}) collective-permute-start(bf16[2,160,768]{2,1,0:T(8,128)(2,1)S(1)} %get-tuple-element.140), channel_id=1, source_target_pairs={{0,2},{1,9},{2,0},{3,11},{4,6},{5,13},{6,4},{7,15},{8,10},{9,1},{1... | collective-permute-start | bytes 1474568 | tf_op jit(solution)/shard_map/ppermute | solution.py:1038
  124.3 6.3 %collective-permute-start.25 = (bf16[160,768]{1,0:T(8,128)(2,1)S(1)}, bf16[160,768]{1,0:T(8,128)(2,1)S(1)}, u32[]{:S(2)}, u32[]{:S(2)}) collective-permute-start(bf16[160,768]{1,0:T(8,128)(2,1)S(1)} %get-tuple-element.142), channel_id=1, source_target_pairs={{0,4},{1,17},{2,6},{3,19},{4,0},{5,21},{6,2},{7,23},{8,12},{9,25},... | collective-permute-start | bytes 737288 | tf_op jit(solution)/shard_map/ppermute | solution.py:1038
  131.4 8.0 %collective-permute-start.26 = (bf16[144,768]{1,0:T(8,128)(2,1)S(1)}, bf16[144,768]{1,0:T(8,128)(2,1)S(1)}, u32[]{:S(2)}, u32[]{:S(2)}) collective-permute-start(bf16[144,768]{1,0:T(8,128)(2,1)S(1)} %get-tuple-element.144), channel_id=1, source_target_pairs={{0,8},{1,3},{2,10},{3,1},{4,12},{5,7},{6,14},{7,5},{8,0},{9,11},{1... | collective-permute-start | bytes 663560 | tf_op jit(solution)/shard_map/ppermute | solution.py:1038
  139.6 9.3 %collective-permute-start.27 = (bf16[144,768]{1,0:T(8,128)(2,1)S(1)}, bf16[144,768]{1,0:T(8,128)(2,1)S(1)}, u32[]{:S(2)}, u32[]{:S(2)}) collective-permute-start(bf16[144,768]{1,0:T(8,128)(2,1)S(1)} %shard_map.520.one), channel_id=1, source_target_pairs={{0,16},{1,5},{2,18},{3,7},{4,20},{5,1},{6,22},{7,3},{8,24},{9,13},... | collective-permute-start | bytes 663560 | tf_op jit(solution)/shard_map/ppermute | solution.py:1038
  148.9 8.6 %copy-start.31 = (f32[2,88,512]{2,1,0:T(8,128)S(1)}, f32[2,88,512]{2,1,0:T(8,128)}, u32[]{:S(2)}) copy-start(f32[2,88,512]{2,1,0:T(8,128)} %get-tuple-element.136) | copy-start | bytes 1081348
  148.9 16.9 %copy-start.36 = (s32[1,1024]{1,0:T(1,128)S(1)}, s32[1,1024]{1,0:T(1,128)}, u32[]{:S(2)}) copy-start(s32[1,1024]{1,0:T(1,128)} %src.1) | copy-start | bytes 12292
  148.9 6.4 %collective-permute-start.28 = (bf16[144,768]{1,0:T(8,128)(2,1)S(1)}, bf16[144,768]{1,0:T(8,128)(2,1)S(1)}, u32[]{:S(2)}, u32[]{:S(2)}) collective-permute-start(bf16[144,768]{1,0:T(8,128)(2,1)S(1)} %shard_map.521.one), channel_id=1, source_target_pairs={{0,8},{1,3},{2,10},{3,1},{4,12},{5,7},{6,14},{7,5},{8,0},{9,11},{1... | collective-permute-start | bytes 663560 | tf_op jit(solution)/shard_map/ppermute | solution.py:1038
  156.0 8.4 %collective-permute-start.29 = (bf16[288,768]{1,0:T(8,128)(2,1)S(1)}, bf16[288,768]{1,0:T(8,128)(2,1)S(1)}, u32[]{:S(2)}, u32[]{:S(2)}) collective-permute-start(bf16[288,768]{1,0:T(8,128)(2,1)S(1)} %shard_map.522.w0), channel_id=1, source_target_pairs={{0,4},{1,17},{2,6},{3,19},{4,0},{5,21},{6,2},{7,23},{8,12},{9,25},... | collective-permute-start | bytes 1327112 | tf_op jit(solution)/shard_map/ppermute | solution.py:1038
  158.3 9.0 %collective-permute-start.22 = (f32[88,512]{1,0:T(8,128)}, f32[88,512]{1,0:T(8,128)}, u32[]{:S(2)}, u32[]{:S(2)}) collective-permute-start(f32[88,512]{1,0:T(8,128)} %get-tuple-element.172), channel_id=1, source_target_pairs={{0,1},{1,0},{2,3},{3,2},{4,5},{5,4},{6,7},{7,6},{8,9},{9,8},{10,11... | collective-permute-start | bytes 540680 | tf_op jit(solution)/shard_map/ppermute | solution.py:903
  158.3 12.8 %collective-permute-start.30 = (bf16[288,768]{1,0:T(8,128)(2,1)S(1)}, bf16[288,768]{1,0:T(8,128)(2,1)S(1)}, u32[]{:S(2)}, u32[]{:S(2)}) collective-permute-start(bf16[288,768]{1,0:T(8,128)(2,1)S(1)} %shard_map.522.w0), channel_id=1, source_target_pairs={{0,2},{1,9},{2,0},{3,11},{4,6},{5,13},{6,4},{7,15},{8,10},{9,1},{1... | collective-permute-start | bytes 1327112 | tf_op jit(solution)/shard_map/ppermute | solution.py:1038
  164.3 8.3 %collective-permute-start.31 = (bf16[288,768]{1,0:T(8,128)(2,1)S(1)}, bf16[288,768]{1,0:T(8,128)(2,1)S(1)}, u32[]{:S(2)}, u32[]{:S(2)}) collective-permute-start(bf16[288,768]{1,0:T(8,128)(2,1)S(1)} %collective-permute-done.29.w1), channel_id=1, source_target_pairs={{0,2},{1,9},{2,0},{3,11},{4,6},{5,13},{6,4},{7,15},{8,10},{9,1},{1... | collective-permute-start | bytes 1327112 | tf_op jit(solution)/shard_map/ppermute | solution.py:1038
  168.5 5.0 %copy-start.13 = (f32[172,258]{1,0:T(8,128)S(1)}, f32[172,258]{1,0:T(8,128)}, u32[]{:S(2)}) copy-start(f32[172,258]{1,0:T(8,128)} %refs_4_.3) | copy-start | bytes 532516
  168.5 5.0 %copy-start.14 = (f32[172,258]{1,0:T(8,128)S(1)}, f32[172,258]{1,0:T(8,128)}, u32[]{:S(2)}) copy-start(f32[172,258]{1,0:T(8,128)} %refs_5_.3) | copy-start | bytes 532516
  168.5 5.0 %copy-start.19 = (f32[2,86,172]{2,0,1:T(2,128)S(1)}, f32[2,86,172]{2,0,1:T(2,128)}, u32[]{:S(2)}) copy-start(f32[2,86,172]{2,0,1:T(2,128)} %param.57) | copy-start | bytes 355012
  168.6 5.0 %copy-start.21 = (f32[172,86]{1,0:T(8,128)S(1)}, f32[172,86]{1,0:T(8,128)}, u32[]{:S(2)}) copy-start(f32[172,86]{1,0:T(8,128)} %refs_16_.1) | copy-start | bytes 177508
  168.6 5.0 %copy-start.22 = (f32[172,86]{1,0:T(8,128)S(1)}, f32[172,86]{1,0:T(8,128)}, u32[]{:S(2)}) copy-start(f32[172,86]{1,0:T(8,128)} %refs_17_.1) | copy-start | bytes 177508
  171.0 2.6 %copy-start.10 = (f32[3,344,86]{1,2,0:T(8,128)S(1)}, f32[3,344,86]{1,2,0:T(8,128)}, u32[]{:S(2)}) copy-start(f32[3,344,86]{1,2,0:T(8,128)} %param.54) | copy-start | bytes 1065028
  173.2 5.5 %collective-permute-start.32 = (bf16[128,768]{1,0:T(8,128)(2,1)S(1)}, bf16[128,768]{1,0:T(8,128)(2,1)S(1)}, u32[]{:S(2)}, u32[]{:S(2)}) collective-permute-start(bf16[128,768]{1,0:T(8,128)(2,1)S(1)} %shard_map.523.own), channel_id=1, source_target_pairs={{0,1},{1,0},{2,3},{3,2},{4,5},{5,4},{6,7},{7,6},{8,9},{9,8},{10,11... | collective-permute-start | bytes 589832 | tf_op jit(solution)/shard_map/ppermute | solution.py:903
  173.6 5.1 %copy-start.15 = (f32[172,172]{1,0:T(8,128)S(1)}, f32[172,172]{1,0:T(8,128)}, u32[]{:S(2)}) copy-start(f32[172,172]{1,0:T(8,128)} %refs_0_.1) | copy-start | bytes 355012
  173.7 5.1 %copy-start.16 = (f32[172,172]{1,0:T(8,128)S(1)}, f32[172,172]{1,0:T(8,128)}, u32[]{:S(2)}) copy-start(f32[172,172]{1,0:T(8,128)} %refs_1_.1) | copy-start | bytes 355012
  173.7 5.1 %copy-start.17 = (f32[172,172]{1,0:T(8,128)S(1)}, f32[172,172]{1,0:T(8,128)}, u32[]{:S(2)}) copy-start(f32[172,172]{1,0:T(8,128)} %refs_2_.1) | copy-start | bytes 355012
  173.7 5.1 %copy-start.26 = (f32[2,172]{1,0:T(2,128)S(1)}, f32[2,172]{1,0:T(2,128)}, u32[]{:S(2)}) copy-start(f32[2,172]{1,0:T(2,128)} %refs_4_.2) | copy-start | bytes 4132
  173.7 5.1 %copy-start.27 = (f32[2,172]{1,0:T(2,128)S(1)}, f32[2,172]{1,0:T(2,128)}, u32[]{:S(2)}) copy-start(f32[2,172]{1,0:T(2,128)} %refs_5_.2) | copy-start | bytes 4132
  173.7 5.1 %copy-start.28 = (s32[2]{0:T(128)S(1)}, s32[2]{0:T(128)}, u32[]{:S(2)}) copy-start(s32[2]{0:T(128)} %pad_add_fusion.meta) | copy-start | bytes 28
  (17 other events, 29.0 us)

commit v3 on v2

--- a/solution.py
+++ b/solution.py
@@ -291,8 +291,12 @@
     n_memory = len(copies)
     first_copy.append(n_memory)
     for src, dst in zip(late_in, late):
-        start(src, dst)
+        copies.append(pltpu.make_async_copy(src, dst, sems.at[len(copies)]))
     n_late = len(copies)
+
+    def start_late():
+        for copy in copies[n_memory:n_late]:
+            copy.start()
 
     def group_here(r):
         for copy in copies[first_copy[r] : first_copy[r + 1]]:
@@ -302,10 +306,14 @@
     def each_group(work):
         if groups <= 8:
             for r in range(groups):
-                work(group_here(r))
+                g = group_here(r)
+                if r == groups - 1:
+                    start_late()
+                work(g)
         else:
             for r in range(groups):
                 group_here(r)
+            start_late()
             lax.fori_loop(0, groups, lambda g, s: (work(g), s)[1], 0)
 
     count[...] = jnp.zeros_like(count)
@@ -610,8 +618,7 @@
         tgrad[1, :width] -= zero_term
 
         def send_fine(k):
-            for place, out in ((1, o_other), (0, o_own)):
-                start(fine.at[place, pl.ds(k * FINE, FINE)], out.at[k, pl.ds(COARSE, FINE)])
+            start(fine.at[0, pl.ds(k * FINE, FINE)], o_own.at[k, pl.ds(COARSE, FINE)])
 
         for k in range(3):
             send_fine(k)
@@ -660,8 +667,10 @@
         o_live[...] = jnp.broadcast_to(stat[0:1, :], o_live.shape)
         send_fine(3)
         for k in range(4):
-            for place, out in ((1, o_other), (0, o_own)):
-                start(coarse.at[place, pl.ds(k * COARSE, COARSE)], out.at[k, pl.ds(0, COARSE)])
+            start(coarse.at[0, pl.ds(k * COARSE, COARSE)], o_own.at[k, pl.ds(0, COARSE)])
+        for k in range(4):
+            rows_c, rows_f = pl.ds(k * COARSE, COARSE), pl.ds(k * FINE, FINE)
+            to_half_wire(o_other.at[k], jnp.concatenate([coarse[1, rows_c], fine[1, rows_f]], 0))
         for copy in copies[n_late:]:
             copy.wait()
 
@@ -708,9 +717,9 @@
 def first_sum_kernel(bits, own, got, o_keep, o_send):
     for k in range(2):
         q = bits[0] * 2 + k
-        o_keep[k] = own[q] + got[q]
+        o_keep[k] = own[q] + from_half_wire(got[q])
         q = (1 - bits[0]) * 2 + k
-        to_half_wire(o_send.at[k], own[q] + got[q])
+        to_half_wire(o_send.at[k], own[q] + from_half_wire(got[q]))
 
 
 def second_sum_kernel(bits, keep, got, o_keep, o_send):
@@ -979,7 +988,7 @@
     late = (
         srct, msg, sin_d, w_md, w_mc, w_q, w_kvm, w_kvct, w_f, w_ft, w_d, w_dt, gin0, gst, code_n, w_kvc, sin_n,
     )
-    n_copies = 2 * (1 + (planes - 1) + (PLANE - 1) * planes + (planes - 1) * PLANE) + len(late) + 16
+    n_copies = 2 * (1 + (planes - 1) + (PLANE - 1) * planes + (planes - 1) * PLANE) + len(late) + 8
     scratch = [
         pltpu.SemaphoreType.DMA((n_copies,)),
         pltpu.VMEM((groups, full, wide_cols), BF),
@@ -1007,7 +1016,7 @@
     fresh, pack_own, pack_other, live = vmem_call(
         functools.partial(step_kernel, planes, use_table),
         (
-            shape(2, PAD, events), shape(4, ROWS, LANES), shape(4, ROWS, LANES), shape(8, 128),
+            shape(2, PAD, events), shape(4, ROWS, LANES), bf(4, ROWS + EXTRA, LANES), shape(8, 128),
         ),
         spaces,
         scratch,

time: 181 us -> 181 us (level)
    unnamed x98 -> x104, local copies, waits for them, and re-layouts: 4.74 us -> 4.79 us
where the time goes in v3:
time: 181 us
  Pallas kernels  83.2 us (46%)
  waiting for transfers between devices  51.9 us (29%)
  starting transfers between devices  30.8 us (17%)
  local copies, waits for them, and re-layouts  10.3 us (6%)
  other arithmetic  2.45 us (1%)
  between operations  2.12 us (1%)
    pallas_call x1, Pallas kernels, per_device(): vmem_call(functools.partial(step_kernel, planes, use_table), (shape(2, PA...  53.1 us
    ppermute x8, waiting for transfers between devices, joint_hop(): return lax.ppermute(x, ('row', 'head'), pairs)  37.8 us
    ppermute x12, starting transfers between devices, hop(): return lax.ppermute(x, 'row', flips(n_row, step))  16.9 us
    ppermute x8, starting transfers between devices, joint_hop(): return lax.ppermute(x, ('row', 'head'), pairs)  11 us
    ppermute x12, waiting for transfers between devices, hop(): return lax.ppermute(x, 'row', flips(n_row, step))  9.77 us
    pallas_call x1, Pallas kernels, per_device(): vmem_call(codes_kernel, code_shapes, 'svvvvvv', micros=9)  9 us
    pallas_call x1, Pallas kernels, per_device(): vmem_call(adam_kernel, tuple((shape(*p.shape) for p in params)), 'svvvv'...  5.63 us
    pallas_call x1, Pallas kernels, per_device(): vmem_call(weights_kernel, w_shapes, 'svvvv', micros=6)  5.19 us
  transfers between devices with their start and end apart: 33, of which 13 were waited for; matrix products, arithmetic and copies ran while one was open for 4% of the time, Pallas kernels for 12%

profile of v3, /device:TPU:0, one launch (start us, length us, event | category | flops | bytes accessed | tf_op | source)
XLA Modules:
  0.0 180.7 jit_solution(10236595245145974426)
XLA Ops:
  1.4 0.6 pad_add_fusion.meta
  2.0 1.9 %shard_map.511.own_piece_0_ = bf16[176,512]{1,0:T(8,128)(2,1)} custom-call(s32[2]{0:T(128)} %pad_add_fusion.meta, s32[1]{0:T(128)S(6)} %copy.64.wcount, f32[172,1024]{1,0:T(8,128)} %bitcast.69, s32[1,1024]{1,0:T(1,128)} %bitcast.78), custom_call_target="tpu_custom_call" | custom-call | flops 1000000000 | bytes 1000000 | tf_op jit(solution)/shard_map/pallas_call | solution.py:921
  3.9 3.9 %collective-permute-start.5 = (bf16[176,512]{1,0:T(8,128)(2,1)}, bf16[176,512]{1,0:T(8,128)(2,1)S(1)}, u32[]{:S(2)}, u32[]{:S(2)}) collective-permute-start(bf16[176,512]{1,0:T(8,128)(2,1)} %shard_map.511.own_piece_0_), channel_id=1, source_target_pairs={{0,6},{2,4},{4,2},{6,0},{8,14},{10,12},{12,10},{14,8},{16,22},{18,... | collective-permute-start | bytes 540680 | tf_op jit(solution)/shard_map/ppermute | solution.py:915
  7.8 0.5 collective-permute-start.4
  8.3 0.9 slice.30
  9.3 1.6 collective-permute-start
  10.9 2.6 %collective-permute-start.1 = (bf16[128,512]{1,0:T(8,128)(2,1)S(1)}, bf16[128,512]{1,0:T(8,128)(2,1)S(1)}, u32[]{:S(2)}, u32[]{:S(2)}) collective-permute-start(bf16[128,512]{1,0:T(8,128)(2,1)S(1)} %slice.30), channel_id=1, source_target_pairs={{0,16},{2,18},{4,20},{6,22},{8,24},{10,26},{12,28},{14,30},{16,0},... | collective-permute-start | bytes 393224 | tf_op jit(solution)/shard_map/ppermute | solution.py:915
  13.7 0.8 slice_bitcast_fusion.3
  14.9 0.9 collective-permute-done
  15.9 7.4 %collective-permute-done.1 = bf16[128,512]{1,0:T(8,128)(2,1)S(1)} collective-permute-done((bf16[128,512]{1,0:T(8,128)(2,1)S(1)}, bf16[128,512]{1,0:T(8,128)(2,1)S(1)}, u32[]{:S(2)}, u32[]{:S(2)}) %collective-permute-start.1) | collective-permute-done | bytes 131104 | tf_op jit(solution)/shard_map/ppermute | solution.py:915
  23.5 0.6 copy-done.33
  24.2 0.8 copy.61
  25.0 0.5 collective-permute-start.10
  25.5 1.5 collective-permute-start.11
  27.0 1.4 collective-permute-start.12
  28.5 2.0 %collective-permute-start.13 = (bf16[4,48,512]{2,1,0:T(8,128)(2,1)S(1)}, bf16[4,48,512]{2,1,0:T(8,128)(2,1)S(1)}, u32[]{:S(2)}, u32[]{:S(2)}) collective-permute-start(bf16[4,48,512]{2,1,0:T(8,128)(2,1)S(1)} %pad_maximum_fusion.2), channel_id=1, source_target_pairs={{0,8},{2,10},{4,12},{6,14},{8,0},{10,2},{12,4},{14,6},{16,24},{18,... | collective-permute-start | bytes 589832 | tf_op jit(solution)/shard_map/ppermute | solution.py:915
  30.4 1.1 collective-permute-start.14
  31.5 9.0 %shard_map.513 = (f32[2,88,512]{2,1,0:T(8,128)}, bf16[516,512]{1,0:T(8,128)(2,1)}, f32[172,512]{1,0:T(8,128)}, bf16[172,5120]{1,0:T(8,128)(2,1)}, bf16[172,5120]{1,0:T(8,128)(2,1)}) custom-call(s32[2]{0:T(128)} %pad_add_fusion.meta, f32[172,1024]{1,0:T(8,128)} %bitcast.70, s32[1,1024]{1,0:T(1,128)} %src.1, f32[1,1024]{1,0:T(1,128)} %bitcast.82, ...), custom_call_target="tpu_custom_call" | custom-call | flops 8999999488 | bytes 9000000 | tf_op jit(solution)/shard_map/pallas_call | solution.py:945
  40.5 1.5 collective-permute-start.15
  42.0 5.2 %shard_map.514 = (bf16[2,264,256]{2,1,0:T(8,128)(2,1)}, bf16[2,258,172]{2,1,0:T(8,128)(2,1)}, bf16[2,88,348]{2,1,0:T(8,128)(2,1)}, bf16[352,256]{1,0:T(8,128)(2,...) custom-call(s32[2]{0:T(128)} %pad_add_fusion.meta, ...), custom_call_target="tpu_custom_call" | custom-call | flops 6000000000 | bytes 6000000 | tf_op jit(solution)/shard_map/pallas_call | solution.py:954
  47.2 1.4 collective-permute-done.15.far_b_0__2_
  48.7 0.5 collective-permute-start.20
  49.3 0.4 collective-permute-start.7
  50.0 1.0 collective-permute-done.7.own_piece_1_
  51.2 0.4 copy-done.50
  51.7 0.2 collective-permute-start.17
  51.9 0.3 collective-permute-start.18
  52.2 0.4 copy-done.48
  52.6 0.7 copy-done.49
  53.3 0.3 collective-permute-start.8
  53.6 0.6 add_multiply_fusion.idx
  54.3 0.8 collective-permute-done.8.z_pieces_1_
  55.3 53.1 %shard_map.515 = (f32[2,88,512]{2,1,0:T(8,128)}, f32[4,144,768]{2,1,0:T(8,128)}, bf16[4,160,768]{2,1,0:T(8,128)(2,1)}, f32[8,128]{1,0:T(8,128)}) custom-call(s32[2]{0:T(128)} %pad_add_fusion.meta, s32[5632]{0:T(1024)} %add_multiply_fusion.idx, s32[1]{0:T(128)S(6)} %copy.64.wcount, bf16[176,512]{1,0:T(8,128)(2,1)} %shard_map.511.own_piece_0_, ...), custom_call_target="tpu_custom_call" | custom-call | flops 40000000000 | bytes 40000000 | tf_op jit(solution)/shard_map/pallas_call | solution.py:1016
  108.4 0.3 collective-permute-start.23
  108.8 2.5 %collective-permute-done.23.got = bf16[4,160,768]{2,1,0:T(8,128)(2,1)S(1)} collective-permute-done((bf16[4,160,768]{2,1,0:T(8,128)(2,1)}, bf16[4,160,768]{2,1,0:T(8,128)(2,1)S(1)}, u32[]{:S(2)}, u32[]{:S(2)}) %collective-permute-start.23) | collective-permute-done | bytes 983072 | tf_op jit(solution)/shard_map/ppermute | solution.py:912
  111.2 1.5 copy-done.30
  112.7 0.7 shard_map.517
  113.4 0.6 collective-permute-start.24
  114.0 8.3 %collective-permute-done.24.got = bf16[2,160,768]{2,1,0:T(8,128)(2,1)S(1)} collective-permute-done((bf16[2,160,768]{2,1,0:T(8,128)(2,1)S(1)}, bf16[2,160,768]{2,1,0:T(8,128)(2,1)S(1)}, u32[]{:S(2)}, u32[]{:S(2)}) %collective-permute-start.24) | collective-permute-done | bytes 491552 | tf_op jit(solution)/shard_map/ppermute | solution.py:1047
  122.3 0.6 shard_map.518
  123.0 1.6 collective-permute-start.25
  124.5 4.7 %collective-permute-done.25.got = bf16[160,768]{1,0:T(8,128)(2,1)S(1)} collective-permute-done((bf16[160,768]{1,0:T(8,128)(2,1)S(1)}, bf16[160,768]{1,0:T(8,128)(2,1)S(1)}, u32[]{:S(2)}, u32[]{:S(2)}) %collective-permute-start.25) | collective-permute-done | bytes 245792 | tf_op jit(solution)/shard_map/ppermute | solution.py:1047
  129.2 0.9 shard_map.519
  130.1 4.1 %collective-permute-start.26 = (bf16[144,768]{1,0:T(8,128)(2,1)S(1)}, bf16[144,768]{1,0:T(8,128)(2,1)S(1)}, u32[]{:S(2)}, u32[]{:S(2)}) collective-permute-start(bf16[144,768]{1,0:T(8,128)(2,1)S(1)} %get-tuple-element.144), channel_id=1, source_target_pairs={{0,8},{1,3},{2,10},{3,1},{4,12},{5,7},{6,14},{7,5},{8,0},{9,11},{1... | collective-permute-start | bytes 663560 | tf_op jit(solution)/shard_map/ppermute | solution.py:1047
  134.3 3.9 %collective-permute-done.26.got = bf16[144,768]{1,0:T(8,128)(2,1)S(1)} collective-permute-done((bf16[144,768]{1,0:T(8,128)(2,1)S(1)}, bf16[144,768]{1,0:T(8,128)(2,1)S(1)}, u32[]{:S(2)}, u32[]{:S(2)}) %collective-permute-start.26) | collective-permute-done | bytes 221216 | tf_op jit(solution)/shard_map/ppermute | solution.py:1047
  138.2 2.0 %collective-permute-start.27 = (bf16[144,768]{1,0:T(8,128)(2,1)S(1)}, bf16[144,768]{1,0:T(8,128)(2,1)S(1)}, u32[]{:S(2)}, u32[]{:S(2)}) collective-permute-start(bf16[144,768]{1,0:T(8,128)(2,1)S(1)} %shard_map.520.one), channel_id=1, source_target_pairs={{0,16},{1,5},{2,18},{3,7},{4,20},{5,1},{6,22},{7,3},{8,24},{9,13},... | collective-permute-start | bytes 663560 | tf_op jit(solution)/shard_map/ppermute | solution.py:1047
  140.2 7.3 %collective-permute-done.27.two = bf16[144,768]{1,0:T(8,128)(2,1)S(1)} collective-permute-done((bf16[144,768]{1,0:T(8,128)(2,1)S(1)}, bf16[144,768]{1,0:T(8,128)(2,1)S(1)}, u32[]{:S(2)}, u32[]{:S(2)}) %collective-permute-start.27) | collective-permute-done | bytes 221216 | tf_op jit(solution)/shard_map/ppermute | solution.py:1047
  147.7 6.3 %collective-permute-done.28.two = bf16[144,768]{1,0:T(8,128)(2,1)S(1)} collective-permute-done((bf16[144,768]{1,0:T(8,128)(2,1)S(1)}, bf16[144,768]{1,0:T(8,128)(2,1)S(1)}, u32[]{:S(2)}, u32[]{:S(2)}) %collective-permute-start.28) | collective-permute-done | bytes 221216 | tf_op jit(solution)/shard_map/ppermute | solution.py:1047
  154.0 0.6 shard_map.522.w0
  154.7 1.6 collective-permute-start.29
  156.2 0.7 dynamic-slice_bitcast_fusion.2
  156.9 0.6 collective-permute-start.30
  157.5 5.5 %collective-permute-done.29.w1 = bf16[288,768]{1,0:T(8,128)(2,1)S(1)} collective-permute-done((bf16[288,768]{1,0:T(8,128)(2,1)S(1)}, bf16[288,768]{1,0:T(8,128)(2,1)S(1)}, u32[]{:S(2)}, u32[]{:S(2)}) %collective-permute-start.29) | collective-permute-done | bytes 442400 | tf_op jit(solution)/shard_map/ppermute | solution.py:1047
  163.0 0.5 collective-permute-start.31
  163.6 1.0 dynamic-slice_bitcast_fusion.mem
  164.8 1.2 slice.29
  166.0 1.0 maximum_select_fusion.fresh
  167.1 2.4 %shard_map.516 = f32[86,1024]{1,0:T(8,128)} custom-call(f32[86,1024]{1,0:T(8,128)S(1)} %dynamic-slice_bitcast_fusion.mem, f32[88,1024]{1,0:T(8,128)S(1)} %maximum_select_fusion.fresh, s32[1024,1]{1,0:T(8,128)S(1)} %copy.63.src, s32[1]{0:T(128)S(6)} %copy.64.wcount), custom_call_target="tpu_custom_call" | custom-call | flops 3000000000 | bytes 3000000 | tf_op jit(solution)/shard_map/pallas_call | solution.py:1039
  169.6 1.8 collective-permute-done.31.w3
  171.4 1.1 shard_map.523.own
  172.5 0.3 collective-permute-start.32
  173.0 5.6 %shard_map.525 = (f32[258,688]{1,0:T(8,128)}, f32[258,688]{1,0:T(8,128)}, f32[258,688]{1,0:T(8,128)}, f32[172,258]{1,0:T(8,128)}, f32[172,258]{1,0:T(8,128)}, /*...) custom-call(s32[3]{0:T(128)S(1)} %pad_add_fusion.1.bits, ...), custom_call_target="tpu_custom_call" | custom-call | flops 4000000000 | bytes 4000000 | tf_op jit(solution)/shard_map/pallas_call | solution.py:1096
  178.7 1.6 shard_map.524
  180.2 0.5 slice.28
  (141 shorter events, 2.3 us)
Async XLA Ops:
  0.7 52.9 %copy-start = (s32[1024,10]{0,1:T(8,128)S(1)}, s32[1024,10]{0,1:T(8,128)}, u32[]{:S(2)}) copy-start(s32[1024,10]{0,1:T(8,128)} %param.35) | copy-start | bytes 122884
  2.0 12.6 %copy-start.1 = (f32[2,86,172]{2,0,1:T(2,128)S(1)}, f32[2,86,172]{2,0,1:T(2,128)}, u32[]{:S(2)}) copy-start(f32[2,86,172]{2,0,1:T(2,128)} %param.55) | copy-start | bytes 355012
  2.0 12.6 %copy-start.4 = (f32[688,258]{0,1:T(8,128)S(1)}, f32[688,258]{0,1:T(8,128)}, u32[]{:S(2)}) copy-start(f32[688,258]{0,1:T(8,128)} %param.40) | copy-start | bytes 2130052
  2.0 12.6 %copy-start.7 = (f32[3,344,86]{1,2,0:T(8,128)S(1)}, f32[3,344,86]{1,2,0:T(8,128)}, u32[]{:S(2)}) copy-start(f32[3,344,86]{1,2,0:T(8,128)} %param.52) | copy-start | bytes 1065028
  2.0 12.6 %copy-start.11 = (f32[172,258]{1,0:T(8,128)S(1)}, f32[172,258]{1,0:T(8,128)}, u32[]{:S(2)}) copy-start(f32[172,258]{1,0:T(8,128)} %refs_3_.3) | copy-start | bytes 532516
  2.0 12.6 %copy-start.20 = (f32[172,86]{1,0:T(8,128)S(1)}, f32[172,86]{1,0:T(8,128)}, u32[]{:S(2)}) copy-start(f32[172,86]{1,0:T(8,128)} %refs_15_.1) | copy-start | bytes 177508
  2.0 12.6 %copy-start.24 = (f32[2,258]{1,0:T(2,128)S(1)}, f32[2,258]{1,0:T(2,128)}, u32[]{:S(2)}) copy-start(f32[2,258]{1,0:T(2,128)} %refs_6_.1) | copy-start | bytes 6196
  3.9 19.4 %collective-permute-start.5 = (bf16[176,512]{1,0:T(8,128)(2,1)}, bf16[176,512]{1,0:T(8,128)(2,1)S(1)}, u32[]{:S(2)}, u32[]{:S(2)}) collective-permute-start(bf16[176,512]{1,0:T(8,128)(2,1)} %shard_map.511.own_piece_0_), channel_id=1, source_target_pairs={{0,6},{2,4},{4,2},{6,0},{8,14},{10,12},{12,10},{14,8},{16,22},{18,... | collective-permute-start | bytes 540680 | tf_op jit(solution)/shard_map/ppermute | solution.py:915
  7.8 15.6 %collective-permute-start.4 = (bf16[176,512]{1,0:T(8,128)(2,1)}, bf16[176,512]{1,0:T(8,128)(2,1)S(1)}, u32[]{:S(2)}, u32[]{:S(2)}) collective-permute-start(bf16[176,512]{1,0:T(8,128)(2,1)} %shard_map.511.own_piece_0_), channel_id=1, source_target_pairs={{0,4},{2,6},{4,0},{6,2},{8,12},{10,14},{12,8},{14,10},{16,20},{18,... | collective-permute-start | bytes 540680 | tf_op jit(solution)/shard_map/ppermute | solution.py:915
  9.3 6.5 %collective-permute-start = (bf16[128,512]{1,0:T(8,128)(2,1)S(1)}, bf16[128,512]{1,0:T(8,128)(2,1)S(1)}, u32[]{:S(2)}, u32[]{:S(2)}) collective-permute-start(bf16[128,512]{1,0:T(8,128)(2,1)S(1)} %slice.30), channel_id=1, source_target_pairs={{0,8},{2,10},{4,12},{6,14},{8,0},{10,2},{12,4},{14,6},{16,24},{18,... | collective-permute-start | bytes 393224 | tf_op jit(solution)/shard_map/ppermute | solution.py:915
  10.9 12.4 %collective-permute-start.1 = (bf16[128,512]{1,0:T(8,128)(2,1)S(1)}, bf16[128,512]{1,0:T(8,128)(2,1)S(1)}, u32[]{:S(2)}, u32[]{:S(2)}) collective-permute-start(bf16[128,512]{1,0:T(8,128)(2,1)S(1)} %slice.30), channel_id=1, source_target_pairs={{0,16},{2,18},{4,20},{6,22},{8,24},{10,26},{12,28},{14,30},{16,0},... | collective-permute-start | bytes 393224 | tf_op jit(solution)/shard_map/ppermute | solution.py:915
  13.5 9.8 %collective-permute-start.2 = (bf16[128,512]{1,0:T(8,128)(2,1)S(1)}, bf16[128,512]{1,0:T(8,128)(2,1)S(1)}, u32[]{:S(2)}, u32[]{:S(2)}) collective-permute-start(bf16[128,512]{1,0:T(8,128)(2,1)S(1)} %slice.30), channel_id=1, source_target_pairs={{0,24},{2,26},{4,28},{6,30},{8,16},{10,18},{12,20},{14,22},{16,8},... | collective-permute-start | bytes 393224 | tf_op jit(solution)/shard_map/ppermute | solution.py:915
  14.9 25.7 %copy-start.3 = (bf16[752,768]{1,0:T(8,128)(2,1)}, bf16[752,768]{1,0:T(8,128)(2,1)S(1)}, u32[]{:S(2)}) copy-start(bf16[752,768]{1,0:T(8,128)(2,1)S(1)} %shard_map.512.own) | copy-start | bytes 3465220
  14.9 9.4 %copy-start.2 = (f32[2,172]{1,0:T(2,128)S(1)}, f32[2,172]{1,0:T(2,128)}, u32[]{:S(2)}) copy-start(f32[2,172]{1,0:T(2,128)} %refs_3_.2) | copy-start | bytes 4132
  15.8 7.6 %collective-permute-start.3 = (bf16[176,512]{1,0:T(8,128)(2,1)S(1)}, bf16[176,512]{1,0:T(8,128)(2,1)S(1)}, u32[]{:S(2)}, u32[]{:S(2)}) collective-permute-start(bf16[176,512]{1,0:T(8,128)(2,1)S(1)} %copy-done.39), channel_id=1, source_target_pairs={{0,2},{2,0},{4,6},{6,4},{8,10},{10,8},{12,14},{14,12},{16,18},{18,... | collective-permute-start | bytes 540680 | tf_op jit(solution)/shard_map/ppermute | solution.py:915
  23.3 28.8 %copy-start.31 = (bf16[3,128,512]{2,1,0:T(8,128)(2,1)}, bf16[3,128,512]{2,1,0:T(8,128)(2,1)S(1)}, u32[]{:S(2)}) copy-start(bf16[3,128,512]{2,1,0:T(8,128)(2,1)S(1)} %pad_maximum_fusion.1.z_pieces_0_) | copy-start | bytes 1179652
  23.4 17.1 %copy-start.37 = (bf16[176,512]{1,0:T(8,128)(2,1)}, bf16[176,512]{1,0:T(8,128)(2,1)S(1)}, u32[]{:S(2)}) copy-start(bf16[176,512]{1,0:T(8,128)(2,1)S(1)} %collective-permute-done.3.xy_pieces_0__0_) | copy-start | bytes 540676
  24.2 6.3 %collective-permute-start.6 = (bf16[752,768]{1,0:T(8,128)(2,1)S(1)}, bf16[752,768]{1,0:T(8,128)(2,1)}, u32[]{:S(2)}, u32[]{:S(2)}) collective-permute-start(bf16[752,768]{1,0:T(8,128)(2,1)S(1)} %shard_map.512.own), channel_id=1, source_target_pairs={{0,1},{1,0},{2,3},{3,2},{4,5},{5,4},{6,7},{7,6},{8,9},{9,8},{10,11... | collective-permute-start | bytes 3465224 | tf_op jit(solution)/shard_map/ppermute | solution.py:912
  25.0 23.7 %collective-permute-start.10 = (bf16[3,128,512]{2,1,0:T(8,128)(2,1)S(1)}, bf16[3,128,512]{2,1,0:T(8,128)(2,1)}, u32[]{:S(2)}, u32[]{:S(2)}) collective-permute-start(bf16[3,128,512]{2,1,0:T(8,128)(2,1)S(1)} %pad_maximum_fusion.1.z_pieces_0_), channel_id=1, source_target_pairs={{0,2},{2,0},{4,6},{6,4},{8,10},{10,8},{12,14},{14,12},{16,18},{18,... | collective-permute-start | bytes 1179656 | tf_op jit(solution)/shard_map/ppermute | solution.py:915
  25.5 23.1 %collective-permute-start.11 = (bf16[3,128,512]{2,1,0:T(8,128)(2,1)S(1)}, bf16[3,128,512]{2,1,0:T(8,128)(2,1)}, u32[]{:S(2)}, u32[]{:S(2)}) collective-permute-start(bf16[3,128,512]{2,1,0:T(8,128)(2,1)S(1)} %pad_maximum_fusion.1.z_pieces_0_), channel_id=1, source_target_pairs={{0,4},{2,6},{4,0},{6,2},{8,12},{10,14},{12,8},{14,10},{16,20},{18,... | collective-permute-start | bytes 1179656 | tf_op jit(solution)/shard_map/ppermute | solution.py:915
  27.0 21.6 %collective-permute-start.12 = (bf16[3,128,512]{2,1,0:T(8,128)(2,1)S(1)}, bf16[3,128,512]{2,1,0:T(8,128)(2,1)}, u32[]{:S(2)}, u32[]{:S(2)}) collective-permute-start(bf16[3,128,512]{2,1,0:T(8,128)(2,1)S(1)} %pad_maximum_fusion.1.z_pieces_0_), channel_id=1, source_target_pairs={{0,6},{2,4},{4,2},{6,0},{8,14},{10,12},{12,10},{14,8},{16,22},{18,... | collective-permute-start | bytes 1179656 | tf_op jit(solution)/shard_map/ppermute | solution.py:915
  28.5 12.1 %collective-permute-start.13 = (bf16[4,48,512]{2,1,0:T(8,128)(2,1)S(1)}, bf16[4,48,512]{2,1,0:T(8,128)(2,1)S(1)}, u32[]{:S(2)}, u32[]{:S(2)}) collective-permute-start(bf16[4,48,512]{2,1,0:T(8,128)(2,1)S(1)} %pad_maximum_fusion.2), channel_id=1, source_target_pairs={{0,8},{2,10},{4,12},{6,14},{8,0},{10,2},{12,4},{14,6},{16,24},{18,... | collective-permute-start | bytes 589832 | tf_op jit(solution)/shard_map/ppermute | solution.py:915
  30.4 16.8 %collective-permute-start.14 = (bf16[4,48,512]{2,1,0:T(8,128)(2,1)S(1)}, bf16[4,48,512]{2,1,0:T(8,128)(2,1)S(1)}, u32[]{:S(2)}, u32[]{:S(2)}) collective-permute-start(bf16[4,48,512]{2,1,0:T(8,128)(2,1)S(1)} %pad_maximum_fusion.2), channel_id=1, source_target_pairs={{0,16},{2,18},{4,20},{6,22},{8,24},{10,26},{12,28},{14,30},{16,0},... | collective-permute-start | bytes 589832 | tf_op jit(solution)/shard_map/ppermute | solution.py:915
  40.5 8.1 %copy-start.45 = (bf16[4,48,512]{2,1,0:T(8,128)(2,1)}, bf16[4,48,512]{2,1,0:T(8,128)(2,1)S(1)}, u32[]{:S(2)}) copy-start(bf16[4,48,512]{2,1,0:T(8,128)(2,1)S(1)} %collective-permute-done.13.far_b_0__0_) | copy-start | bytes 589828
  40.5 8.1 %collective-permute-start.15 = (bf16[4,48,512]{2,1,0:T(8,128)(2,1)S(1)}, bf16[4,48,512]{2,1,0:T(8,128)(2,1)S(1)}, u32[]{:S(2)}, u32[]{:S(2)}) collective-permute-start(bf16[4,48,512]{2,1,0:T(8,128)(2,1)S(1)} %pad_maximum_fusion.2), channel_id=1, source_target_pairs={{0,24},{2,26},{4,28},{6,30},{8,16},{10,18},{12,20},{14,22},{16,8},... | collective-permute-start | bytes 589832 | tf_op jit(solution)/shard_map/ppermute | solution.py:915
  42.0 7.7 %copy-start.34 = (bf16[176,512]{1,0:T(8,128)(2,1)S(1)}, bf16[176,512]{1,0:T(8,128)(2,1)}, u32[]{:S(2)}) copy-start(bf16[176,512]{1,0:T(8,128)(2,1)} %copy-done.33) | copy-start | bytes 540676
  42.0 7.7 %copy-start.36 = (bf16[176,512]{1,0:T(8,128)(2,1)S(1)}, bf16[176,512]{1,0:T(8,128)(2,1)}, u32[]{:S(2)}) copy-start(bf16[176,512]{1,0:T(8,128)(2,1)} %copy-done.35) | copy-start | bytes 540676
  42.0 7.7 %copy-start.38 = (bf16[176,512]{1,0:T(8,128)(2,1)S(1)}, bf16[176,512]{1,0:T(8,128)(2,1)}, u32[]{:S(2)}) copy-start(bf16[176,512]{1,0:T(8,128)(2,1)} %copy-done.37) | copy-start | bytes 540676
  42.0 11.5 %copy-start.41 = (s32[1024]{0:T(1024)S(1)}, s32[1024]{0:T(1024)}, u32[]{:S(2)}) copy-start(s32[1024]{0:T(1024)} %param.34) | copy-start | bytes 12292
  47.2 5.0 %copy-start.46 = (bf16[4,48,512]{2,1,0:T(8,128)(2,1)}, bf16[4,48,512]{2,1,0:T(8,128)(2,1)S(1)}, u32[]{:S(2)}) copy-start(bf16[4,48,512]{2,1,0:T(8,128)(2,1)S(1)} %collective-permute-done.14.far_b_0__1_) | copy-start | bytes 589828
  48.6 3.6 %copy-start.47 = (bf16[4,48,512]{2,1,0:T(8,128)(2,1)}, bf16[4,48,512]{2,1,0:T(8,128)(2,1)S(1)}, u32[]{:S(2)}) copy-start(bf16[4,48,512]{2,1,0:T(8,128)(2,1)S(1)} %collective-permute-done.15.far_b_0__2_) | copy-start | bytes 589828
  48.7 3.0 %collective-permute-start.19 = (bf16[4,48,512]{2,1,0:T(8,128)(2,1)S(1)}, bf16[4,48,512]{2,1,0:T(8,128)(2,1)}, u32[]{:S(2)}, u32[]{:S(2)}) collective-permute-start(bf16[4,48,512]{2,1,0:T(8,128)(2,1)S(1)} %collective-permute-done.13.far_b_0__0_), channel_id=1, source_target_pairs={{0,1},{1,0},{2,3},{3,2},{4,5},{5,4},{6,7},{7,6},{8,9},{9,8},{10,11... | collective-permute-start | bytes 589832 | tf_op jit(solution)/shard_map/ppermute | solution.py:912
  48.7 3.2 %collective-permute-start.20 = (bf16[4,48,512]{2,1,0:T(8,128)(2,1)S(1)}, bf16[4,48,512]{2,1,0:T(8,128)(2,1)S(1)}, u32[]{:S(2)}, u32[]{:S(2)}) collective-permute-start(bf16[4,48,512]{2,1,0:T(8,128)(2,1)S(1)} %collective-permute-done.14.far_b_0__1_), channel_id=1, source_target_pairs={{0,1},{1,0},{2,3},{3,2},{4,5},{5,4},{6,7},{7,6},{8,9},{9,8},{10,11... | collective-permute-start | bytes 589832 | tf_op jit(solution)/shard_map/ppermute | solution.py:912
  49.2 2.9 %collective-permute-start.21 = (bf16[4,48,512]{2,1,0:T(8,128)(2,1)S(1)}, bf16[4,48,512]{2,1,0:T(8,128)(2,1)S(1)}, u32[]{:S(2)}, u32[]{:S(2)}) collective-permute-start(bf16[4,48,512]{2,1,0:T(8,128)(2,1)S(1)} %collective-permute-done.15.far_b_0__2_), channel_id=1, source_target_pairs={{0,1},{1,0},{2,3},{3,2},{4,5},{5,4},{6,7},{7,6},{8,9},{9,8},{10,11... | collective-permute-start | bytes 589832 | tf_op jit(solution)/shard_map/ppermute | solution.py:912
  49.3 1.7 collective-permute-start.7
  49.8 5.3 %collective-permute-start.9 = (bf16[3,176,512]{2,1,0:T(8,128)(2,1)S(1)}, bf16[3,176,512]{2,1,0:T(8,128)(2,1)}, u32[]{:S(2)}, u32[]{:S(2)}) collective-permute-start(bf16[3,176,512]{2,1,0:T(8,128)(2,1)S(1)} %pad_maximum_fusion), channel_id=1, source_target_pairs={{0,1},{1,0},{2,3},{3,2},{4,5},{5,4},{6,7},{7,6},{8,9},{9,8},{10,11... | collective-permute-start | bytes 1622024 | tf_op jit(solution)/shard_map/ppermute | solution.py:912
  51.0 3.2 %collective-permute-start.16 = (bf16[3,128,512]{2,1,0:T(8,128)(2,1)}, bf16[3,128,512]{2,1,0:T(8,128)(2,1)S(1)}, u32[]{:S(2)}, u32[]{:S(2)}) collective-permute-start(bf16[3,128,512]{2,1,0:T(8,128)(2,1)} %collective-permute-done.10.far_a_0__0_), channel_id=1, source_target_pairs={{0,1},{1,0},{2,3},{3,2},{4,5},{5,4},{6,7},{7,6},{8,9},{9,8},{10,11... | collective-permute-start | bytes 1179656 | tf_op jit(solution)/shard_map/ppermute | solution.py:912
  51.7 2.6 %collective-permute-start.17 = (bf16[3,128,512]{2,1,0:T(8,128)(2,1)}, bf16[3,128,512]{2,1,0:T(8,128)(2,1)S(1)}, u32[]{:S(2)}, u32[]{:S(2)}) collective-permute-start(bf16[3,128,512]{2,1,0:T(8,128)(2,1)} %collective-permute-done.11.far_a_0__1_), channel_id=1, source_target_pairs={{0,1},{1,0},{2,3},{3,2},{4,5},{5,4},{6,7},{7,6},{8,9},{9,8},{10,11... | collective-permute-start | bytes 1179656 | tf_op jit(solution)/shard_map/ppermute | solution.py:912
  51.9 2.4 %collective-permute-start.18 = (bf16[3,128,512]{2,1,0:T(8,128)(2,1)}, bf16[3,128,512]{2,1,0:T(8,128)(2,1)S(1)}, u32[]{:S(2)}, u32[]{:S(2)}) collective-permute-start(bf16[3,128,512]{2,1,0:T(8,128)(2,1)} %collective-permute-done.12.far_a_0__2_), channel_id=1, source_target_pairs={{0,1},{1,0},{2,3},{3,2},{4,5},{5,4},{6,7},{7,6},{8,9},{9,8},{10,11... | collective-permute-start | bytes 1179656 | tf_op jit(solution)/shard_map/ppermute | solution.py:912
  53.3 1.9 %collective-permute-start.8 = (bf16[3,128,512]{2,1,0:T(8,128)(2,1)S(1)}, bf16[3,128,512]{2,1,0:T(8,128)(2,1)}, u32[]{:S(2)}, u32[]{:S(2)}) collective-permute-start(bf16[3,128,512]{2,1,0:T(8,128)(2,1)S(1)} %pad_maximum_fusion.1.z_pieces_0_), channel_id=1, source_target_pairs={{0,1},{1,0},{2,3},{3,2},{4,5},{5,4},{6,7},{7,6},{8,9},{9,8},{10,11... | collective-permute-start | bytes 1179656 | tf_op jit(solution)/shard_map/ppermute | solution.py:912
  108.4 2.8 %collective-permute-start.23 = (bf16[4,160,768]{2,1,0:T(8,128)(2,1)}, bf16[4,160,768]{2,1,0:T(8,128)(2,1)S(1)}, u32[]{:S(2)}, u32[]{:S(2)}) collective-permute-start(bf16[4,160,768]{2,1,0:T(8,128)(2,1)} %get-tuple-element.138), channel_id=1, source_target_pairs={{0,1},{1,0},{2,3},{3,2},{4,5},{5,4},{6,7},{7,6},{8,9},{9,8},{10,11... | collective-permute-start | bytes 2949128 | tf_op jit(solution)/shard_map/ppermute | solution.py:912
  113.4 8.9 %collective-permute-start.24 = (bf16[2,160,768]{2,1,0:T(8,128)(2,1)S(1)}, bf16[2,160,768]{2,1,0:T(8,128)(2,1)S(1)}, u32[]{:S(2)}, u32[]{:S(2)}) collective-permute-start(bf16[2,160,768]{2,1,0:T(8,128)(2,1)S(1)} %get-tuple-element.140), channel_id=1, source_target_pairs={{0,2},{1,9},{2,0},{3,11},{4,6},{5,13},{6,4},{7,15},{8,10},{9,1},{1... | collective-permute-start | bytes 1474568 | tf_op jit(solution)/shard_map/ppermute | solution.py:1047
  123.0 6.3 %collective-permute-start.25 = (bf16[160,768]{1,0:T(8,128)(2,1)S(1)}, bf16[160,768]{1,0:T(8,128)(2,1)S(1)}, u32[]{:S(2)}, u32[]{:S(2)}) collective-permute-start(bf16[160,768]{1,0:T(8,128)(2,1)S(1)} %get-tuple-element.142), channel_id=1, source_target_pairs={{0,4},{1,17},{2,6},{3,19},{4,0},{5,21},{6,2},{7,23},{8,12},{9,25},... | collective-permute-start | bytes 737288 | tf_op jit(solution)/shard_map/ppermute | solution.py:1047
  130.1 8.0 %collective-permute-start.26 = (bf16[144,768]{1,0:T(8,128)(2,1)S(1)}, bf16[144,768]{1,0:T(8,128)(2,1)S(1)}, u32[]{:S(2)}, u32[]{:S(2)}) collective-permute-start(bf16[144,768]{1,0:T(8,128)(2,1)S(1)} %get-tuple-element.144), channel_id=1, source_target_pairs={{0,8},{1,3},{2,10},{3,1},{4,12},{5,7},{6,14},{7,5},{8,0},{9,11},{1... | collective-permute-start | bytes 663560 | tf_op jit(solution)/shard_map/ppermute | solution.py:1047
  138.2 9.3 %collective-permute-start.27 = (bf16[144,768]{1,0:T(8,128)(2,1)S(1)}, bf16[144,768]{1,0:T(8,128)(2,1)S(1)}, u32[]{:S(2)}, u32[]{:S(2)}) collective-permute-start(bf16[144,768]{1,0:T(8,128)(2,1)S(1)} %shard_map.520.one), channel_id=1, source_target_pairs={{0,16},{1,5},{2,18},{3,7},{4,20},{5,1},{6,22},{7,3},{8,24},{9,13},... | collective-permute-start | bytes 663560 | tf_op jit(solution)/shard_map/ppermute | solution.py:1047
  147.6 8.6 %copy-start.32 = (f32[2,88,512]{2,1,0:T(8,128)S(1)}, f32[2,88,512]{2,1,0:T(8,128)}, u32[]{:S(2)}) copy-start(f32[2,88,512]{2,1,0:T(8,128)} %get-tuple-element.136) | copy-start | bytes 1081348
  147.6 6.4 %collective-permute-start.28 = (bf16[144,768]{1,0:T(8,128)(2,1)S(1)}, bf16[144,768]{1,0:T(8,128)(2,1)S(1)}, u32[]{:S(2)}, u32[]{:S(2)}) collective-permute-start(bf16[144,768]{1,0:T(8,128)(2,1)S(1)} %shard_map.521.one), channel_id=1, source_target_pairs={{0,8},{1,3},{2,10},{3,1},{4,12},{5,7},{6,14},{7,5},{8,0},{9,11},{1... | collective-permute-start | bytes 663560 | tf_op jit(solution)/shard_map/ppermute | solution.py:1047
  154.6 10.0 %copy-start.40 = (s32[1,1024]{1,0:T(1,128)S(1)}, s32[1,1024]{1,0:T(1,128)}, u32[]{:S(2)}) copy-start(s32[1,1024]{1,0:T(1,128)} %src.1) | copy-start | bytes 12292
  154.7 8.4 %collective-permute-start.29 = (bf16[288,768]{1,0:T(8,128)(2,1)S(1)}, bf16[288,768]{1,0:T(8,128)(2,1)S(1)}, u32[]{:S(2)}, u32[]{:S(2)}) collective-permute-start(bf16[288,768]{1,0:T(8,128)(2,1)S(1)} %shard_map.522.w0), channel_id=1, source_target_pairs={{0,4},{1,17},{2,6},{3,19},{4,0},{5,21},{6,2},{7,23},{8,12},{9,25},... | collective-permute-start | bytes 1327112 | tf_op jit(solution)/shard_map/ppermute | solution.py:1047
  156.9 9.1 %collective-permute-start.22 = (f32[88,512]{1,0:T(8,128)}, f32[88,512]{1,0:T(8,128)}, u32[]{:S(2)}, u32[]{:S(2)}) collective-permute-start(f32[88,512]{1,0:T(8,128)} %get-tuple-element.172), channel_id=1, source_target_pairs={{0,1},{1,0},{2,3},{3,2},{4,5},{5,4},{6,7},{7,6},{8,9},{9,8},{10,11... | collective-permute-start | bytes 540680 | tf_op jit(solution)/shard_map/ppermute | solution.py:912
  156.9 12.7 %collective-permute-start.30 = (bf16[288,768]{1,0:T(8,128)(2,1)S(1)}, bf16[288,768]{1,0:T(8,128)(2,1)S(1)}, u32[]{:S(2)}, u32[]{:S(2)}) collective-permute-start(bf16[288,768]{1,0:T(8,128)(2,1)S(1)} %shard_map.522.w0), channel_id=1, source_target_pairs={{0,2},{1,9},{2,0},{3,11},{4,6},{5,13},{6,4},{7,15},{8,10},{9,1},{1... | collective-permute-start | bytes 1327112 | tf_op jit(solution)/shard_map/ppermute | solution.py:1047
  163.0 8.4 %collective-permute-start.31 = (bf16[288,768]{1,0:T(8,128)(2,1)S(1)}, bf16[288,768]{1,0:T(8,128)(2,1)}, u32[]{:S(2)}, u32[]{:S(2)}) collective-permute-start(bf16[288,768]{1,0:T(8,128)(2,1)S(1)} %collective-permute-done.29.w1), channel_id=1, source_target_pairs={{0,2},{1,9},{2,0},{3,11},{4,6},{5,13},{6,4},{7,15},{8,10},{9,1},{1... | collective-permute-start | bytes 1327112 | tf_op jit(solution)/shard_map/ppermute | solution.py:1047
  167.1 5.7 %copy-start.18 = (f32[2,86,172]{2,0,1:T(2,128)S(1)}, f32[2,86,172]{2,0,1:T(2,128)}, u32[]{:S(2)}) copy-start(f32[2,86,172]{2,0,1:T(2,128)} %param.56) | copy-start | bytes 355012
  167.1 5.7 %copy-start.19 = (f32[2,86,172]{2,0,1:T(2,128)S(1)}, f32[2,86,172]{2,0,1:T(2,128)}, u32[]{:S(2)}) copy-start(f32[2,86,172]{2,0,1:T(2,128)} %param.57) | copy-start | bytes 355012
  167.1 5.7 %copy-start.21 = (f32[172,86]{1,0:T(8,128)S(1)}, f32[172,86]{1,0:T(8,128)}, u32[]{:S(2)}) copy-start(f32[172,86]{1,0:T(8,128)} %refs_15_.1) | copy-start | bytes 177508
  167.1 5.7 %copy-start.22 = (f32[172,86]{1,0:T(8,128)S(1)}, f32[172,86]{1,0:T(8,128)}, u32[]{:S(2)}) copy-start(f32[172,86]{1,0:T(8,128)} %refs_16_.1) | copy-start | bytes 177508
  167.1 5.7 %copy-start.23 = (f32[172,86]{1,0:T(8,128)S(1)}, f32[172,86]{1,0:T(8,128)}, u32[]{:S(2)}) copy-start(f32[172,86]{1,0:T(8,128)} %refs_17_.1) | copy-start | bytes 177508
  172.5 6.1 %collective-permute-start.32 = (bf16[128,768]{1,0:T(8,128)(2,1)S(1)}, bf16[128,768]{1,0:T(8,128)(2,1)S(1)}, u32[]{:S(2)}, u32[]{:S(2)}) collective-permute-start(bf16[128,768]{1,0:T(8,128)(2,1)S(1)} %shard_map.523.own), channel_id=1, source_target_pairs={{0,1},{1,0},{2,3},{3,2},{4,5},{5,4},{6,7},{7,6},{8,9},{9,8},{10,11... | collective-permute-start | bytes 589832 | tf_op jit(solution)/shard_map/ppermute | solution.py:912
  172.9 5.7 %copy-start.15 = (f32[172,172]{1,0:T(8,128)S(1)}, f32[172,172]{1,0:T(8,128)}, u32[]{:S(2)}) copy-start(f32[172,172]{1,0:T(8,128)} %refs_0_.1) | copy-start | bytes 355012
  172.9 5.7 %copy-start.16 = (f32[172,172]{1,0:T(8,128)S(1)}, f32[172,172]{1,0:T(8,128)}, u32[]{:S(2)}) copy-start(f32[172,172]{1,0:T(8,128)} %refs_1_.1) | copy-start | bytes 355012
  172.9 5.7 %copy-start.17 = (f32[172,172]{1,0:T(8,128)S(1)}, f32[172,172]{1,0:T(8,128)}, u32[]{:S(2)}) copy-start(f32[172,172]{1,0:T(8,128)} %refs_2_.1) | copy-start | bytes 355012
  172.9 5.7 %copy-start.27 = (f32[2,172]{1,0:T(2,128)S(1)}, f32[2,172]{1,0:T(2,128)}, u32[]{:S(2)}) copy-start(f32[2,172]{1,0:T(2,128)} %refs_4_.2) | copy-start | bytes 4132
  172.9 5.7 %copy-start.28 = (f32[2,172]{1,0:T(2,128)S(1)}, f32[2,172]{1,0:T(2,128)}, u32[]{:S(2)}) copy-start(f32[2,172]{1,0:T(2,128)} %refs_5_.2) | copy-start | bytes 4132
  173.0 5.7 %copy-start.29 = (s32[2]{0:T(128)S(1)}, s32[2]{0:T(128)}, u32[]{:S(2)}) copy-start(s32[2]{0:T(128)} %pad_add_fusion.meta) | copy-start | bytes 28
  (20 other events, 41.7 us)
